TPU v7x, 32 devices: a whole 2x2x4 slice. The times are simulated.
32 devices in a mesh: dp: 8 (over y, x, core), seq: 4 (over z).
Axes of the slice: x: 2, y: 2, z: 4, core: 2. Of those that a mesh axis runs over, the one named last changes fastest.
Arguments:
- tokens: bfloat16 [8, 1024, 2048], P('dp', 'seq'), may hold values from -6 to 6
- cotangent: bfloat16 [8, 1024, 2048], P('dp', 'seq'), may hold values from -6 to 6
- norm_gain: bfloat16 [2048], P(('dp', 'seq')), may hold values from 0.5 to 1.5
- in_weight: bfloat16 [2048, 8192], P(('dp', 'seq')), may hold values from -0.125 to 0.125
- conv_weight: bfloat16 [4096, 4], P(('dp', 'seq')), may hold values from -3 to 3
- conv_bias: bfloat16 [4096], P(('dp', 'seq')), may hold values from -3 to 3
- select_weight: bfloat16 [4096, 160], P(('dp', 'seq')), may hold values from -0.09375 to 0.09375
- beta_weight: bfloat16 [4096, 128], P(('dp', 'seq')), may hold values from -0.5 to 0.5
- beta_bias: bfloat16 [4096], P(('dp', 'seq')), may hold values from -8 to 0
- skip_gain: bfloat16 [4096], P(('dp', 'seq')), may hold values from 0.25 to 1.5
- out_weight: bfloat16 [4096, 2048], P(('dp', 'seq')), may hold values from -0.09375 to 0.09375
Outputs:
- result: bfloat16 [8, 1024, 2048], P('dp', 'seq')
- input_grad: bfloat16 [8, 1024, 2048], P('dp', 'seq')
- norm_gain_grad: float32 [2048], P(('dp', 'seq'))
- in_weight_grad: float32 [2048, 8192], P(('dp', 'seq'))
- conv_weight_grad: float32 [4096, 4], P(('dp', 'seq'))
- conv_bias_grad: float32 [4096], P(('dp', 'seq'))
- select_weight_grad: float32 [4096, 160], P(('dp', 'seq'))
- beta_weight_grad: float32 [4096, 128], P(('dp', 'seq'))
- beta_bias_grad: float32 [4096], P(('dp', 'seq'))
- skip_gain_grad: float32 [4096], P(('dp', 'seq'))
- out_weight_grad: float32 [4096, 2048], P(('dp', 'seq'))
All inputs are finite; a program needn't handle non-finite values.
Results may differ from a plain program's by a relative error of at most 0.012.
Values may be sent and summed in bfloat16 or wider, within the bound.
A program may use at most 320 MiB of HBM per device.

v0:
```python
import jax
import jax.numpy as jnp
from jax import lax
from jax.sharding import PartitionSpec as P


def passed_along(value, axis, by):
    size = lax.axis_size(axis)
    pairs = [(i, i + by) for i in range(size) if 0 <= i + by < size]
    return lax.ppermute(value, axis, pairs)


def contract(left, right, left_dim, right_dim):
    return lax.dot_general(
        left, right, (((left_dim,), (right_dim,)), ((), ())), preferred_element_type=jnp.float32
    )


def rms_scaled(rows, gain):
    return rows * lax.rsqrt(jnp.mean(rows * rows, axis=-1, keepdims=True) + 1e-05) * gain


def convolve(padded, weight, bias):
    length = padded.shape[1] - weight.shape[1] + 1
    total = bias + padded[:, 0:length, :] * weight[:, 0]
    for offset in range(1, weight.shape[1]):
        total = total + padded[:, offset : offset + length, :] * weight[:, offset]
    return jax.nn.silu(total)


def rates_of(pre, keys):
    beta = jax.nn.sigmoid(pre)
    return beta / (1.0 + beta * jnp.sum(keys * keys, axis=-1, keepdims=True))


def recurrence(start, rates, keys, queries, values, emit):
    count_seqs, length, inner = rates.shape
    span = min(16, length)
    blocks = length // span

    def block(carry, index):
        state, decayed = carry
        begin = index * span
        rate_rows = lax.dynamic_slice_in_dim(rates, begin, span, 1)
        key_rows = lax.dynamic_slice_in_dim(keys, begin, span, 1)
        value_rows = lax.dynamic_slice_in_dim(values, begin, span, 1)
        if emit:
            query_rows = lax.dynamic_slice_in_dim(queries, begin, span, 1)
        emitted = []
        for offset in range(span):
            rate_now = rate_rows[:, offset, None, :]
            key_now = key_rows[:, offset, :, None]
            decay = 1.0 - rate_now * (key_now * key_now)
            state = decay * state + key_now * (rate_now * value_rows[:, offset, None, :])
            if emit:
                emitted.append(jnp.sum(state * query_rows[:, offset, :, None], axis=1))
            else:
                decayed = decayed * decay
        if emit:
            return ((state, decayed), jnp.stack(emitted, axis=1))
        return ((state, decayed), None)

    carry_init = (start, jnp.ones_like(start))
    (final, decayed), emitted = lax.scan(jax.checkpoint(block), carry_init, jnp.arange(blocks))
    if emit:
        outputs = jnp.transpose(emitted, (1, 0, 2, 3)).reshape(count_seqs, length, inner)
        return (outputs, final, decayed)
    return (None, final, decayed)


def mixer(pre, keys, queries, values, start, skip, gate_in):
    rates = rates_of(pre, keys)
    outputs, final, unused = recurrence(start, rates, keys, queries, values, True)
    return ((outputs + skip * values) * jax.nn.silu(gate_in), final)


def local(
    tokens,
    cotangent,
    norm_gain,
    in_weight,
    conv_weight,
    conv_bias,
    select_weight,
    beta_weight,
    beta_bias,
    skip_gain,
    out_weight,
):
    shards = (
        norm_gain,
        in_weight,
        conv_weight,
        conv_bias,
        select_weight,
        beta_weight,
        beta_bias,
        skip_gain,
        out_weight,
    )
    whole = (
        lax.all_gather(shards[0], ("dp", "seq"), axis=0, tiled=True),
        lax.all_gather(shards[1], ("dp", "seq"), axis=0, tiled=True),
        lax.all_gather(shards[2], ("dp", "seq"), axis=0, tiled=True),
        lax.all_gather(shards[3], ("dp", "seq"), axis=0, tiled=True),
        lax.all_gather(shards[4], ("dp", "seq"), axis=0, tiled=True),
        lax.all_gather(shards[5], ("dp", "seq"), axis=0, tiled=True),
        lax.all_gather(shards[6], ("dp", "seq"), axis=0, tiled=True),
        lax.all_gather(shards[7], ("dp", "seq"), axis=0, tiled=True),
        lax.all_gather(shards[8], ("dp", "seq"), axis=0, tiled=True),
    )
    gain_w, in_w, conv_w, conv_b, select_w, beta_w, beta_b, skip_w, out_w = whole
    count_seqs, length, width_d = tokens.shape
    inner = conv_w.shape[0]
    taps = conv_w.shape[1]
    rank = beta_w.shape[1]
    states = (select_w.shape[1] - rank) // 2
    rows = count_seqs * length
    seq_devices = lax.axis_size("seq")
    flat = tokens.reshape(rows, width_d).astype(jnp.float32)
    normed = rms_scaled(flat, gain_w.astype(jnp.float32)).astype(jnp.bfloat16)
    mixed = jnp.dot(normed, in_w, preferred_element_type=jnp.float32)
    conv_in = mixed[:, :inner].astype(jnp.bfloat16).reshape(count_seqs, length, inner)
    gate_in = mixed[:, inner:].reshape(count_seqs, length, inner)
    rim = passed_along(conv_in[:, length - taps + 1 :, :], "seq", 1)
    padded = jnp.concatenate([rim, conv_in], axis=1).astype(jnp.float32)
    values_low = convolve(padded, conv_w.astype(jnp.float32), conv_b.astype(jnp.float32)).astype(
        jnp.bfloat16
    )
    values_rows = values_low.reshape(rows, inner)
    projected = jnp.dot(values_rows, select_w, preferred_element_type=jnp.float32)
    lowrank = projected[:, :rank].astype(jnp.bfloat16)
    keys = projected[:, rank : rank + states].reshape(count_seqs, length, states)
    queries = projected[:, rank + states :].reshape(count_seqs, length, states)
    pre = (contract(lowrank, beta_w, 1, 1) + beta_b.astype(jnp.float32)).reshape(
        count_seqs, length, inner
    )
    values = values_low.astype(jnp.float32)
    zeros_state = jnp.zeros((count_seqs, states, inner), jnp.float32)
    unused, ends, decayed = recurrence(zeros_state, rates_of(pre, keys), keys, None, values, False)

    def relay_step(turn, carry):
        incoming, outgoing = carry
        incoming = passed_along(outgoing.astype(jnp.bfloat16), "seq", 1).astype(outgoing.dtype)
        return (incoming, decayed * incoming + ends)

    start, unused = lax.fori_loop(0, seq_devices - 1, relay_step, (zeros_state, ends))
    gated, unused = mixer(pre, keys, queries, values, start, skip_w.astype(jnp.float32), gate_in)
    gated_low = gated.astype(jnp.bfloat16).reshape(rows, inner)
    result = (flat + jnp.dot(gated_low, out_w, preferred_element_type=jnp.float32)).astype(
        jnp.bfloat16
    )
    again = (
        lax.all_gather(shards[0], ("dp", "seq"), axis=0, tiled=True),
        lax.all_gather(shards[1], ("dp", "seq"), axis=0, tiled=True),
        lax.all_gather(shards[2], ("dp", "seq"), axis=0, tiled=True),
        lax.all_gather(shards[3], ("dp", "seq"), axis=0, tiled=True),
        lax.all_gather(shards[4], ("dp", "seq"), axis=0, tiled=True),
        lax.all_gather(shards[5], ("dp", "seq"), axis=0, tiled=True),
        lax.all_gather(shards[6], ("dp", "seq"), axis=0, tiled=True),
        lax.all_gather(shards[7], ("dp", "seq"), axis=0, tiled=True),
        lax.all_gather(shards[8], ("dp", "seq"), axis=0, tiled=True),
    )
    gain_b, in_b, conv_wb, conv_bb, select_b, beta_wb, beta_bb, skip_b, out_b = again
    cot_low = cotangent.reshape(rows, width_d)
    out_grad = contract(gated_low, cot_low, 0, 0)
    dgated = contract(cot_low, out_b, 1, 1).reshape(count_seqs, length, inner)
    primal, pullback = jax.vjp(
        mixer, pre, keys, queries, values, start, skip_b.astype(jnp.float32), gate_in
    )
    local_back = pullback((dgated, zeros_state))[4]

    def relay_back(turn, carry):
        incoming, outgoing = carry
        incoming = passed_along(outgoing.astype(jnp.bfloat16), "seq", -1).astype(outgoing.dtype)
        return (incoming, decayed * incoming + local_back)

    end_grad, unused = lax.fori_loop(0, seq_devices - 1, relay_back, (zeros_state, local_back))
    dpre, dkeys, dqueries, dvalues_mix, unused, skip_grad, dgate = pullback((dgated, end_grad))
    bias_grad = jnp.sum(dpre, axis=(0, 1))
    dpre_low = dpre.reshape(rows, inner).astype(jnp.bfloat16)
    beta_grad = contract(dpre_low, lowrank, 0, 0)
    dlowrank = jnp.dot(dpre_low, beta_wb, preferred_element_type=jnp.float32)
    dprojected = jnp.concatenate(
        [dlowrank, dkeys.reshape(rows, states), dqueries.reshape(rows, states)], axis=1
    ).astype(jnp.bfloat16)
    select_grad = contract(values_rows, dprojected, 0, 0)
    dvalues = contract(dprojected, select_b, 1, 1).reshape(count_seqs, length, inner) + dvalues_mix
    unused, conv_pull = jax.vjp(
        convolve, padded, conv_wb.astype(jnp.float32), conv_bb.astype(jnp.float32)
    )
    dpadded, conv_w_grad, conv_b_grad = conv_pull(dvalues)
    back_rim = passed_along(dpadded[:, : taps - 1, :].astype(jnp.bfloat16), "seq", -1).astype(
        jnp.float32
    )
    dconv_own = dpadded[:, taps - 1 :, :]
    dconv_in = jnp.concatenate(
        [dconv_own[:, : length - taps + 1, :], dconv_own[:, length - taps + 1 :, :] + back_rim],
        axis=1,
    )
    dmixed = jnp.concatenate(
        [dconv_in.reshape(rows, inner), dgate.reshape(rows, inner)], axis=1
    ).astype(jnp.bfloat16)
    in_grad = contract(normed, dmixed, 0, 0)
    dnormed = contract(dmixed, in_b, 1, 1)
    unused, norm_pull = jax.vjp(rms_scaled, flat, gain_b.astype(jnp.float32))
    dflat, gain_grad = norm_pull(dnormed)
    input_grad = (cot_low.astype(jnp.float32) + dflat).astype(jnp.bfloat16)
    grads = (
        lax.psum_scatter(gain_grad, ("dp", "seq"), scatter_dimension=0, tiled=True),
        lax.psum_scatter(in_grad, ("dp", "seq"), scatter_dimension=0, tiled=True),
        lax.psum_scatter(conv_w_grad, ("dp", "seq"), scatter_dimension=0, tiled=True),
        lax.psum_scatter(conv_b_grad, ("dp", "seq"), scatter_dimension=0, tiled=True),
        lax.psum_scatter(select_grad, ("dp", "seq"), scatter_dimension=0, tiled=True),
        lax.psum_scatter(beta_grad, ("dp", "seq"), scatter_dimension=0, tiled=True),
        lax.psum_scatter(bias_grad, ("dp", "seq"), scatter_dimension=0, tiled=True),
        lax.psum_scatter(skip_grad, ("dp", "seq"), scatter_dimension=0, tiled=True),
        lax.psum_scatter(out_grad, ("dp", "seq"), scatter_dimension=0, tiled=True),
    )
    return (
        result.reshape(count_seqs, length, width_d),
        input_grad.reshape(count_seqs, length, width_d),
    ) + tuple(grads)


def solution(mesh):
    in_specs = (
        P("dp", "seq", None),
        P("dp", "seq", None),
        P(("dp", "seq")),
        P(("dp", "seq"), None),
        P(("dp", "seq"), None),
        P(("dp", "seq")),
        P(("dp", "seq"), None),
        P(("dp", "seq"), None),
        P(("dp", "seq")),
        P(("dp", "seq")),
        P(("dp", "seq"), None),
    )
    out_specs = (
        P("dp", "seq", None),
        P("dp", "seq", None),
        P(("dp", "seq")),
        P(("dp", "seq"), None),
        P(("dp", "seq"), None),
        P(("dp", "seq")),
        P(("dp", "seq"), None),
        P(("dp", "seq"), None),
        P(("dp", "seq")),
        P(("dp", "seq")),
        P(("dp", "seq"), None),
    )
    return jax.shard_map(local, mesh=mesh, in_specs=in_specs, out_specs=out_specs, check_vma=False)
```

profile of v0, /device:TPU:25, one launch (start us, length us, event | category | flops | bytes accessed | tf_op | source)
XLA Modules:
  0.0 4037.7 jit_solution(8893176502942488308)
XLA Ops:
  10.9 40.3 all-reduce.72
  52.8 59.3 %all_gather.38 = bf16[4096,4]{0,1:T(4,128)(2,1)S(1)} all-gather(bf16[128,4]{0,1:T(4,128)(2,1)} %param.29), channel_id=1, replica_groups=mesh['dp'=8,'seq'=4] {'dp','seq'}, dimensions={0}, use_global_device_ids=true | all-gather | bytes 33792 | tf_op jit(solution)/shard_map/all_gather | solution.py:104
  112.1 94.5 %all-gather.8.cloned.1.call-done = bf16[2048,8192]{1,0:T(8,128)(2,1)} async-done(((bf16[64,8192]{1,0:T(8,128)(2,1)}), bf16[2048,8192]{1,0:T(8,128)(2,1)}) %all-gather.8.cloned.1.call-update) | async-done | bytes 33554448 | tf_op jit(solution)/shard_map/all_gather | solution.py:103
  206.6 17.4 fusion.301
  228.0 57.6 %all-gather = bf16[32,1,128]{2,1,0:T(2,128)(2,1)S(1)} all-gather(bf16[1,1,128]{2,1,0:T(2,128)(2,1)S(1)} %bitcast.1851), channel_id=1, replica_groups=mesh['dp'=8,'seq'=4] {'dp','seq'}, dimensions={0}, use_global_device_ids=true | all-gather | bytes 8448 | tf_op jit(solution)/shard_map/all_gather | solution.py:105
  285.6 63.9 %all-gather.1 = bf16[32,1,128]{2,1,0:T(2,128)(2,1)S(1)} all-gather(bf16[1,1,128]{2,1,0:T(2,128)(2,1)S(1)} %bitcast.1852), channel_id=1, replica_groups=mesh['dp'=8,'seq'=4] {'dp','seq'}, dimensions={0}, use_global_device_ids=true | all-gather | bytes 8448 | tf_op jit(solution)/shard_map/all_gather | solution.py:108
  349.6 63.8 %all-gather.2 = bf16[32,1,128]{2,1,0:T(2,128)(2,1)S(1)} all-gather(bf16[1,1,128]{2,1,0:T(2,128)(2,1)S(1)} %bitcast.1853), channel_id=1, replica_groups=mesh['dp'=8,'seq'=4] {'dp','seq'}, dimensions={0}, use_global_device_ids=true | all-gather | bytes 8448 | tf_op jit(solution)/shard_map/all_gather | solution.py:109
  416.7 21.6 fusion.260
  449.6 127.0 %while.105 = (s32[]{:T(128)}, f32[1,16,4096]{2,1,0:T(8,128)S(1)}, f32[1,16,4096]{2,1,0:T(8,128)S(1)}, s32[16]{0:T(128)}, f32[1,256,4096]{2,1,0:T(8,128)}, /*inde...) while((s32[]{:T(128)}, f32[1,16,4096]{2,1,0:T(8,128)S(1)}, ...), condition=%wide.region_3.4_spmd.clone, body=%wide.region_2.3_spmd.clone.sunk | while | flops 8585494 | bytes 2890342 | solution.py:64
  577.3 24.5 while.100
  578.6 4.6 collective-permute-done
  585.3 7.0 collective-permute-done
  594.3 6.7 collective-permute-done
  608.9 253.1 %while.103 = (s32[]{:T(128)}, f32[1,16,4096]{2,1,0:T(8,128)S(1)}, f32[16,1,16,4096]{3,2,1,0:T(8,128)}, f32[16,1,16,4096]{3,2,1,0:T(8,128)}, s32[16]{0:T(128)}, /...) while((s32[]{:T(128)}, f32[1,16,4096]{2,1,0:T(8,128)S(1)}, ...), condition=%wide.region_45.46_spmd, body=%wide.region_28.45_spmd.sunk | while | flops 9961749 | bytes 8660655 | solution.py:64
  848.7 3.9 fusion.475
  862.0 112.3 %while.106 = (s32[]{:T(128)}, f32[1,16,4096]{2,1,0:T(8,128)S(1)}, s32[16]{0:T(128)S(1)}, f32[16,1,16,4096]{3,2,1,0:T(8,128)}, f32[1,256,4096]{2,1,0:T(8,128)}, /...) while((s32[]{:T(128)}, f32[1,16,4096]{2,1,0:T(8,128)S(1)}, ...), condition=%wide.region_25.26_spmd.clone, body=%wide.region_24.25_spmd.clone.sunk | while | flops 5308695 | bytes 3152509 | solution.py:64
  975.1 19.0 while.102
  999.0 449.0 %while.104 = (s32[]{:T(128)}, f32[1,256,4096]{2,1,0:T(8,128)}, f32[1,256,16]{1,2,0:T(8,128)S(1)}, f32[1,256,4096]{2,1,0:T(8,128)}, f32[1,256,16]{1,2,0:T(8,128)S...) while((s32[]{:T(128)}, f32[1,256,4096]{2,1,0:T(8,128)}, ...), condition=%wide.region_127.128_spmd, body=%wide.region_46.127_spmd.sunk | while | flops 30023956 | bytes 19277820 | solution.py:64
  1448.1 6.5 fusion.440
  1456.9 14.8 multiply_reduce_fusion.115
  1482.1 174.6 %while.101 = (s32[]{:T(128)}, f32[1,16,4096]{2,1,0:T(8,128)S(1)}, f32[16,1,16,4096]{3,2,1,0:T(8,128)}, s32[16]{0:T(128)S(1)}, f32[1,256,4096]{2,1,0:T(8,128)}, /...) while((s32[]{:T(128)}, f32[1,16,4096]{2,1,0:T(8,128)S(1)}, ...), condition=%wide.region_23.24_spmd, body=%wide.region_6.23_spmd.sunk | while | flops 9961749 | bytes 8136359 | solution.py:64
  1647.7 3.9 fusion.472
  1656.7 8.5 fusion.288
  1666.6 13.2 fusion.293
  1679.9 6.9 fusion.442
  1693.3 25.8 fusion.266
  1720.7 9.8 fusion.271
  1730.6 16.4 fusion.273
  1747.0 54.2 %all-reduce.77 = (f32[2048]{0:T(1024)S(1)}, f32[4096]{0:T(1024)S(1)}, f32[4096]{0:T(1024)S(1)}, f32[4096]{0:T(1024)S(1)}) all-reduce(f32[2048]{0:T(1024)S(1)} %get-tuple-element.887, f32[4096]{0:T(1024)S(1)} %get-tuple-element.886, f32[4096]{0:T(1024)S(1)} %get-tuple-element.1267, ...), channel_id=2, replica_groups=mesh['dp'=8,'seq'=4] {'dp','seq'}, use_global_device_ids=true, to_apply=%region_131.132.clone | all-reduce | flops 14336 | bytes 114688
  1808.3 84.1 %reduce-scatter.10.cloned.1.call-done = f32[128,160]{0,1:T(8,128)} async-done(((f32[4096,160]{0,1:T(8,128)}), f32[128,160]{0,1:T(8,128)}) %reduce-scatter.10.cloned.1.call-update) | async-done | bytes 81936 | tf_op jit(solution)/shard_map/reduce_scatter | solution.py:214
  1892.5 724.7 %reduce-scatter.14.cloned.1.call-done = f32[128,2048]{1,0:T(8,128)} async-done(((f32[4096,2048]{1,0:T(8,128)}), f32[128,2048]{1,0:T(8,128)}) %reduce-scatter.14.cloned.1.call-update) | async-done | bytes 1048592 | tf_op jit(solution)/shard_map/reduce_scatter | solution.py:218
  2617.1 1413.9 %reduce-scatter.8.cloned.1.call-done = f32[64,8192]{1,0:T(8,128)} async-done(((f32[2048,8192]{1,0:T(8,128)}), f32[64,8192]{1,0:T(8,128)}) %reduce-scatter.8.cloned.1.call-update) | async-done | bytes 2097168 | tf_op jit(solution)/shard_map/reduce_scatter | solution.py:211
  (1535 shorter events, 1139.3 us)
Async XLA Ops:
  7.2 199.4 %all-gather.8.cloned.1.call-start = ((), (), s32[]{:S(2)}) async-start(), calls=%async_computation.5 | async-start | bytes 34603008 | tf_op jit(solution)/shard_map/all_gather | solution.py:103
  7.9 408.7 %all-gather.14.cloned.1.call-start = ((), (), s32[]{:S(2)}) async-start(), calls=%async_computation.8 | async-start | bytes 17301504 | tf_op jit(solution)/shard_map/all_gather | solution.py:110
  8.7 432.1 %all-gather.10.cloned.1.call-start = ((), (), s32[]{:S(2)}) async-start(), calls=%async_computation.6 | async-start | bytes 1351680 | tf_op jit(solution)/shard_map/all_gather | solution.py:106
  9.4 434.3 %all-gather.12.cloned.1.call-start = ((), (), s32[]{:S(2)}) async-start(), calls=%async_computation.7 | async-start | bytes 1081344 | tf_op jit(solution)/shard_map/all_gather | solution.py:107
  10.0 1796.9 %reduce-scatter.16.cloned.1.call-start = ((), (), s32[]{:S(2)}) async-start(), calls=%async_computation.13 | async-start | bytes 2162688
  51.2 155.3 %copy-start.18 = (f32[2048]{0:T(1024)}, f32[2048]{0:T(1024)S(1)}, u32[]{:S(2)}) copy-start(f32[2048]{0:T(1024)S(1)} %convert_element_type.86) | copy-start | bytes 24580
  52.8 171.2 %copy-start.34 = (f32[256]{0:T(256)}, f32[256]{0:T(256)S(1)}, u32[]{:S(2)}) copy-start(f32[256]{0:T(256)S(1)} %fusion.276) | copy-start | bytes 3076
  52.8 171.2 %copy-start.20 = (f32[256]{0:T(256)}, f32[256]{0:T(256)S(1)}, u32[]{:S(2)}) copy-start(f32[256]{0:T(256)S(1)} %fusion.306) | copy-start | bytes 3076
  224.0 61.6 %copy-start.37 = (bf16[128]{0:T(256)(128)(2,1)S(1)}, bf16[128]{0:T(256)(128)(2,1)}, u32[]{:S(2)}) copy-start(bf16[128]{0:T(256)(128)(2,1)} %param.33) | copy-start | bytes 772
  224.0 125.6 %copy-start.38 = (bf16[128]{0:T(256)(128)(2,1)S(1)}, bf16[128]{0:T(256)(128)(2,1)}, u32[]{:S(2)}) copy-start(bf16[128]{0:T(256)(128)(2,1)} %param.34) | copy-start | bytes 772
  226.6 187.5 %collective-permute-start.2 = (bf16[1,3,4096]{2,1,0:T(4,128)(2,1)S(1)}, bf16[1,3,4096]{2,1,0:T(4,128)(2,1)S(1)}, u32[]{:S(2)}, u32[]{:S(2)}) collective-permute-start(bf16[1,3,4096]{2,1,0:T(4,128)(2,1)S(1)} %slice.1716), channel_id=1, source_target_pairs={{0,1},{1,2},{2,3},{4,5},{5,6},{6,7},{8,9},{9,10},{10,11},{12,13},{... | collective-permute-start | bytes 73736 | tf_op jit(solution)/shard_map/ppermute | solution.py:10
  227.9 210.4 %copy-start.26 = (f32[4096,1]{0,1:T(1,128)}, f32[4096,1]{0,1:T(1,128)S(1)}, u32[]{:S(2)}) copy-start(f32[4096,1]{0,1:T(1,128)S(1)} %get-tuple-element.1714) | copy-start | bytes 49156
  227.9 210.4 %copy-start.28 = (f32[4096,1]{0,1:T(1,128)}, f32[4096,1]{0,1:T(1,128)S(1)}, u32[]{:S(2)}) copy-start(f32[4096,1]{0,1:T(1,128)S(1)} %get-tuple-element.1715) | copy-start | bytes 49156
  227.9 210.3 %copy-start.30 = (f32[4096,1]{0,1:T(1,128)}, f32[4096,1]{0,1:T(1,128)S(1)}, u32[]{:S(2)}) copy-start(f32[4096,1]{0,1:T(1,128)S(1)} %get-tuple-element.1716) | copy-start | bytes 49156
  228.0 210.3 %copy-start.32 = (f32[4096,1]{0,1:T(1,128)}, f32[4096,1]{0,1:T(1,128)S(1)}, u32[]{:S(2)}) copy-start(f32[4096,1]{0,1:T(1,128)S(1)} %get-tuple-element.1717) | copy-start | bytes 49156
  577.3 5.9 collective-permute-start
  584.0 8.3 collective-permute-start
  593.0 8.0 collective-permute-start
  975.1 5.4 collective-permute-start.1
  981.2 5.7 collective-permute-start.1
  987.6 5.7 collective-permute-start.1
  999.0 449.0 %copy-start.24 = (f32[256]{0:T(256)S(1)}, f32[256]{0:T(256)}, u32[]{:S(2)}) copy-start(f32[256]{0:T(256)} %copy-done.23) | copy-start | bytes 3076
  1473.7 334.6 %reduce-scatter.12.cloned.1.call-start = ((), (), s32[]{:S(2)}) async-start(), calls=%async_computation.11 | async-start | bytes 2162688 | tf_op jit(solution)/shard_map/reduce_scatter | solution.py:215
  1477.5 414.9 %reduce-scatter.10.cloned.1.call-start = ((), (), s32[]{:S(2)}) async-start(), calls=%async_computation.10 | async-start | bytes 2703360 | tf_op jit(solution)/shard_map/reduce_scatter | solution.py:214
  1479.6 1137.5 %reduce-scatter.14.cloned.1.call-start = ((), (), s32[]{:S(2)}) async-start(), calls=%async_computation.12 | async-start | bytes 34603008 | tf_op jit(solution)/shard_map/reduce_scatter | solution.py:218
  1656.7 9.9 copy-start.12
  1679.8 2351.2 %reduce-scatter.8.cloned.1.call-start = ((), (), s32[]{:S(2)}) async-start(), calls=%async_computation.9 | async-start | bytes 69206016 | tf_op jit(solution)/shard_map/reduce_scatter | solution.py:211
  1686.9 4.9 collective-permute-start.3
  1730.6 16.4 copy-start.25
  1730.6 73.0 %copy-start.35 = (f32[256]{0:T(256)S(1)}, f32[256]{0:T(256)}, u32[]{:S(2)}) copy-start(f32[256]{0:T(256)} %copy-done.34) | copy-start | bytes 3076
  1730.6 73.0 %copy-start.8 = (bf16[1,256,2048]{2,1,0:T(8,128)(2,1)S(1)}, bf16[1,256,2048]{2,1,0:T(8,128)(2,1)}, u32[]{:S(2)}) copy-start(bf16[1,256,2048]{2,1,0:T(8,128)(2,1)} %param.25) | copy-start | bytes 3145732
  1730.6 73.0 %copy-start.13 = (bf16[1,256,2048]{2,1,0:T(8,128)(2,1)S(1)}, bf16[1,256,2048]{2,1,0:T(8,128)(2,1)}, u32[]{:S(2)}) copy-start(bf16[1,256,2048]{2,1,0:T(8,128)(2,1)} %param.26) | copy-start | bytes 3145732
  (24 other events, 156.0 us)
Sparse Core Ops, SparseCore 0:
  10.9 195.5 all-gather.7
  209.6 113.7 all-gather.13
  326.2 48.3 all-gather.9
  377.4 53.4 all-gather.11
  1473.8 137.7 reduce-scatter.15
  1614.5 135.8 reduce-scatter.11
  1753.2 139.2 reduce-scatter.9
  1895.3 721.7 reduce-scatter.13
  2620.1 1410.8 reduce-scatter.7
where the time goes:
time: 4060 us; the launch traced here: 4040 us
  waiting for transfers between devices  2340 us (58%)
  other arithmetic  824 us (20%)
  blocking collectives  339 us (8%)
  local copies, waits for them, and re-layouts  305 us (8%)
  matrix products  130 us (3%)
  loops' own time  60.2 us (1%)
    reduce_scatter x1, waiting for transfers between devices, local(): lax.psum_scatter(in_grad, ('dp', 'seq'), scatter_dimension=0, tiled=True)  1410 us
    reduce_scatter x1, waiting for transfers between devices, local(): lax.psum_scatter(out_grad, ('dp', 'seq'), scatter_dimension=0, tiled=True)  725 us
    mul x256, other arithmetic, block(): rate_now * value_rows[:, offset, None, :]  220 us
    reduce_sum x224, other arithmetic, block(): emitted.append(jnp.sum(state * query_rows[:, offset, :, None], axis=1))  133 us
    add_any x96, other arithmetic, block(): decay = 1.0 - rate_now * (key_now * key_now)  108 us
    reduce_sum x128, other arithmetic, block(): decay = 1.0 - rate_now * (key_now * key_now)  108 us
    dot_general x8, matrix products, contract(): lax.dot_general(left, right, (((left_dim,), (right_dim,)), ((), ())), pre...  99.5 us
    unnamed x2, blocking collectives  94.6 us
  transfers between devices with their start and end apart: 17, of which 11 were waited for; matrix products, arithmetic and copies ran while one was open for 8% of the time, Pallas kernels for 0%

commit v1 on v0

v1 whole, which is shorter than its diff:
```python
import jax
import jax.numpy as jnp
from jax import lax
from jax.experimental import pallas as pl
from jax.experimental.pallas import tpu as pltpu
from jax.sharding import PartitionSpec as P

LANE = 128


def sigmoid(v):
    return 1.0 / (1.0 + jnp.exp(-v))


def by_eights(value):
    return value.reshape(value.shape[0] // 8, 8, value.shape[1])


def as_rows(value):
    return value.reshape(value.shape[0] * 8, value.shape[2])


def spread_columns(row_ref, key_ref, query_ref, rows, states):
    lane = lax.broadcasted_iota(jnp.int32, (states, LANE), 1)
    entry = lax.broadcasted_iota(jnp.int32, (states, LANE), 0)
    pick_key = lane == entry
    pick_query = lane == entry + states

    def body(group, carry):
        for offset in range(8):
            t = group * 8 + offset
            row = jnp.broadcast_to(row_ref[group, offset : offset + 1, :], (states, LANE))
            at = pl.multiple_of(t * states, states)
            key = jnp.sum(jnp.where(pick_key, row, 0.0), axis=1, keepdims=True)
            query = jnp.sum(jnp.where(pick_query, row, 0.0), axis=1, keepdims=True)
            key_ref[pl.ds(at, states), :] = jnp.broadcast_to(key, (states, LANE))
            query_ref[pl.ds(at, states), :] = jnp.broadcast_to(query, (states, LANE))
        return carry

    lax.fori_loop(0, rows // 8, body, 0)


def step_sizes(low_ref, kq_ref, weight_ref, bias_ref, states):
    pre = lax.dot_general(
        low_ref[...], weight_ref[...], (((1,), (1,)), ((), ())), preferred_element_type=jnp.float32
    )
    beta = sigmoid(pre + bias_ref[...])
    lane = lax.broadcasted_iota(jnp.int32, kq_ref.shape, 1)
    keys = jnp.where(lane < states, kq_ref[...], 0.0)
    square = jnp.sum(keys * keys, axis=1, keepdims=True)
    return beta, 1.0 / (1.0 + beta * square)


def forward_body(
    states, low_ref, kq_ref, values_ref, gate_ref, weight_ref, bias_ref, skip_ref,
    gated_ref, mixed_ref, history_ref, final_ref,
    state_ref, key_ref, query_ref, rate_ref, input_ref, out_ref, row_ref,
):
    rows, channels = values_ref.shape
    tiles = channels // LANE
    per_group = min(4, tiles)

    @pl.when(pl.program_id(0) == 0)
    def _():
        state_ref[...] = jnp.zeros_like(state_ref)

    beta, inverse = step_sizes(low_ref, kq_ref, weight_ref, bias_ref, states)
    rates = beta * inverse
    rate_ref[...] = by_eights(rates)
    input_ref[...] = by_eights(rates * values_ref[...].astype(jnp.float32))
    row_ref[...] = by_eights(kq_ref[...])
    spread_columns(row_ref, key_ref, query_ref, rows, states)

    for first in range(0, tiles, per_group):
        columns = [slice((first + j) * LANE, (first + j + 1) * LANE) for j in range(per_group)]

        def body(group, carry):
            carry = list(carry)
            for offset in range(8):
                t = group * 8 + offset
                at = pl.multiple_of(t * states, states)
                key = key_ref[pl.ds(at, states), :]
                query = query_ref[pl.ds(at, states), :]
                square = key * key
                for j, cols in enumerate(columns):
                    history_ref[pl.ds(at, states), cols] = carry[j].astype(jnp.bfloat16)
                    rate = rate_ref[group, offset : offset + 1, cols]
                    fed = input_ref[group, offset : offset + 1, cols]
                    carry[j] = (1.0 - rate * square) * carry[j] + key * fed
                    out_ref[group, offset : offset + 1, cols] = jnp.sum(query * carry[j], axis=0, keepdims=True)
            return tuple(carry)

        done = lax.fori_loop(0, rows // 8, body, tuple(state_ref[:, cols] for cols in columns))
        for cols, state in zip(columns, done):
            state_ref[:, cols] = state

    mixed = as_rows(out_ref[...]) + skip_ref[...] * values_ref[...].astype(jnp.float32)
    gate = gate_ref[...]
    mixed_ref[...] = mixed
    gated_ref[...] = (mixed * gate * sigmoid(gate)).astype(jnp.bfloat16)

    @pl.when(pl.program_id(0) == pl.num_programs(0) - 1)
    def _():
        final_ref[...] = state_ref[...]


def forward_scan(low, kq, values, gate, weight, bias, skip, states):
    length, channels = values.shape
    rank = low.shape[1]
    rows = min(128, length)
    blocks = length // rows
    by_row = lambda width: pl.BlockSpec((rows, width), lambda i: (i, 0))
    whole = lambda a: pl.BlockSpec(a.shape, lambda i: (0, 0))
    return pl.pallas_call(
        lambda *refs: forward_body(states, *refs),
        grid=(blocks,),
        in_specs=[by_row(rank), by_row(LANE), by_row(channels), by_row(channels), whole(weight), whole(bias), whole(skip)],
        out_specs=[
            by_row(channels),
            by_row(channels),
            pl.BlockSpec((rows * states, channels), lambda i: (i, 0)),
            pl.BlockSpec((states, channels), lambda i: (0, 0)),
        ],
        out_shape=[
            jax.ShapeDtypeStruct((length, channels), jnp.bfloat16),
            jax.ShapeDtypeStruct((length, channels), jnp.float32),
            jax.ShapeDtypeStruct((length * states, channels), jnp.bfloat16),
            jax.ShapeDtypeStruct((states, channels), jnp.float32),
        ],
        scratch_shapes=[
            pltpu.VMEM((states, channels), jnp.float32),
            pltpu.VMEM((rows * states, LANE), jnp.float32),
            pltpu.VMEM((rows * states, LANE), jnp.float32),
            pltpu.VMEM((rows // 8, 8, channels), jnp.float32),
            pltpu.VMEM((rows // 8, 8, channels), jnp.float32),
            pltpu.VMEM((rows // 8, 8, channels), jnp.float32),
            pltpu.VMEM((rows // 8, 8, LANE), jnp.float32),
        ],
        compiler_params=pltpu.CompilerParams(vmem_limit_bytes=48 * 1024 * 1024),
        cost_estimate=pl.CostEstimate(flops=14 * length * states * channels, bytes_accessed=2 * length * states * channels, transcendentals=0),
    )(low, kq, values, gate, weight, bias, skip)


def backward_body(
    states, low_ref, kq_ref, values_ref, gate_ref, mixed_ref, dgated_ref, history_ref, final_ref, weight_ref, bias_ref, skip_ref,
    dgate_ref, dpre_ref, dvalues_ref, dlow_ref, dkq_ref, bias_grad_ref, skip_grad_ref,
    grad_ref, state_ref, key_ref, query_ref, rate_ref, do_ref, values32_ref, fed_ref, kept_ref, part_key_ref, part_query_ref, row_ref, placed_ref,
):
    rows, channels = values_ref.shape
    tiles = channels // LANE
    per_group = min(4, tiles)

    @pl.when(pl.program_id(0) == 0)
    def _():
        grad_ref[...] = jnp.zeros_like(grad_ref)
        state_ref[...] = final_ref[...]
        bias_grad_ref[...] = jnp.zeros_like(bias_grad_ref)
        skip_grad_ref[...] = jnp.zeros_like(skip_grad_ref)

    beta, inverse = step_sizes(low_ref, kq_ref, weight_ref, bias_ref, states)
    rate_ref[...] = by_eights(beta * inverse)
    values = values_ref[...].astype(jnp.float32)
    values32_ref[...] = by_eights(values)
    gate = gate_ref[...]
    dgated = dgated_ref[...].astype(jnp.float32)
    s = sigmoid(gate)
    do = dgated * (gate * s)
    do_ref[...] = by_eights(do)
    dgate_ref[...] = (dgated * mixed_ref[...] * (s + gate * s * (1.0 - s))).astype(jnp.bfloat16)
    skip_grad_ref[...] += jnp.sum(do * values, axis=0, keepdims=True)
    row_ref[...] = by_eights(kq_ref[...])
    spread_columns(row_ref, key_ref, query_ref, rows, states)

    for first in range(0, tiles, per_group):
        columns = [slice((first + j) * LANE, (first + j + 1) * LANE) for j in range(per_group)]

        def body(step, carry):
            grads, lates = list(carry[0]), list(carry[1])
            group = rows // 8 - 1 - step
            for offset in reversed(range(8)):
                t = group * 8 + offset
                at = pl.multiple_of(t * states, states)
                key = key_ref[pl.ds(at, states), :]
                query = query_ref[pl.ds(at, states), :]
                sum_key = None
                sum_query = None
                for j, cols in enumerate(columns):
                    rate = rate_ref[group, offset : offset + 1, cols]
                    out_grad = do_ref[group, offset : offset + 1, cols]
                    value = values32_ref[group, offset : offset + 1, cols]
                    before = history_ref[pl.ds(at, states), cols].astype(jnp.float32)
                    grad = grads[j] + query * out_grad
                    scaled = rate * grad
                    by_key = key * scaled
                    kept = scaled * before
                    fed_ref[group, offset : offset + 1, cols] = jnp.sum(by_key, axis=0, keepdims=True)
                    kept_ref[group, offset : offset + 1, cols] = jnp.sum(key * (key * kept), axis=0, keepdims=True)
                    term_key = value * scaled - 2.0 * (key * kept)
                    term_query = lates[j] * out_grad
                    sum_key = term_key if sum_key is None else sum_key + term_key
                    sum_query = term_query if sum_query is None else sum_query + term_query
                    grads[j] = grad - key * by_key
                    lates[j] = before
                if first == 0:
                    part_key_ref[pl.ds(at, states), :] = sum_key
                    part_query_ref[pl.ds(at, states), :] = sum_query
                else:
                    part_key_ref[pl.ds(at, states), :] += sum_key
                    part_query_ref[pl.ds(at, states), :] += sum_query
            return (tuple(grads), tuple(lates))

        start = (tuple(grad_ref[:, cols] for cols in columns), tuple(state_ref[:, cols] for cols in columns))
        grads, lates = lax.fori_loop(0, rows // 8, body, start)
        for cols, grad, late in zip(columns, grads, lates):
            grad_ref[:, cols] = grad
            state_ref[:, cols] = late

    fed = as_rows(fed_ref[...])
    dvalues_ref[...] = fed + skip_ref[...] * as_rows(do_ref[...])
    scaled = as_rows(values32_ref[...]) * fed - as_rows(kept_ref[...])
    beta, inverse = step_sizes(low_ref, kq_ref, weight_ref, bias_ref, states)
    dpre = scaled * (1.0 - beta) * inverse
    bias_grad_ref[...] += jnp.sum(dpre, axis=0, keepdims=True)
    dpre_low = dpre.astype(jnp.bfloat16)
    dpre_ref[...] = dpre_low
    dlow_ref[...] = jnp.dot(dpre_low, weight_ref[...], preferred_element_type=jnp.float32)
    through = -2.0 * jnp.sum(scaled * beta * inverse, axis=1, keepdims=True)

    lane = lax.broadcasted_iota(jnp.int32, (states, LANE), 1)
    entry = lax.broadcasted_iota(jnp.int32, (states, LANE), 0)

    def gather(group, carry):
        for offset in range(8):
            t = group * 8 + offset
            at = pl.multiple_of(t * states, states)
            key = jnp.sum(part_key_ref[pl.ds(at, states), :], axis=1, keepdims=True)
            query = jnp.sum(part_query_ref[pl.ds(at, states), :], axis=1, keepdims=True)
            placed = jnp.where(lane == entry, key, 0.0) + jnp.where(lane == entry + states, query, 0.0)
            placed_ref[group, offset : offset + 1, :] = jnp.sum(placed, axis=0, keepdims=True)
        return carry

    lax.fori_loop(0, rows // 8, gather, 0)
    lanes = lax.broadcasted_iota(jnp.int32, kq_ref.shape, 1)
    dkq_ref[...] = as_rows(placed_ref[...]) + jnp.where(lanes < states, kq_ref[...] * through, 0.0)


def backward_scan(low, kq, values, gate, mixed, dgated, history, final, weight, bias, skip, states):
    length, channels = values.shape
    rank = low.shape[1]
    rows = min(128, length)
    blocks = length // rows
    by_row = lambda width: pl.BlockSpec((rows, width), lambda i: (blocks - 1 - i, 0))
    whole = lambda a: pl.BlockSpec(a.shape, lambda i: (0, 0))
    total = pl.BlockSpec((1, channels), lambda i: (0, 0))
    wide = pltpu.VMEM((rows // 8, 8, channels), jnp.float32)
    spread = pltpu.VMEM((rows * states, LANE), jnp.float32)
    return pl.pallas_call(
        lambda *refs: backward_body(states, *refs),
        grid=(blocks,),
        in_specs=[
            by_row(rank), by_row(LANE), by_row(channels), by_row(channels), by_row(channels), by_row(channels),
            pl.BlockSpec((rows * states, channels), lambda i: (blocks - 1 - i, 0)),
            whole(final), whole(weight), whole(bias), whole(skip),
        ],
        out_specs=[by_row(channels), by_row(channels), by_row(channels), by_row(rank), by_row(LANE), total, total],
        out_shape=[
            jax.ShapeDtypeStruct((length, channels), jnp.bfloat16),
            jax.ShapeDtypeStruct((length, channels), jnp.bfloat16),
            jax.ShapeDtypeStruct((length, channels), jnp.float32),
            jax.ShapeDtypeStruct((length, rank), jnp.float32),
            jax.ShapeDtypeStruct((length, LANE), jnp.float32),
            jax.ShapeDtypeStruct((1, channels), jnp.float32),
            jax.ShapeDtypeStruct((1, channels), jnp.float32),
        ],
        scratch_shapes=[
            pltpu.VMEM((states, channels), jnp.float32),
            pltpu.VMEM((states, channels), jnp.float32),
            spread, spread, wide, wide, wide, wide, wide, spread, spread,
            pltpu.VMEM((rows // 8, 8, LANE), jnp.float32), pltpu.VMEM((rows // 8, 8, LANE), jnp.float32),
        ],
        compiler_params=pltpu.CompilerParams(vmem_limit_bytes=56 * 1024 * 1024),
        cost_estimate=pl.CostEstimate(flops=30 * length * states * channels, bytes_accessed=2 * length * states * channels, transcendentals=0),
    )(low, kq, values, gate, mixed, dgated, history, final, weight, bias, skip)


def contract(left, right, left_dim, right_dim):
    return lax.dot_general(
        left, right, (((left_dim,), (right_dim,)), ((), ())), preferred_element_type=jnp.float32
    )


def gathered(shard, axis):
    return lax.all_gather(shard, axis, axis=0, tiled=True)


def scattered(total, axis):
    return lax.psum_scatter(total, axis, scatter_dimension=0, tiled=True)


def summed_rows(partial, axis):
    size = lax.axis_size(axis)
    parts = partial.astype(jnp.bfloat16).reshape((size, partial.shape[0] // size) + partial.shape[1:])
    parts = lax.all_to_all(parts, axis, 0, 0)
    return jnp.sum(parts.astype(jnp.float32), axis=0)


def later(rows, by):
    if by == 0:
        return rows
    return jnp.pad(rows, ((by, 0), (0, 0)))[: rows.shape[0]]


def sooner(rows, by):
    if by == 0:
        return rows
    return jnp.pad(rows, ((0, by), (0, 0)))[by:]


def local(
    tokens,
    cotangent,
    norm_gain,
    in_weight,
    conv_weight,
    conv_bias,
    select_weight,
    beta_weight,
    beta_bias,
    skip_gain,
    out_weight,
):
    parts, dps = lax.axis_size("seq"), lax.axis_size("dp")
    rows, width = tokens.shape[1:]
    block = conv_weight.shape[0]
    channels = block * dps
    taps = conv_weight.shape[1]
    rank = beta_weight.shape[1]
    states = (select_weight.shape[1] - rank) // 2
    own = in_weight.shape[0]

    gain = gathered(norm_gain, ("dp", "seq")).astype(jnp.float32)
    flat = tokens.reshape(rows, width).astype(jnp.float32)
    scale = lax.rsqrt(jnp.mean(flat * flat, axis=-1, keepdims=True) + 1e-05)
    normed = gathered((flat * scale * gain).astype(jnp.bfloat16), "seq")
    spread = in_weight.reshape(own, 2, dps, parts, block).transpose(3, 0, 1, 2, 4).reshape(parts, own, 2 * channels)
    in_w = gathered(lax.all_to_all(spread, "seq", 0, 0).reshape(parts * own, 2 * channels), "dp")
    conv_w = gathered(conv_weight, "dp").astype(jnp.float32)
    conv_b = gathered(conv_bias, "dp").astype(jnp.float32)
    select_w = gathered(select_weight, "dp")
    beta_w = gathered(beta_weight, "dp")
    beta_b = gathered(beta_bias, "dp").astype(jnp.float32).reshape(1, channels)
    skip = gathered(skip_gain, "dp").astype(jnp.float32).reshape(1, channels)
    out_w = gathered(out_weight, "dp")
    cot = gathered(cotangent.reshape(rows, width), "seq")

    conv_in = jnp.dot(normed, in_w[:, :channels], preferred_element_type=jnp.float32).astype(jnp.bfloat16)
    gate = jnp.dot(normed, in_w[:, channels:], preferred_element_type=jnp.float32)
    conv_wide = conv_in.astype(jnp.float32)
    conv_sum = conv_b
    for tap in range(taps):
        conv_sum = conv_sum + later(conv_wide, taps - 1 - tap) * conv_w[:, tap]
    values = jax.nn.silu(conv_sum).astype(jnp.bfloat16)
    projected = lax.psum(jnp.dot(values, select_w, preferred_element_type=jnp.float32), "seq")
    low = projected[:, :rank].astype(jnp.bfloat16)
    kq = jnp.pad(projected[:, rank:], ((0, 0), (0, LANE - 2 * states)))

    gated, mixed, history, final = forward_scan(low, kq, values, gate, beta_w, beta_b, skip, states)
    result_part = jnp.dot(gated, out_w, preferred_element_type=jnp.float32)
    result = (flat + summed_rows(result_part, "seq")).astype(jnp.bfloat16)
    out_grad = summed_rows(contract(gated, cot, 0, 0), "dp")
    dgated = contract(cot, out_w, 1, 1)
    dgate, dpre_low, dvalues, dlow, dkq, bias_grad, skip_grad = backward_scan(
        low, kq, values, gate, mixed, dgated, history, final, beta_w, beta_b, skip, states
    )
    dprojected = lax.psum(jnp.concatenate([dlow, dkq[:, : 2 * states]], axis=1), "seq").astype(jnp.bfloat16)
    beta_grad = scattered(contract(dpre_low, low, 0, 0), "dp")
    select_grad = scattered(contract(values, dprojected, 0, 0), "dp")
    dvalues = contract(dprojected, select_w, 1, 1) + dvalues
    s = jax.nn.sigmoid(conv_sum)
    dconv = dvalues * (s + conv_sum * s * (1.0 - s))
    conv_w_grad = jnp.stack(
        [jnp.sum(dconv * later(conv_wide, taps - 1 - tap), axis=0) for tap in range(taps)], axis=1
    )
    conv_b_grad = jnp.sum(dconv, axis=0)
    dconv_in = 0.0
    for tap in range(taps):
        dconv_in = dconv_in + sooner(dconv, taps - 1 - tap) * conv_w[:, tap]
    dmixed = jnp.concatenate([dconv_in.astype(jnp.bfloat16), dgate], axis=1)
    in_grad = summed_rows(contract(normed, dmixed, 0, 0), "dp").astype(jnp.bfloat16)
    in_grad = lax.all_to_all(in_grad.reshape(parts, own, 2 * channels), "seq", 0, 0)
    in_grad = in_grad.reshape(parts, own, 2, dps, block).transpose(1, 2, 3, 0, 4).reshape(own, 2 * parts * channels)
    dnormed = summed_rows(contract(dmixed, in_w, 1, 1), "seq")
    v = dnormed * gain
    du = scale * v - flat * (scale * scale * scale) * jnp.mean(flat * v, axis=-1, keepdims=True)
    input_grad = (cotangent.reshape(rows, width).astype(jnp.float32) + du).astype(jnp.bfloat16)
    gain_grad = scattered(jnp.sum(dnormed * flat * scale, axis=0), ("dp", "seq"))
    rows_grad = scattered(
        jnp.concatenate(
            [conv_w_grad, conv_b_grad[:, None], bias_grad.reshape(channels, 1), skip_grad.reshape(channels, 1)], axis=1
        ),
        "dp",
    )
    return (
        result.reshape(tokens.shape),
        input_grad.reshape(tokens.shape),
        gain_grad,
        in_grad.astype(jnp.float32),
        rows_grad[:, :taps],
        rows_grad[:, taps],
        select_grad,
        beta_grad,
        rows_grad[:, taps + 1],
        rows_grad[:, taps + 2],
        out_grad,
    )


def solution(mesh):
    split = P(("dp", "seq"))
    rows = P("dp", "seq", None)
    return jax.shard_map(
        local,
        mesh=mesh,
        in_specs=(rows, rows) + (split,) * 9,
        out_specs=(rows, rows) + (split,) * 9,
        check_vma=False,
    )
```

time: 4060 us -> 980 us (0.24)
  waiting for transfers between devices: 2340 us -> 405 us
  other arithmetic: 824 us -> 32.9 us
  local copies, waits for them, and re-layouts: 305 us -> 16.6 us
  Pallas kernels: 0 us -> 147 us
  blocking collectives: 339 us -> 229 us
  loops' own time: 60.2 us -> 0 us
  matrix products: 130 us -> 82.5 us
    reduce_scatter x4 -> x3, waiting for transfers between devices: 2220 us -> 32.8 us  [scattered(): return lax.psum_scatter(total, axis, scatter_dimension=0, tiled=True)]
    mul x384 -> x1, other arithmetic: 351 us -> 0.01 us  [local(): scale * scale * scale]
    reduce_sum x354 -> x7, other arithmetic: 249 us -> 22.9 us  [the longest x4 16.8 us: summed_rows(): return jnp.sum(parts.astype(jnp.float32), axis=0)]
    all_to_all x0 -> x5, waiting for transfers between devices: none -> 215 us  [the longest x4 215 us: summed_rows(): parts = lax.all_to_all(parts, axis, 0, 0)]
    all_gather x4 -> x6, blocking collectives: 245 us -> 53 us  [gathered(): return lax.all_gather(shard, axis, axis=0, tiled=True)]
    add_any x129 -> x0, other arithmetic: 173 us -> none  [the longest x96 108 us: block(): decay = 1.0 - rate_now * (key_now * key_now)]
    pallas_call x0 -> x2, Pallas kernels: none -> 147 us  [the longest x1 98.1 us: backward_scan(): pl.pallas_call(lambda *refs: backward_body(states, *refs), grid=(blocks,)...]
    dynamic_slice x80 -> x0, local copies, waits for them, and re-layouts: 67.9 us -> none  [recurrence(): lax.scan(jax.checkpoint(block), carry_init, jnp.arange(blocks))]
  transfers between devices with their start and end apart: 17 -> 13, of which waited for: 11 -> 8; matrix products, arithmetic and copies ran while one was open for 8% -> 11% of each run, Pallas kernels for 0% -> 0%
where the time goes in v1:
time: 980 us; the launch traced here: 969 us
  waiting for transfers between devices  405 us (41%)
  blocking collectives  229 us (23%)
  Pallas kernels  147 us (15%)
  matrix products  82.5 us (8%)
  starting transfers between devices  41.8 us (4%)
  other arithmetic  32.9 us (3%)
  local copies, waits for them, and re-layouts  16.6 us (2%)
  between operations  14.8 us (2%)
    all_to_all x4, waiting for transfers between devices, summed_rows(): parts = lax.all_to_all(parts, axis, 0, 0)  215 us
    all_gather x4, waiting for transfers between devices, gathered(): return lax.all_gather(shard, axis, axis=0, tiled=True)  116 us
    pallas_call x1, Pallas kernels, backward_scan(): pl.pallas_call(lambda *refs: backward_body(states, *refs), grid=(blocks,)...  98.1 us
    unnamed x2, blocking collectives  86.1 us
    dot_general x7, matrix products, contract(): lax.dot_general(left, right, (((left_dim,), (right_dim,)), ((), ())), pre...  55.1 us
    all_gather x6, blocking collectives, gathered(): return lax.all_gather(shard, axis, axis=0, tiled=True)  53 us
    all_to_all x1, blocking collectives, local(): lax.all_to_all(spread, 'seq', 0, 0).reshape(parts * own, 2 * channels)  50.7 us
    pallas_call x1, Pallas kernels, forward_scan(): pl.pallas_call(lambda *refs: forward_body(states, *refs), grid=(blocks,),...  48.5 us
  transfers between devices with their start and end apart: 13, of which 8 were waited for; matrix products, arithmetic and copies ran while one was open for 11% of the time, Pallas kernels for 0%

profile of v1, /device:TPU:25, one launch (start us, length us, event | category | flops | bytes accessed | tf_op | source)
XLA Modules:
  0.0 969.4 jit_solution(10631214784816111458)
XLA Ops:
  9.6 44.7 %all-reduce.7 = bf16[2048]{0:T(1024)(128)(2,1)S(1)} all-reduce(bf16[2048]{0:T(1024)(128)(2,1)S(1)} %dynamic-update-slice), channel_id=1, replica_groups=mesh['dp'=8,'seq'=4] {'dp','seq'}, use_global_device_ids=true, to_apply=%add.7 | all-reduce | flops 2048 | bytes 8192
  59.9 50.7 %all_to_all.30 = bf16[4,64,2048]{2,1,0:T(8,128)(2,1)} all-to-all(bf16[4,64,2048]{2,1,0:T(8,128)(2,1)S(1)} %reshape.166), channel_id=1, replica_groups=mesh['dp'=8,'seq'=4] {'seq'}, dimensions={0} | all-to-all | bytes 2097152 | tf_op jit(solution)/shard_map/all_to_all | solution.py:346
  110.6 10.0 %all-gather.1 = bf16[8,1,128]{2,1,0:T(2,128)(2,1)S(1)} all-gather(bf16[1,1,128]{2,1,0:T(2,128)(2,1)S(1)} %bitcast.122), channel_id=1, replica_groups=mesh['dp'=8,'seq'=4] {'dp'}, dimensions={0}, use_global_device_ids=true | all-gather | bytes 2304 | tf_op jit(solution)/shard_map/all_gather | solution.py:293
  120.6 8.3 all-gather.2
  128.9 8.2 all-gather.3
  137.1 8.4 all_gather.37
  145.6 9.1 all_gather.39.refs_4_.refs_8_
  154.7 8.9 all_gather.38
  163.7 10.2 %fusion.13.refs_5_ = f32[1024,1024]{1,0:T(8,128)} fusion(bf16[1024,2048]{1,0:T(8,128)(2,1)} %all-gather.13.cloned.1.call-done, bf16[1,1024,2048]{2,1,0:T(8,128)(2,1)} %all-gather.15.cloned.1.call-done), kind=kOutput, calls=%fused_computation.24 | convolution fusion | flops 4294967296 | bytes 12582912 | tf_op jit(solution)/shard_map/dot_general | solution.py:287
  174.0 58.5 %all-gather.9.cloned.1.call-done = bf16[1024,2048]{1,0:T(8,128)(2,1)} async-done(((bf16[256,2048]{1,0:T(8,128)(2,1)}), bf16[1024,2048]{1,0:T(8,128)(2,1)}) %all-gather.9.cloned.1.call-update) | async-done | bytes 4194320 | tf_op jit(solution)/shard_map/all_gather | solution.py:293
  232.5 57.6 %all-gather.11.cloned.1.call-done = bf16[2048,2048]{1,0:T(8,128)(2,1)} async-done(((bf16[256,2048]{1,0:T(8,128)(2,1)}), bf16[2048,2048]{1,0:T(8,128)(2,1)}) %all-gather.11.cloned.1.call-update) | async-done | bytes 8388624 | tf_op jit(solution)/shard_map/all_gather | solution.py:293
  290.2 7.7 convert_convert_fusion
  303.6 9.9 %fusion.7.refs_3_ = f32[1024,1024]{1,0:T(8,128)} fusion(bf16[1024,2048]{1,0:T(8,128)(2,1)} %all-gather.9.cloned.1.call-done, bf16[2048,2048]{1,0:T(8,128)(2,1)} %all-gather.11.cloned.1.call-done), kind=kOutput, calls=%fused_computation.17 | convolution fusion | flops 4294967296 | bytes 12582912 | tf_op jit(solution)/shard_map/dot_general | solution.py:357
  313.5 40.0 %all-reduce.12.cloned.1.call-done = f32[1024,160]{1,0:T(8,128)} async-done(((f32[1024,160]{1,0:T(8,128)}), f32[1024,160]{1,0:T(8,128)}) %all-reduce.12.cloned.1.call-update) | async-done | bytes 655376 | tf_op jit(solution)/shard_map/psum | solution.py:363
  356.0 48.5 %shard_map.194 = (bf16[1024,1024]{1,0:T(8,128)(2,1)S(1)}, f32[1024,1024]{1,0:T(8,128)}, bf16[16384,1024]{1,0:T(8,128)(2,1)}, f32[16,1024]{1,0:T(8,128)S(1)}) custom-call(bf16[1024,128]{1,0:T(8,128)(2,1)S(1)} %slice.138.refs_0_, f32[1024,128]{1,0:T(8,128)S(1)} %pad.34.refs_1_, bf16[1024,1024]{1,0:T(8,128)(2,1)S(1)} %get-tuple-element.40.refs_2_, ...), custom_call_target="tpu_custom_call" | custom-call | flops 234881024 | bytes 33554432 | tf_op jit(solution)/shard_map/pallas_call | solution.py:114
  406.4 98.1 %shard_map.195 = (bf16[1024,1024]{1,0:T(8,128)(2,1)}, bf16[1024,1024]{1,0:T(8,128)(2,1)}, f32[1024,1024]{1,0:T(8,128)}, f32[1024,128]{1,0:T(8,128)}, f32[1024,12...) custom-call(bf16[1024,128]{1,0:T(8,128)(2,1)} %copy-done.4, f32[1024,128]{1,0:T(8,128)} %copy-done.2, ...), custom_call_target="tpu_custom_call" | custom-call | flops 503316480 | bytes 33554432 | tf_op jit(solution)/shard_map/pallas_call | solution.py:257
  505.8 39.3 %all-reduce.13 = bf16[1024,160]{1,0:T(8,128)(2,1)} all-reduce(f32[1024,160]{1,0:T(8,128)S(1)} %pad_maximum_fusion.3), channel_id=1, replica_groups=mesh['dp'=8,'seq'=4] {'seq'}, use_global_device_ids=true, to_apply=%region_3.4 | all-reduce | flops 163840 | bytes 983040 | tf_op jit(solution)/shard_map/psum | solution.py:375
  545.0 8.3 fusion.15
  553.3 8.5 all-to-all-start.5
  572.4 12.6 %convolution_convert_fusion.1 = bf16[1024,2048]{1,0:T(8,128)(2,1)} fusion(bf16[2048,2048]{1,0:T(8,128)(2,1)} %all-gather.11.cloned.1.call-done, bf16[1024,1024]{1,0:T(8,128)(2,1)S(1)} %copy-done.25, bf16[1024,1024]{1,0:T(8,128)(2,1)S(1)} %get-tuple-element.42), kind=kOutput, calls=%fused_computation.33 | convolution fusion | flops 8600420352 | bytes 16777216 | tf_op jit(solution)/shard_map/dot_general | solution.py:287
  585.0 22.4 %all-to-all-done.5 = bf16[8,128,2048]{2,1,0:T(8,128)(2,1)} async-done(((bf16[8,128,2048]{2,1,0:T(8,128)(2,1)}), bf16[8,128,2048]{2,1,0:T(8,128)(2,1)}, u32[]{:S(2)}, u32[]{:S(2)}) %all-to-all-start.5) | async-done | bytes 4194336 | tf_op jit(solution)/shard_map/all_to_all | solution.py:303
  607.4 6.6 all-to-all-start.2
  614.0 14.0 %convolution_convert_fusion = bf16[2048,2048]{1,0:T(8,128)(2,1)} fusion(bf16[1024,2048]{1,0:T(8,128)(2,1)} %all-gather.9.cloned.1.call-done, bf16[1024,1024]{1,0:T(8,128)(2,1)} %get-tuple-element.29, bf16[1024,1024]{1,0:T(8,128)(2,1)} %copy-done.14), kind=kOutput, calls=%fused_computation.3 | convolution fusion | flops 8602517504 | bytes 16777216 | tf_op jit(solution)/shard_map/dot_general | solution.py:287
  627.9 73.6 %all-to-all-done.2 = bf16[4,256,2048]{2,1,0:T(8,128)(2,1)} async-done(((bf16[4,256,2048]{2,1,0:T(8,128)(2,1)}), bf16[4,256,2048]{2,1,0:T(8,128)(2,1)}, u32[]{:S(2)}, u32[]{:S(2)}) %all-to-all-start.2) | async-done | bytes 4194336 | tf_op jit(solution)/shard_map/all_to_all | solution.py:303
  701.5 10.0 %all-to-all-start.3 = ((bf16[8,256,2048]{2,1,0:T(8,128)(2,1)}), bf16[8,256,2048]{2,1,0:T(8,128)(2,1)}, u32[]{:S(2)}, u32[]{:S(2)}) async-start(bf16[8,256,2048]{2,1,0:T(8,128)(2,1)} %bitcast.98), calls=%async_computation.3 | async-start | bytes 16777216 | tf_op jit(solution)/shard_map/all_to_all | solution.py:303
  711.5 8.2 convolution_convert_fusion.2
  719.7 82.4 %all-to-all-done.3 = bf16[8,256,2048]{2,1,0:T(8,128)(2,1)} async-done(((bf16[8,256,2048]{2,1,0:T(8,128)(2,1)}), bf16[8,256,2048]{2,1,0:T(8,128)(2,1)}, u32[]{:S(2)}, u32[]{:S(2)}) %all-to-all-start.3) | async-done | bytes 8388640 | tf_op jit(solution)/shard_map/all_to_all | solution.py:303
  802.1 7.1 all-to-all-start.1
  814.8 32.8 %reduce-scatter.4.cloned.1.call-done = f32[128,7]{0,1:T(8,128)} async-done(((f32[1024,7]{0,1:T(8,128)}), f32[128,7]{0,1:T(8,128)}) %reduce-scatter.4.cloned.1.call-update) | async-done | bytes 3600 | tf_op jit(solution)/shard_map/reduce_scatter | solution.py:297
  860.5 36.3 %all-to-all-done.1 = bf16[4,256,2048]{2,1,0:T(8,128)(2,1)} async-done(((bf16[4,256,2048]{2,1,0:T(8,128)(2,1)}), bf16[4,256,2048]{2,1,0:T(8,128)(2,1)}, u32[]{:S(2)}, u32[]{:S(2)}) %all-to-all-start.1) | async-done | bytes 4194336 | tf_op jit(solution)/shard_map/all_to_all | solution.py:303
  896.9 9.4 all-to-all-start.4
  910.1 41.5 %all-reduce.8 = f32[2048]{0:T(1024)S(1)} all-reduce(f32[2048]{0:T(1024)S(1)} %get-tuple-element.38), channel_id=3, replica_groups=mesh['dp'=8,'seq'=4] {'dp','seq'}, use_global_device_ids=true, to_apply=%region_7.8.clone | all-reduce | flops 2048 | bytes 16384
  (110 shorter events, 63.0 us)
Async XLA Ops:
  7.2 51.2 %copy-start.16 = (bf16[64,8192]{1,0:T(8,128)(2,1)S(1)}, bf16[64,8192]{1,0:T(8,128)(2,1)}, u32[]{:S(2)}) copy-start(bf16[64,8192]{1,0:T(8,128)(2,1)} %param.14) | copy-start | bytes 3145732
  7.2 156.5 %all-gather.15.cloned.1.call-start = ((), (), s32[]{:S(2)}) async-start(), calls=%async_computation.16 | async-start | bytes 5242880 | tf_op jit(solution)/shard_map/all_gather | solution.py:293
  7.9 155.8 %all-gather.13.cloned.1.call-start = ((), (), s32[]{:S(2)}) async-start(), calls=%async_computation.12 | async-start | bytes 4718592 | tf_op jit(solution)/shard_map/all_gather | solution.py:293
  8.7 223.9 %all-gather.9.cloned.1.call-start = ((), (), s32[]{:S(2)}) async-start(), calls=%async_computation.9 | async-start | bytes 5242880 | tf_op jit(solution)/shard_map/all_gather | solution.py:293
  58.3 231.8 %all-gather.11.cloned.1.call-start = ((), (), s32[]{:S(2)}) async-start(), calls=%async_computation.10 | async-start | bytes 9437184 | tf_op jit(solution)/shard_map/all_gather | solution.py:293
  59.2 51.5 %copy-start.22 = (bf16[128]{0:T(256)(128)(2,1)S(1)}, bf16[128]{0:T(256)(128)(2,1)}, u32[]{:S(2)}) copy-start(bf16[128]{0:T(256)(128)(2,1)} %param.16) | copy-start | bytes 772
  59.2 61.5 %copy-start.23 = (bf16[128]{0:T(256)(128)(2,1)S(1)}, bf16[128]{0:T(256)(128)(2,1)}, u32[]{:S(2)}) copy-start(bf16[128]{0:T(256)(128)(2,1)} %param.19) | copy-start | bytes 772
  59.2 69.7 %copy-start.24 = (bf16[128]{0:T(256)(128)(2,1)S(1)}, bf16[128]{0:T(256)(128)(2,1)}, u32[]{:S(2)}) copy-start(bf16[128]{0:T(256)(128)(2,1)} %param.20) | copy-start | bytes 772
  59.2 77.9 %copy-start.21 = (bf16[128,4]{0,1:T(4,128)(2,1)S(1)}, bf16[128,4]{0,1:T(4,128)(2,1)}, u32[]{:S(2)}) copy-start(bf16[128,4]{0,1:T(4,128)(2,1)} %param.15) | copy-start | bytes 3076
  59.2 86.4 %copy-start.18 = (bf16[128,128]{1,0:T(8,128)(2,1)S(1)}, bf16[128,128]{1,0:T(8,128)(2,1)}, u32[]{:S(2)}) copy-start(bf16[128,128]{1,0:T(8,128)(2,1)} %param.18) | copy-start | bytes 98308
  59.2 95.4 %copy-start.17 = (bf16[128,160]{0,1:T(8,128)(2,1)S(1)}, bf16[128,160]{0,1:T(8,128)(2,1)}, u32[]{:S(2)}) copy-start(bf16[128,160]{0,1:T(8,128)(2,1)} %param.17) | copy-start | bytes 122884
  110.6 243.0 %all-reduce.12.cloned.1.call-start = ((), (), s32[]{:S(2)}) async-start(), calls=%async_computation.11 | async-start | bytes 2097152 | tf_op jit(solution)/shard_map/psum | solution.py:363
  154.7 201.3 %copy-start.3 = (bf16[1024,128]{1,0:T(8,128)(2,1)}, bf16[1024,128]{1,0:T(8,128)(2,1)S(1)}, u32[]{:S(2)}) copy-start(bf16[1024,128]{1,0:T(8,128)(2,1)S(1)} %all_gather.39.refs_4_.refs_8_) | copy-start | bytes 786436
  163.6 192.3 %copy-start.6 = (f32[1,1024]{1,0:T(1,128)}, f32[1,1024]{1,0:T(1,128)S(1)}, u32[]{:S(2)}) copy-start(f32[1,1024]{1,0:T(1,128)S(1)} %bitcast_convert_fusion.1.refs_5_.refs_9_) | copy-start | bytes 12292
  163.6 192.3 %copy-start.7 = (f32[1,1024]{1,0:T(1,128)}, f32[1,1024]{1,0:T(1,128)S(1)}, u32[]{:S(2)}) copy-start(f32[1,1024]{1,0:T(1,128)S(1)} %bitcast_convert_fusion.refs_6_.refs_10_) | copy-start | bytes 12292
  301.9 54.1 %copy-start = (bf16[1024,1024]{1,0:T(8,128)(2,1)}, bf16[1024,1024]{1,0:T(8,128)(2,1)S(1)}, u32[]{:S(2)}) copy-start(bf16[1024,1024]{1,0:T(8,128)(2,1)S(1)} %get-tuple-element.40.refs_2_) | copy-start | bytes 6291460
  354.7 51.7 %copy-start.2 = (f32[1024,128]{1,0:T(8,128)}, f32[1024,128]{1,0:T(8,128)S(1)}, u32[]{:S(2)}) copy-start(f32[1024,128]{1,0:T(8,128)S(1)} %pad.34.refs_1_) | copy-start | bytes 1572868
  356.0 50.4 %copy-start.4 = (bf16[1024,128]{1,0:T(8,128)(2,1)}, bf16[1024,128]{1,0:T(8,128)(2,1)S(1)}, u32[]{:S(2)}) copy-start(bf16[1024,128]{1,0:T(8,128)(2,1)S(1)} %slice.138.refs_0_) | copy-start | bytes 786436
  406.4 138.6 %copy-start.9 = (bf16[1024,1024]{1,0:T(8,128)(2,1)S(1)}, bf16[1024,1024]{1,0:T(8,128)(2,1)}, u32[]{:S(2)}) copy-start(bf16[1024,1024]{1,0:T(8,128)(2,1)} %copy-done.8) | copy-start | bytes 6291460
  553.3 8.5 copy-start.15
  553.3 54.1 %all-to-all-start.5 = ((bf16[8,128,2048]{2,1,0:T(8,128)(2,1)}), bf16[8,128,2048]{2,1,0:T(8,128)(2,1)}, u32[]{:S(2)}, u32[]{:S(2)}) async-start(bf16[8,128,2048]{2,1,0:T(8,128)(2,1)} %bitcast.101), calls=%async_computation.8 | async-start | bytes 8388608 | tf_op jit(solution)/shard_map/all_to_all | solution.py:303
  567.1 5.3 copy-start.25
  607.4 94.1 %all-to-all-start.2 = ((bf16[4,256,2048]{2,1,0:T(8,128)(2,1)}), bf16[4,256,2048]{2,1,0:T(8,128)(2,1)}, u32[]{:S(2)}, u32[]{:S(2)}) async-start(bf16[4,256,2048]{2,1,0:T(8,128)(2,1)} %bitcast.102), calls=%async_computation.2 | async-start | bytes 8388608 | tf_op jit(solution)/shard_map/all_to_all | solution.py:303
  701.5 100.6 %all-to-all-start.3 = ((bf16[8,256,2048]{2,1,0:T(8,128)(2,1)}), bf16[8,256,2048]{2,1,0:T(8,128)(2,1)}, u32[]{:S(2)}, u32[]{:S(2)}) async-start(bf16[8,256,2048]{2,1,0:T(8,128)(2,1)} %bitcast.98), calls=%async_computation.3 | async-start | bytes 16777216 | tf_op jit(solution)/shard_map/all_to_all | solution.py:303
  802.1 7.1 copy-start.19
  802.1 7.1 copy-start.20
  802.1 94.8 %all-to-all-start.1 = ((bf16[4,256,2048]{2,1,0:T(8,128)(2,1)}), bf16[4,256,2048]{2,1,0:T(8,128)(2,1)}, u32[]{:S(2)}, u32[]{:S(2)}) async-start(bf16[4,256,2048]{2,1,0:T(8,128)(2,1)} %bitcast.100), calls=%async_computation.1 | async-start | bytes 8388608 | tf_op jit(solution)/shard_map/all_to_all | solution.py:303
  809.2 38.4 %reduce-scatter.4.cloned.1.call-start = ((), (), s32[]{:S(2)}) async-start(), calls=%async_computation.13 | async-start | bytes 36864 | tf_op jit(solution)/shard_map/reduce_scatter | solution.py:297
  809.9 152.5 %reduce-scatter.8.cloned.1.call-start = ((), (), s32[]{:S(2)}) async-start(), calls=%async_computation.15 | async-start | bytes 589824 | tf_op jit(solution)/shard_map/reduce_scatter | solution.py:297
  813.2 149.2 %reduce-scatter.6.cloned.1.call-start = ((), (), s32[]{:S(2)}) async-start(), calls=%async_computation.14 | async-start | bytes 737280 | tf_op jit(solution)/shard_map/reduce_scatter | solution.py:297
  896.9 12.6 %copy-start.12 = (bf16[1,256,2048]{2,1,0:T(8,128)(2,1)S(1)}, bf16[1,256,2048]{2,1,0:T(8,128)(2,1)}, u32[]{:S(2)}) copy-start(bf16[1,256,2048]{2,1,0:T(8,128)(2,1)} %param.11) | copy-start | bytes 3145732
  896.9 60.8 %all-to-all-start.4 = ((bf16[4,64,2048]{2,1,0:T(8,128)(2,1)}), bf16[4,64,2048]{2,1,0:T(8,128)(2,1)}, u32[]{:S(2)}, u32[]{:S(2)}) async-start(bf16[4,64,2048]{2,1,0:T(8,128)(2,1)} %bitcast.21), calls=%async_computation.4 | async-start | bytes 2097152 | tf_op jit(solution)/shard_map/all_to_all | solution.py:390
  (7 other events, 20.6 us)
Sparse Core Ops, SparseCore 0:
  9.6 102.5 all-gather.14
  114.1 38.3 all-gather.12
  154.7 77.8 all-gather.8
  234.3 55.8 all-gather.10
  303.8 49.7 all-reduce.11
  813.6 33.9 reduce-scatter.3
  851.2 34.1 reduce-scatter.7
  889.4 34.3 reduce-scatter.5

commit v2 on v1

--- a/solution.py
+++ b/solution.py
@@ -283,6 +283,280 @@
     )(low, kq, values, gate, mixed, dgated, history, final, weight, bias, skip)
 
 
+MESH = pl.DeviceIdType.MESH
+GAIN_ROWS = 16
+
+
+def plane_mates(d):
+    core, x, y = lax.rem(d, 2), lax.rem(d // 2, 2), d // 4
+    return d + 1 - 2 * core, d + 2 - 4 * x, d + 4 - 8 * y
+
+
+def start_body(
+    parts, block,
+    tokens_ref, spread_ref, extra_ref, gain_ref,
+    normed_out, weight_out, conv_ref, gate_ref, extra_out,
+    tokens_all, normed_all, weight_all, extra_all,
+    near_send, near_recv, plane_send, plane_recv, gain_send, gain_recv, line_send, line_recv, local_sem,
+):
+    d, s = lax.axis_index("dp"), lax.axis_index("seq")
+    sib, xm, ym = plane_mates(d)
+    own = spread_ref.shape[1]
+    rows, width = tokens_ref.shape
+    small = extra_ref.shape[0]
+    channels = conv_ref.shape[1]
+    chunk = rows // 4
+
+    barrier = pltpu.get_barrier_semaphore()
+    for mate in (sib, xm, ym):
+        pl.semaphore_signal(barrier, inc=1, device_id=(mate, s), device_id_type=MESH)
+    for k in range(1, parts):
+        pl.semaphore_signal(barrier, inc=1, device_id=(d, lax.rem(s + k, parts)), device_id_type=MESH)
+    pl.semaphore_wait(barrier, 3 + parts - 1)
+
+    def remote(src, dst, send, recv, to):
+        return pltpu.make_async_remote_copy(
+            src_ref=src, dst_ref=dst, send_sem=send, recv_sem=recv, device_id=to, device_id_type=MESH
+        )
+
+    def weight_rows(owner, source):
+        return weight_all.at[pl.ds(pl.multiple_of((owner * parts + source) * own, own), own), :]
+
+    def extra_rows(owner):
+        return extra_all.at[owner]
+
+    def gain_rows(source):
+        return extra_all.at[d, pl.ds(pl.multiple_of(small + source * GAIN_ROWS, GAIN_ROWS), GAIN_ROWS), pl.ds(0, LANE)]
+
+    near = []
+    for k in range(1, parts):
+        to = (d, lax.rem(s + k, parts))
+        near.append(remote(spread_ref.at[to[1]], weight_rows(d, s), near_send.at[k], near_recv.at[k], to))
+        near.append(remote(gain_ref, gain_rows(s), gain_send.at[k], gain_recv.at[k], to))
+    for copy in near:
+        copy.start()
+    mine = [
+        pltpu.make_async_copy(spread_ref.at[s], weight_rows(d, s), local_sem.at[0]),
+        pltpu.make_async_copy(gain_ref, gain_rows(s), local_sem.at[1]),
+        pltpu.make_async_copy(extra_ref, extra_all.at[d, pl.ds(0, small), :], local_sem.at[2]),
+        pltpu.make_async_copy(tokens_ref, tokens_all.at[pl.ds(pl.multiple_of(s * rows, rows), rows), :], local_sem.at[3]),
+    ]
+    for copy in mine:
+        copy.start()
+
+    def token_rows(part, c):
+        return tokens_all.at[pl.ds(pl.multiple_of(part * rows + c * chunk, chunk), chunk), :]
+
+    def token_copy(way, distance, c):
+        part = s - way * (distance - 1)
+        src = tokens_ref.at[pl.ds(c * chunk, chunk), :] if distance == 1 else token_rows(part, c)
+        side = 0 if way == 1 else 1
+        return remote(
+            src, token_rows(part, c), line_send.at[side, distance, c], line_recv.at[side, distance, c], (d, s + way)
+        )
+
+    def can_send(way, distance):
+        reach = s + 1 < parts if way == 1 else s >= 1
+        came = s - (distance - 1) >= 0 if way == 1 else s + (distance - 1) < parts
+        return jnp.logical_and(reach, came)
+
+    def arrives(way, distance):
+        return s >= distance if way == 1 else s + distance < parts
+
+    def send_tokens(distance, c):
+        for way in (1, -1):
+            @pl.when(can_send(way, distance))
+            def _():
+                token_copy(way, distance, c).start()
+
+    def sent_tokens(distance, c):
+        for way in (1, -1):
+            @pl.when(can_send(way, distance))
+            def _():
+                token_copy(way, distance, c).wait_send()
+
+    def take_tokens(distance, c):
+        for way in (1, -1):
+            @pl.when(arrives(way, distance))
+            def _():
+                part = s - way * distance
+                side = 0 if way == 1 else 1
+                remote(
+                    token_rows(part, c), token_rows(part, c), line_send.at[side, distance, c],
+                    line_recv.at[side, distance, c], (d, s),
+                ).wait_recv()
+
+    units = parts + 1
+
+    def unit(owner, k):
+        return extra_rows(owner) if k == parts else weight_rows(owner, lax.rem(s - k + parts, parts))
+
+    kinds = {"own": (d, 0), "x": (xm, 2), "y": (ym, 4)}
+
+    def plane_copy(owner, k, rel, kind, to):
+        return remote(unit(owner, k), unit(owner, k), plane_send.at[kind, k], plane_recv.at[rel, k], (to, s))
+
+    diag = xm + ym - d
+    sib_of = lambda mate: mate + sib - d
+
+    def route(k):
+        steps = [
+            (0, d, 1, 0, sib), (0, d, 2, 1, xm), (0, d, 4, 2, ym),
+            (2, xm, 3, 3, sib), (4, ym, 5, 5, sib), (6, diag, 7, 7, sib),
+        ]
+        steps.append((2, xm, 6, 4, ym) if k % 2 == 0 else (4, ym, 6, 6, xm))
+        return steps
+
+    def pass_on(stage, k):
+        for at, owner, rel, kind, to in route(k):
+            if at == stage:
+                plane_copy(owner, k, rel, kind, to).start()
+
+    owners = {1: sib, 2: xm, 3: sib_of(xm), 4: ym, 5: sib_of(ym), 6: diag, 7: sib_of(diag)}
+
+    def take(rel, k):
+        plane_copy(owners[rel], k, rel, 0, d).wait_recv()
+
+    for c in range(4):
+        send_tokens(1, c)
+    mine[0].wait()
+    pass_on(0, 0)
+    for k in range(1, parts):
+        near_wait = remote(
+            spread_ref.at[s], weight_rows(d, lax.rem(s - k + parts, parts)), near_send.at[k], near_recv.at[k], (d, s)
+        )
+        near_wait.wait_recv()
+        pass_on(0, k)
+    mine[1].wait()
+    mine[2].wait()
+    for k in range(1, parts):
+        remote(gain_ref, gain_rows(lax.rem(s - k + parts, parts)), gain_send.at[k], gain_recv.at[k], (d, s)).wait_recv()
+    pass_on(0, parts)
+    for k in range(units):
+        take(2, k)
+        pass_on(2, k)
+        take(4, k)
+        pass_on(4, k)
+        if k < 4:
+            take_tokens(1, k)
+            send_tokens(2, k)
+    for k in range(units):
+        take(6, k)
+        pass_on(6, k)
+        if k < 4:
+            take_tokens(2, k)
+            send_tokens(3, k)
+    for rel in (1, 3, 5, 7):
+        for k in range(units):
+            take(rel, k)
+    mine[3].wait()
+    weight_copy = pltpu.make_async_copy(weight_all, weight_out, local_sem.at[4])
+    weight_copy.start()
+    extra_out[...] = extra_all[...]
+
+    lane = lax.broadcasted_iota(jnp.int32, (1, LANE), 1)
+    pieces = []
+    for owner in range(extra_all.shape[0]):
+        for source in range(0, parts, 2):
+            row = small + source * GAIN_ROWS
+            even = extra_all[owner, row : row + GAIN_ROWS, 0:LANE].astype(jnp.float32)[0:1]
+            odd = extra_all[owner, row + GAIN_ROWS : row + 2 * GAIN_ROWS, 0:LANE].astype(jnp.float32)[0:1]
+            pieces.append(jnp.where(lane < own, even, odd))
+    gain = jnp.concatenate(pieces, axis=1)
+
+    tile = min(512, channels)
+
+    def work(part):
+        for c in range(4):
+            at = pl.ds(pl.multiple_of(part * rows + c * chunk, chunk), chunk)
+            flat = tokens_all[at, :].astype(jnp.float32)
+            scale = lax.rsqrt(jnp.mean(flat * flat, axis=-1, keepdims=True) + 1e-05)
+            normed_all[at, :] = (flat * scale * gain).astype(jnp.bfloat16)
+        at = pl.ds(pl.multiple_of(part * rows, rows), rows)
+
+        def columns(n, carry):
+            left = pl.multiple_of(n * tile, tile)
+            right = pl.multiple_of(channels + n * tile, tile)
+            conv_ref[at, pl.ds(left, tile)] = jnp.dot(
+                normed_all[at, :], weight_all[:, pl.ds(left, tile)], preferred_element_type=jnp.float32
+            ).astype(jnp.bfloat16)
+            gate_ref[at, pl.ds(left, tile)] = jnp.dot(
+                normed_all[at, :], weight_all[:, pl.ds(right, tile)], preferred_element_type=jnp.float32
+            )
+            return carry
+
+        lax.fori_loop(0, channels // tile, columns, 0)
+
+    def work_at(low, high):
+        def each(part, carry):
+            away = jnp.abs(part - s)
+
+            @pl.when(jnp.logical_and(away >= low, away <= high))
+            def _():
+                work(part)
+
+            return carry
+
+        lax.fori_loop(0, parts, each, 0)
+
+    work_at(0, 2)
+    for c in range(4):
+        take_tokens(3, c)
+    work_at(3, 3)
+    normed_copy = pltpu.make_async_copy(normed_all, normed_out, local_sem.at[5])
+    normed_copy.start()
+
+    for copy in near:
+        copy.wait_send()
+    for k in range(units):
+        for at, owner, rel, kind, to in route(k):
+            plane_copy(owner, k, rel, kind, to).wait_send()
+    for distance in range(1, parts):
+        for c in range(4):
+            sent_tokens(distance, c)
+    weight_copy.wait()
+    normed_copy.wait()
+
+
+def start(tokens, spread, extra, gain, dps):
+    parts, own, both = spread.shape
+    rows, width = tokens.shape
+    small, lanes = extra.shape
+    any_space = pl.BlockSpec(memory_space=pl.ANY)
+    vmem = pl.BlockSpec(memory_space=pltpu.VMEM)
+    tall = small + parts * GAIN_ROWS
+    dma = pltpu.SemaphoreType.DMA
+    return pl.pallas_call(
+        lambda *refs: start_body(parts, own, *refs),
+        out_shape=[
+            jax.ShapeDtypeStruct((parts * rows, width), jnp.bfloat16),
+            jax.ShapeDtypeStruct((dps * parts * own, both), jnp.bfloat16),
+            jax.ShapeDtypeStruct((parts * rows, both // 2), jnp.bfloat16),
+            jax.ShapeDtypeStruct((parts * rows, both // 2), jnp.float32),
+            jax.ShapeDtypeStruct((dps, tall, lanes), jnp.bfloat16),
+        ],
+        in_specs=[vmem, vmem, vmem, vmem],
+        out_specs=[any_space, any_space, vmem, vmem, vmem],
+        scratch_shapes=[
+            pltpu.VMEM((parts * rows, width), jnp.bfloat16),
+            pltpu.VMEM((parts * rows, width), jnp.bfloat16),
+            pltpu.VMEM((dps * parts * own, both), jnp.bfloat16),
+            pltpu.VMEM((dps, tall, lanes), jnp.bfloat16),
+            dma((parts,)), dma((parts,)),
+            dma((8, parts + 1)), dma((8, parts + 1)),
+            dma((parts,)), dma((parts,)),
+            dma((2, parts, 4)), dma((2, parts, 4)),
+            dma((6,)),
+        ],
+        compiler_params=pltpu.CompilerParams(
+            collective_id=1, has_side_effects=True, vmem_limit_bytes=56 * 1024 * 1024
+        ),
+        cost_estimate=pl.CostEstimate(
+            flops=2 * parts * rows * width * both, bytes_accessed=40 * 1024 * 1024, transcendentals=0
+        ),
+    )(tokens, spread, extra, gain)
+
+
 def contract(left, right, left_dim, right_dim):
     return lax.dot_general(
         left, right, (((left_dim,), (right_dim,)), ((), ())), preferred_element_type=jnp.float32
@@ -338,23 +612,43 @@
     states = (select_weight.shape[1] - rank) // 2
     own = in_weight.shape[0]
 
-    gain = gathered(norm_gain, ("dp", "seq")).astype(jnp.float32)
     flat = tokens.reshape(rows, width).astype(jnp.float32)
     scale = lax.rsqrt(jnp.mean(flat * flat, axis=-1, keepdims=True) + 1e-05)
-    normed = gathered((flat * scale * gain).astype(jnp.bfloat16), "seq")
     spread = in_weight.reshape(own, 2, dps, parts, block).transpose(3, 0, 1, 2, 4).reshape(parts, own, 2 * channels)
-    in_w = gathered(lax.all_to_all(spread, "seq", 0, 0).reshape(parts * own, 2 * channels), "dp")
-    conv_w = gathered(conv_weight, "dp").astype(jnp.float32)
-    conv_b = gathered(conv_bias, "dp").astype(jnp.float32)
-    select_w = gathered(select_weight, "dp")
-    beta_w = gathered(beta_weight, "dp")
-    beta_b = gathered(beta_bias, "dp").astype(jnp.float32).reshape(1, channels)
-    skip = gathered(skip_gain, "dp").astype(jnp.float32).reshape(1, channels)
-    out_w = gathered(out_weight, "dp")
-    cot = gathered(cotangent.reshape(rows, width), "seq")
-
-    conv_in = jnp.dot(normed, in_w[:, :channels], preferred_element_type=jnp.float32).astype(jnp.bfloat16)
-    gate = jnp.dot(normed, in_w[:, channels:], preferred_element_type=jnp.float32)
+    vectors = jnp.concatenate(
+        [conv_weight, conv_bias[:, None], beta_bias[:, None], skip_gain[:, None]], axis=1
+    )
+    wide = -(-select_weight.shape[1] // LANE) * LANE
+    small = jnp.concatenate(
+        [
+            jnp.pad(select_weight, ((0, 0), (0, wide - select_weight.shape[1]))),
+            beta_weight,
+            jnp.pad(vectors, ((0, 0), (0, LANE - vectors.shape[1]))),
+        ],
+        axis=1,
+    )
+    if (dps, parts, 2 * own) == (8, 4, LANE):
+        doubled = jnp.broadcast_to(jnp.tile(norm_gain.reshape(1, own), (1, 2)), (GAIN_ROWS, LANE))
+        normed, in_w, conv_in, gate, extra = start(tokens.reshape(rows, width), spread, small, doubled, dps)
+        smalls = extra[:, :block].reshape(channels, small.shape[1])
+        gain = extra[:, block:, :own].reshape(dps * parts, GAIN_ROWS, own)[:, 0].reshape(width)
+    else:
+        gain = gathered(norm_gain, ("dp", "seq"))
+        normed = gathered((flat * scale * gain.astype(jnp.float32)).astype(jnp.bfloat16), "seq")
+        in_w = gathered(lax.all_to_all(spread, "seq", 0, 0).reshape(parts * own, 2 * channels), "dp")
+        smalls = gathered(small, "dp")
+        conv_in = jnp.dot(normed, in_w[:, :channels], preferred_element_type=jnp.float32).astype(jnp.bfloat16)
+        gate = jnp.dot(normed, in_w[:, channels:], preferred_element_type=jnp.float32)
+    gain = gain.astype(jnp.float32)
+    select_w = smalls[:, : select_weight.shape[1]]
+    beta_w = smalls[:, wide : wide + rank]
+    vectors = smalls[:, wide + rank :].astype(jnp.float32)
+    conv_w, conv_b = vectors[:, :taps], vectors[:, taps]
+    beta_b, skip = vectors[:, taps + 1].reshape(1, channels), vectors[:, taps + 2].reshape(1, channels)
+    out_shard, cot_shard, conv_in = lax.optimization_barrier((out_weight, cotangent.reshape(rows, width), conv_in))
+    out_w = gathered(out_shard, "dp")
+    cot = gathered(cot_shard, "seq")
+
     conv_wide = conv_in.astype(jnp.float32)
     conv_sum = conv_b
     for tap in range(taps):

time: 980 us -> 873 us (0.89)
  blocking collectives: 229 us -> 81.2 us
  Pallas kernels: 147 us -> 244 us
  waiting for transfers between devices: 405 us -> 356 us
  matrix products: 82.5 us -> 66.4 us
    pallas_call x0 -> x1, Pallas kernels: none -> 97.1 us  [start(): pl.pallas_call(lambda *refs: start_body(parts, own, *refs), out_shape=[ja...]
    all_gather x6 -> x0, blocking collectives: 53 us -> none  [gathered(): return lax.all_gather(shard, axis, axis=0, tiled=True)]
    all_to_all x1 -> x0, blocking collectives: 50.7 us -> none  [local(): lax.all_to_all(spread, 'seq', 0, 0).reshape(parts * own, 2 * channels)]
    unnamed x2 -> x1, blocking collectives: 86.1 us -> 41.5 us
    all_gather x4 -> x2, waiting for transfers between devices: 116 us -> 80.1 us  [gathered(): return lax.all_gather(shard, axis, axis=0, tiled=True)]
    all_to_all x4, waiting for transfers between devices: 215 us -> 194 us  [summed_rows(): parts = lax.all_to_all(parts, axis, 0, 0)]
    dot_general x2 -> x0, matrix products: 17.6 us -> none  [the longest x1 9.9 us: local(): jnp.dot(normed, in_w[:, channels:], preferred_element_type=jnp.float32)]
    psum x1, waiting for transfers between devices: 40 us -> 50.7 us  [local(): lax.psum(jnp.dot(values, select_w, preferred_element_type=jnp.float32), '...]
  transfers between devices with their start and end apart: 13 -> 11, of which waited for: 8 -> 7; matrix products, arithmetic and copies ran while one was open for 11% -> 12% of each run, Pallas kernels for 0% -> 17%
where the time goes in v2:
time: 873 us; the launch traced here: 862 us
  waiting for transfers between devices  356 us (41%)
  Pallas kernels  244 us (28%)
  blocking collectives  81.2 us (9%)
  matrix products  66.4 us (8%)
  starting transfers between devices  45.5 us (5%)
  other arithmetic  31.3 us (4%)
  local copies, waits for them, and re-layouts  23.1 us (3%)
  between operations  14.7 us (2%)
    all_to_all x4, waiting for transfers between devices, summed_rows(): parts = lax.all_to_all(parts, axis, 0, 0)  194 us
    pallas_call x1, Pallas kernels, backward_scan(): pl.pallas_call(lambda *refs: backward_body(states, *refs), grid=(blocks,)...  98 us
    pallas_call x1, Pallas kernels, start(): pl.pallas_call(lambda *refs: start_body(parts, own, *refs), out_shape=[ja...  97.1 us
    all_gather x2, waiting for transfers between devices, gathered(): return lax.all_gather(shard, axis, axis=0, tiled=True)  80.1 us
    dot_general x7, matrix products, contract(): lax.dot_general(left, right, (((left_dim,), (right_dim,)), ((), ())), pre...  56.5 us
    psum x1, waiting for transfers between devices, local(): lax.psum(jnp.dot(values, select_w, preferred_element_type=jnp.float32), '...  50.7 us
    pallas_call x1, Pallas kernels, forward_scan(): pl.pallas_call(lambda *refs: forward_body(states, *refs), grid=(blocks,),...  48.5 us
    unnamed x1, blocking collectives  41.5 us
  transfers between devices with their start and end apart: 11, of which 7 were waited for; matrix products, arithmetic and copies ran while one was open for 12% of the time, Pallas kernels for 17%

profile of v2, /device:TPU:25, one launch (start us, length us, event | category | flops | bytes accessed | tf_op | source)
XLA Modules:
  0.0 862.1 jit_solution(12386229517571439633)
XLA Ops:
  14.2 97.1 %shard_map.194 = (bf16[1024,2048]{1,0:T(8,128)(2,1)}, bf16[2048,2048]{1,0:T(8,128)(2,1)}, bf16[1024,1024]{1,0:T(8,128)(2,1)}, f32[1024,1024]{1,0:T(8,128)}, bf16[8,192,512]{2,1,0:T(8,128)(2,1)}) custom-call(bf16[256,2048]{1,0:T(8,128)(2,1)} %bitcast.68, bf16[4,64,2048]{2,1,0:T(8,128)(2,1)} %reshape.174.refs_1_, bf16[128,512]{1,0:T(8,128)(2,1)} %fusion.27.refs_2_, ...), custom_call_target="tpu_custom_call" | custom-call | flops 8589934592 | bytes 41943040 | tf_op jit(solution)/shard_map/pallas_call | solution.py:529
  115.3 4.1 fusion.8
  122.6 50.7 %all-reduce.13.cloned.1.call-done = f32[1024,160]{1,0:T(8,128)} async-done(((f32[1024,160]{1,0:T(8,128)}), f32[1024,160]{1,0:T(8,128)}) %all-reduce.13.cloned.1.call-update) | async-done | bytes 655376 | tf_op jit(solution)/shard_map/psum | solution.py:657
  175.7 48.5 %shard_map.195 = (bf16[1024,1024]{1,0:T(8,128)(2,1)S(1)}, f32[1024,1024]{1,0:T(8,128)}, bf16[16384,1024]{1,0:T(8,128)(2,1)}, f32[16,1024]{1,0:T(8,128)S(1)}) custom-call(bf16[1024,128]{1,0:T(8,128)(2,1)S(1)} %slice.185.refs_0_, f32[1024,128]{1,0:T(8,128)S(1)} %pad.44.refs_1_, bf16[1024,1024]{1,0:T(8,128)(2,1)S(1)} %get-tuple-element.63.refs_2_, ...), custom_call_target="tpu_custom_call" | custom-call | flops 234881024 | bytes 33554432 | tf_op jit(solution)/shard_map/pallas_call | solution.py:114
  226.2 28.1 %all-gather.5.cloned.1.call-done = bf16[1024,2048]{1,0:T(8,128)(2,1)} async-done(((bf16[256,2048]{1,0:T(8,128)(2,1)}), bf16[1024,2048]{1,0:T(8,128)(2,1)}) %all-gather.5.cloned.1.call-update) | async-done | bytes 4194320 | tf_op jit(solution)/shard_map/all_gather | solution.py:567
  254.2 9.4 %convolution_convert_fusion.2 = bf16[1024,2048]{1,0:T(8,128)(2,1)} fusion(bf16[1024,1024]{1,0:T(8,128)(2,1)} %copy-done.8, bf16[1024,2048]{1,0:T(8,128)(2,1)} %all-gather.5.cloned.1.call-done), kind=kOutput, calls=%fused_computation.26 | convolution fusion | flops 4297064448 | bytes 10485760 | tf_op jit(solution)/shard_map/dot_general | solution.py:561
  263.6 4.9 all-to-all-start.4
  268.5 52.1 %all-gather.3.cloned.1.call-done = bf16[1024,2048]{1,0:T(8,128)(2,1)} async-done(((bf16[128,2048]{1,0:T(8,128)(2,1)}), bf16[1024,2048]{1,0:T(8,128)(2,1)}) %all-gather.3.cloned.1.call-update) | async-done | bytes 4194320 | tf_op jit(solution)/shard_map/all_gather | solution.py:567
  320.6 10.0 %fusion.35.refs_5_ = f32[1024,1024]{1,0:T(8,128)} fusion(bf16[1024,2048]{1,0:T(8,128)(2,1)} %all-gather.5.cloned.1.call-done, bf16[1024,2048]{1,0:T(8,128)(2,1)} %all-gather.3.cloned.1.call-done), kind=kOutput, calls=%fused_computation.83 | convolution fusion | flops 4294967296 | bytes 12582912 | tf_op jit(solution)/shard_map/dot_general | solution.py:561
  330.5 98.0 %shard_map.196 = (bf16[1024,1024]{1,0:T(8,128)(2,1)}, bf16[1024,1024]{1,0:T(8,128)(2,1)}, f32[1024,1024]{1,0:T(8,128)}, f32[1024,128]{1,0:T(8,128)}, f32[1024,12...) custom-call(bf16[1024,128]{1,0:T(8,128)(2,1)} %copy-done.4, f32[1024,128]{1,0:T(8,128)} %copy-done.2, ...), custom_call_target="tpu_custom_call" | custom-call | flops 503316480 | bytes 33554432 | tf_op jit(solution)/shard_map/pallas_call | solution.py:257
  429.9 39.7 %all-reduce.14 = bf16[1024,160]{1,0:T(8,128)(2,1)S(1)} all-reduce(f32[1024,160]{1,0:T(8,128)S(1)} %pad_maximum_fusion.3), channel_id=1, replica_groups=mesh['dp'=8,'seq'=4] {'seq'}, use_global_device_ids=true, to_apply=%region_3.4 | all-reduce | flops 163840 | bytes 983040 | tf_op jit(solution)/shard_map/psum | solution.py:669
  469.6 5.4 add_multiply_fusion
  475.1 4.1 multiply_reduce_fusion.1
  479.2 12.6 %convolution_convert_fusion.1 = bf16[1024,2048]{1,0:T(8,128)(2,1)} fusion(bf16[2048,2048]{1,0:T(8,128)(2,1)} %get-tuple-element.44, bf16[1024,1024]{1,0:T(8,128)(2,1)S(1)} %copy-done.22, bf16[1024,1024]{1,0:T(8,128)(2,1)S(1)} %get-tuple-element.65), kind=kOutput, calls=%fused_computation.25 | convolution fusion | flops 8600420352 | bytes 16777216 | tf_op jit(solution)/shard_map/dot_general | solution.py:561
  491.8 7.1 all-to-all-start.1
  498.9 13.5 %convolution_convert_fusion = bf16[2048,2048]{1,0:T(8,128)(2,1)} fusion(bf16[1024,2048]{1,0:T(8,128)(2,1)} %get-tuple-element.45, bf16[1024,1024]{1,0:T(8,128)(2,1)} %get-tuple-element.43, bf16[1024,1024]{1,0:T(8,128)(2,1)S(1)} %get-tuple-element.65), kind=kOutput, calls=%fused_computation.3 | convolution fusion | flops 8602517504 | bytes 16777216 | tf_op jit(solution)/shard_map/dot_general | solution.py:561
  512.4 75.1 %all-to-all-done.1 = bf16[4,256,2048]{2,1,0:T(8,128)(2,1)} async-done(((bf16[4,256,2048]{2,1,0:T(8,128)(2,1)}), bf16[4,256,2048]{2,1,0:T(8,128)(2,1)}, u32[]{:S(2)}, u32[]{:S(2)}) %all-to-all-start.1) | async-done | bytes 4194336 | tf_op jit(solution)/shard_map/all_to_all | solution.py:577
  587.5 16.7 %all-to-all-start.2 = ((bf16[8,256,2048]{2,1,0:T(8,128)(2,1)}), bf16[8,256,2048]{2,1,0:T(8,128)(2,1)}, u32[]{:S(2)}, u32[]{:S(2)}) async-start(bf16[8,256,2048]{2,1,0:T(8,128)(2,1)} %bitcast.69), calls=%async_computation.2 | async-start | bytes 16777216 | tf_op jit(solution)/shard_map/all_to_all | solution.py:577
  604.3 8.2 convolution_convert_fusion.3
  612.4 82.4 %all-to-all-done.2 = bf16[8,256,2048]{2,1,0:T(8,128)(2,1)} async-done(((bf16[8,256,2048]{2,1,0:T(8,128)(2,1)}), bf16[8,256,2048]{2,1,0:T(8,128)(2,1)}, u32[]{:S(2)}, u32[]{:S(2)}) %all-to-all-start.2) | async-done | bytes 8388640 | tf_op jit(solution)/shard_map/all_to_all | solution.py:577
  694.9 7.1 all-to-all-start
  703.8 3.2 fusion.33
  707.5 2.4 fusion.36
  710.0 30.6 %reduce-scatter.4.cloned.1.call-done = f32[128,7]{0,1:T(8,128)} async-done(((f32[1024,7]{0,1:T(8,128)}), f32[128,7]{0,1:T(8,128)}) %reduce-scatter.4.cloned.1.call-update) | async-done | bytes 3600 | tf_op jit(solution)/shard_map/reduce_scatter | solution.py:571
  743.1 4.0 convert_reduce_fusion
  747.1 6.4 reduce_sum.122
  753.5 36.1 %all-to-all-done = bf16[4,256,2048]{2,1,0:T(8,128)(2,1)} async-done(((bf16[4,256,2048]{2,1,0:T(8,128)(2,1)}), bf16[4,256,2048]{2,1,0:T(8,128)(2,1)}, u32[]{:S(2)}, u32[]{:S(2)}) %all-to-all-start) | async-done | bytes 4194336 | tf_op jit(solution)/shard_map/all_to_all | solution.py:577
  789.6 9.3 %all-to-all-start.3 = ((bf16[4,64,2048]{2,1,0:T(8,128)(2,1)}), bf16[4,64,2048]{2,1,0:T(8,128)(2,1)}, u32[]{:S(2)}, u32[]{:S(2)}) async-start(bf16[4,64,2048]{2,1,0:T(8,128)(2,1)} %bitcast.13), calls=%async_computation.3 | async-start | bytes 2097152 | tf_op jit(solution)/shard_map/all_to_all | solution.py:684
  798.9 3.2 convert_reduce_fusion.1
  802.7 41.5 %all-reduce.9 = f32[2048]{0:T(1024)S(1)} all-reduce(f32[2048]{0:T(1024)S(1)} %get-tuple-element.54), channel_id=2, replica_groups=mesh['dp'=8,'seq'=4] {'dp','seq'}, use_global_device_ids=true, to_apply=%region_7.8.clone | all-reduce | flops 2048 | bytes 16384
  844.8 3.3 convert_reduce_fusion.2
  848.1 2.2 fusion.13
  (95 shorter events, 30.6 us)
Async XLA Ops:
  7.2 5.8 copy-start.19
  7.2 166.1 %all-reduce.13.cloned.1.call-start = ((), (), s32[]{:S(2)}) async-start(), calls=%async_computation.8 | async-start | bytes 2097152 | tf_op jit(solution)/shard_map/psum | solution.py:657
  111.4 3.5 copy-start.13
  112.8 6.5 copy-start.16
  112.9 62.7 %copy-start.3 = (bf16[1024,128]{1,0:T(8,128)(2,1)}, bf16[1024,128]{1,0:T(8,128)(2,1)S(1)}, u32[]{:S(2)}) copy-start(bf16[1024,128]{1,0:T(8,128)(2,1)S(1)} %get-tuple-element.68.refs_4_.refs_8_) | copy-start | bytes 786436
  114.8 60.9 %copy-start.6 = (f32[1024]{0:T(1024)}, f32[1024]{0:T(1024)S(1)}, u32[]{:S(2)}) copy-start(f32[1024]{0:T(1024)S(1)} %get-tuple-element.56) | copy-start | bytes 12292
  114.8 60.9 %copy-start.7 = (f32[1024]{0:T(1024)}, f32[1024]{0:T(1024)S(1)}, u32[]{:S(2)}) copy-start(f32[1024]{0:T(1024)S(1)} %get-tuple-element.57) | copy-start | bytes 12292
  115.3 4.1 copy-start.10
  119.4 56.3 %copy-start = (bf16[1024,1024]{1,0:T(8,128)(2,1)}, bf16[1024,1024]{1,0:T(8,128)(2,1)S(1)}, u32[]{:S(2)}) copy-start(bf16[1024,1024]{1,0:T(8,128)(2,1)S(1)} %get-tuple-element.63.refs_2_) | copy-start | bytes 6291460
  121.1 133.1 %all-gather.5.cloned.1.call-start = ((), (), s32[]{:S(2)}) async-start(), calls=%async_computation.10 | async-start | bytes 5242880 | tf_op jit(solution)/shard_map/all_gather | solution.py:567
  121.8 198.8 %all-gather.3.cloned.1.call-start = ((), (), s32[]{:S(2)}) async-start(), calls=%async_computation.9 | async-start | bytes 4718592 | tf_op jit(solution)/shard_map/all_gather | solution.py:567
  174.4 89.2 %copy-start.2 = (f32[1024,128]{1,0:T(8,128)}, f32[1024,128]{1,0:T(8,128)S(1)}, u32[]{:S(2)}) copy-start(f32[1024,128]{1,0:T(8,128)S(1)} %pad.44.refs_1_) | copy-start | bytes 1572868
  175.7 87.9 %copy-start.4 = (bf16[1024,128]{1,0:T(8,128)(2,1)}, bf16[1024,128]{1,0:T(8,128)(2,1)S(1)}, u32[]{:S(2)}) copy-start(bf16[1024,128]{1,0:T(8,128)(2,1)S(1)} %slice.185.refs_0_) | copy-start | bytes 786436
  263.6 228.2 %all-to-all-start.4 = ((bf16[8,128,2048]{2,1,0:T(8,128)(2,1)}), bf16[8,128,2048]{2,1,0:T(8,128)(2,1)}, u32[]{:S(2)}, u32[]{:S(2)}) async-start(bf16[8,128,2048]{2,1,0:T(8,128)(2,1)} %bitcast.72), calls=%async_computation.7 | async-start | bytes 8388608 | tf_op jit(solution)/shard_map/all_to_all | solution.py:577
  330.5 139.0 %copy-start.17 = (bf16[8,128,512]{2,1,0:T(8,128)(2,1)S(1)}, bf16[8,128,512]{2,1,0:T(8,128)(2,1)}, u32[]{:S(2)}) copy-start(bf16[8,128,512]{2,1,0:T(8,128)(2,1)} %copy-done.16) | copy-start | bytes 3145732
  469.6 5.5 copy-start.18
  469.6 5.4 copy-start.11
  469.6 5.5 copy-start.14
  475.1 4.1 copy-start.22
  491.8 95.7 %all-to-all-start.1 = ((bf16[4,256,2048]{2,1,0:T(8,128)(2,1)}), bf16[4,256,2048]{2,1,0:T(8,128)(2,1)}, u32[]{:S(2)}, u32[]{:S(2)}) async-start(bf16[4,256,2048]{2,1,0:T(8,128)(2,1)} %bitcast.73), calls=%async_computation.1 | async-start | bytes 8388608 | tf_op jit(solution)/shard_map/all_to_all | solution.py:577
  587.5 16.7 %copy-start.9 = (bf16[1024,1024]{1,0:T(8,128)(2,1)S(1)}, bf16[1024,1024]{1,0:T(8,128)(2,1)}, u32[]{:S(2)}) copy-start(bf16[1024,1024]{1,0:T(8,128)(2,1)} %copy-done.8) | copy-start | bytes 6291460
  587.5 107.3 %all-to-all-start.2 = ((bf16[8,256,2048]{2,1,0:T(8,128)(2,1)}), bf16[8,256,2048]{2,1,0:T(8,128)(2,1)}, u32[]{:S(2)}, u32[]{:S(2)}) async-start(bf16[8,256,2048]{2,1,0:T(8,128)(2,1)} %bitcast.69), calls=%async_computation.2 | async-start | bytes 16777216 | tf_op jit(solution)/shard_map/all_to_all | solution.py:577
  694.9 8.2 copy-start.20
  694.9 8.2 copy-start.21
  694.9 94.7 %all-to-all-start = ((bf16[4,256,2048]{2,1,0:T(8,128)(2,1)}), bf16[4,256,2048]{2,1,0:T(8,128)(2,1)}, u32[]{:S(2)}, u32[]{:S(2)}) async-start(bf16[4,256,2048]{2,1,0:T(8,128)(2,1)} %bitcast.71), calls=%async_computation | async-start | bytes 8388608 | tf_op jit(solution)/shard_map/all_to_all | solution.py:577
  702.0 5.2 copy-start.12
  702.0 5.5 copy-start.1
  702.0 38.6 %reduce-scatter.4.cloned.1.call-start = ((), (), s32[]{:S(2)}) async-start(), calls=%async_computation.11 | async-start | bytes 36864 | tf_op jit(solution)/shard_map/reduce_scatter | solution.py:571
  703.8 151.3 %reduce-scatter.8.cloned.1.call-start = ((), (), s32[]{:S(2)}) async-start(), calls=%async_computation.13 | async-start | bytes 589824 | tf_op jit(solution)/shard_map/reduce_scatter | solution.py:571
  707.0 148.0 %reduce-scatter.6.cloned.1.call-start = ((), (), s32[]{:S(2)}) async-start(), calls=%async_computation.12 | async-start | bytes 737280 | tf_op jit(solution)/shard_map/reduce_scatter | solution.py:571
  789.6 60.7 %all-to-all-start.3 = ((bf16[4,64,2048]{2,1,0:T(8,128)(2,1)}), bf16[4,64,2048]{2,1,0:T(8,128)(2,1)}, u32[]{:S(2)}, u32[]{:S(2)}) async-start(bf16[4,64,2048]{2,1,0:T(8,128)(2,1)} %bitcast.13), calls=%async_computation.3 | async-start | bytes 2097152 | tf_op jit(solution)/shard_map/all_to_all | solution.py:684
  844.2 3.9 copy-start.15
  (2 other events, 2.0 us)
Sparse Core Ops, SparseCore 0:
  121.2 52.0 all-reduce.12
  174.9 79.2 all-gather.4
  256.3 64.2 all-gather.2
  706.3 34.1 reduce-scatter.3
  744.0 34.1 reduce-scatter.7
  782.0 34.3 reduce-scatter.5

commit v3 on v2

--- a/solution.py
+++ b/solution.py
@@ -142,13 +142,14 @@
 
 
 def backward_body(
-    states, low_ref, kq_ref, values_ref, gate_ref, mixed_ref, dgated_ref, history_ref, final_ref, weight_ref, bias_ref, skip_ref,
-    dgate_ref, dpre_ref, dvalues_ref, dlow_ref, dkq_ref, bias_grad_ref, skip_grad_ref,
-    grad_ref, state_ref, key_ref, query_ref, rate_ref, do_ref, values32_ref, fed_ref, kept_ref, part_key_ref, part_query_ref, row_ref, placed_ref,
+    states, links, low_ref, kq_ref, values_ref, gate_ref, mixed_ref, dgated_ref, history_ref, final_ref, weight_ref, bias_ref, skip_ref,
+    result_ref, out_ref, dgate_ref, dpre_ref, dvalues_ref, dlow_ref, dkq_ref, bias_grad_ref, skip_grad_ref, result_came, out_came,
+    grad_ref, state_ref, key_ref, query_ref, rate_ref, do_ref, values32_ref, fed_ref, kept_ref, part_key_ref, part_query_ref, row_ref, placed_ref, *sems,
 ):
     rows, channels = values_ref.shape
     tiles = channels // LANE
     per_group = min(4, tiles)
+    copies = links(result_ref, out_ref, result_came, out_came, *sems)
 
     @pl.when(pl.program_id(0) == 0)
     def _():
@@ -156,6 +157,8 @@
         state_ref[...] = final_ref[...]
         bias_grad_ref[...] = jnp.zeros_like(bias_grad_ref)
         skip_grad_ref[...] = jnp.zeros_like(skip_grad_ref)
+        for copy in copies:
+            copy.start()
 
     beta, inverse = step_sizes(low_ref, kq_ref, weight_ref, bias_ref, states)
     rate_ref[...] = by_eights(beta * inverse)
@@ -243,8 +246,47 @@
     lanes = lax.broadcasted_iota(jnp.int32, kq_ref.shape, 1)
     dkq_ref[...] = as_rows(placed_ref[...]) + jnp.where(lanes < states, kq_ref[...] * through, 0.0)
 
-
-def backward_scan(low, kq, values, gate, mixed, dgated, history, final, weight, bias, skip, states):
+    @pl.when(pl.program_id(0) == pl.num_programs(0) - 1)
+    def _():
+        for copy in copies:
+            copy.wait_recv()
+        for copy in copies:
+            copy.wait_send()
+
+
+def exchange(parts, dps, result_ref, out_ref, result_came, out_came, result_send, result_recv, out_send, out_recv):
+    d, s = lax.axis_index("dp"), lax.axis_index("seq")
+
+    @pl.when(pl.program_id(0) == 0)
+    def _():
+        barrier = pltpu.get_barrier_semaphore()
+        for k in range(1, parts):
+            pl.semaphore_signal(barrier, inc=1, device_id=(d, lax.rem(s + k, parts)), device_id_type=MESH)
+        for k in range(1, dps):
+            pl.semaphore_signal(barrier, inc=1, device_id=(lax.rem(d + k, dps), s), device_id_type=MESH)
+        pl.semaphore_wait(barrier, parts + dps - 2)
+
+    copies = []
+    for k in range(1, parts):
+        to = lax.rem(s + k, parts)
+        copies.append(
+            pltpu.make_async_remote_copy(
+                src_ref=result_ref.at[to], dst_ref=result_came.at[k - 1], send_sem=result_send.at[k - 1],
+                recv_sem=result_recv.at[k - 1], device_id=(d, to), device_id_type=MESH,
+            )
+        )
+    for k in range(1, dps):
+        to = lax.rem(d + k, dps)
+        copies.append(
+            pltpu.make_async_remote_copy(
+                src_ref=out_ref.at[to], dst_ref=out_came.at[k - 1], send_sem=out_send.at[k - 1],
+                recv_sem=out_recv.at[k - 1], device_id=(to, s), device_id_type=MESH,
+            )
+        )
+    return copies
+
+
+def backward_scan(low, kq, values, gate, mixed, dgated, history, final, weight, bias, skip, result_part, out_part, states):
     length, channels = values.shape
     rank = low.shape[1]
     rows = min(128, length)
@@ -254,15 +296,19 @@
     total = pl.BlockSpec((1, channels), lambda i: (0, 0))
     wide = pltpu.VMEM((rows // 8, 8, channels), jnp.float32)
     spread = pltpu.VMEM((rows * states, LANE), jnp.float32)
+    anywhere = pl.BlockSpec(memory_space=pl.ANY)
+    dma = pltpu.SemaphoreType.DMA
+    parts, dps = result_part.shape[0], out_part.shape[0]
+    links = lambda *refs: exchange(parts, dps, *refs)
     return pl.pallas_call(
-        lambda *refs: backward_body(states, *refs),
+        lambda *refs: backward_body(states, links, *refs),
         grid=(blocks,),
         in_specs=[
             by_row(rank), by_row(LANE), by_row(channels), by_row(channels), by_row(channels), by_row(channels),
             pl.BlockSpec((rows * states, channels), lambda i: (blocks - 1 - i, 0)),
-            whole(final), whole(weight), whole(bias), whole(skip),
-        ],
-        out_specs=[by_row(channels), by_row(channels), by_row(channels), by_row(rank), by_row(LANE), total, total],
+            whole(final), whole(weight), whole(bias), whole(skip), anywhere, anywhere,
+        ],
+        out_specs=[by_row(channels), by_row(channels), by_row(channels), by_row(rank), by_row(LANE), total, total, anywhere, anywhere],
         out_shape=[
             jax.ShapeDtypeStruct((length, channels), jnp.bfloat16),
             jax.ShapeDtypeStruct((length, channels), jnp.bfloat16),
@@ -271,16 +317,19 @@
             jax.ShapeDtypeStruct((length, LANE), jnp.float32),
             jax.ShapeDtypeStruct((1, channels), jnp.float32),
             jax.ShapeDtypeStruct((1, channels), jnp.float32),
+            jax.ShapeDtypeStruct((parts - 1,) + result_part.shape[1:], jnp.bfloat16),
+            jax.ShapeDtypeStruct((dps - 1,) + out_part.shape[1:], jnp.bfloat16),
         ],
         scratch_shapes=[
             pltpu.VMEM((states, channels), jnp.float32),
             pltpu.VMEM((states, channels), jnp.float32),
             spread, spread, wide, wide, wide, wide, wide, spread, spread,
             pltpu.VMEM((rows // 8, 8, LANE), jnp.float32), pltpu.VMEM((rows // 8, 8, LANE), jnp.float32),
-        ],
-        compiler_params=pltpu.CompilerParams(vmem_limit_bytes=56 * 1024 * 1024),
+            dma((parts - 1,)), dma((parts - 1,)), dma((dps - 1,)), dma((dps - 1,)),
+        ],
+        compiler_params=pltpu.CompilerParams(collective_id=3, has_side_effects=True, vmem_limit_bytes=56 * 1024 * 1024),
         cost_estimate=pl.CostEstimate(flops=30 * length * states * channels, bytes_accessed=2 * length * states * channels, transcendentals=0),
-    )(low, kq, values, gate, mixed, dgated, history, final, weight, bias, skip)
+    )(low, kq, values, gate, mixed, dgated, history, final, weight, bias, skip, result_part, out_part)
 
 
 MESH = pl.DeviceIdType.MESH
@@ -557,6 +606,264 @@
     )(tokens, spread, extra, gain)
 
 
+def end_body(
+    parts, block,
+    dmixed_ref, normed_ref, weight_ref, tokens_ref, cot_ref, gain_ref, shard_ref, small_ref,
+    input_grad_ref, in_grad_ref, gain_grad_ref, small_grad_ref,
+    dn, dn_recv, sib_send, sib_recv, q_send, q_recv, total, z_send, z_recv,
+    small_sib_send, small_sib_recv, small_q_send, small_q_recv,
+    line_send, line_recv, pair_send, pair_recv, cross_send, cross_recv, near_send, near_recv,
+):
+    d, s = lax.axis_index("dp"), lax.axis_index("seq")
+    sib, xm, ym = plane_mates(d)
+    diag = xm + ym - d
+    own, both = shard_ref.shape[0], dmixed_ref.shape[1]
+    rows, width = tokens_ref.shape
+    chunk = rows // 4
+    tall = parts * own
+    tile = min(512, both)
+
+    barrier = pltpu.get_barrier_semaphore()
+    for mate in (sib, xm, ym, diag):
+        pl.semaphore_signal(barrier, inc=1, device_id=(mate, s), device_id_type=MESH)
+    for k in range(1, parts):
+        pl.semaphore_signal(barrier, inc=1, device_id=(d, lax.rem(s + k, parts)), device_id_type=MESH)
+    pl.semaphore_wait(barrier, 4 + parts - 1)
+
+    def remote(src, dst, send, recv, to):
+        return pltpu.make_async_remote_copy(
+            src_ref=src, dst_ref=dst, send_sem=send, recv_sem=recv, device_id=to, device_id_type=MESH
+        )
+
+    def dn_rows(part, c):
+        return pl.ds(pl.multiple_of(part * rows + c * chunk, chunk), chunk)
+
+    def slot(way, left, part, c):
+        at = parts if way == -1 and left == 0 else part
+        return dn_recv.at[at, pl.ds(c * chunk, chunk), :]
+
+    def line_copy(way, steps, c):
+        side = 0 if way == 1 else 1
+        part = s + way * steps
+        return remote(
+            dn.at[dn_rows(part, c), :], slot(way, steps - 1, part, c), line_send.at[side, steps, c],
+            line_recv.at[side, steps - 1, c], (d, s + way),
+        )
+
+    def valid(way, steps):
+        return s + steps < parts if way == 1 else s >= steps
+
+    def upstream(way):
+        return s >= 1 if way == 1 else s + 1 < parts
+
+    def line_wait(way, left, c):
+        side = 0 if way == 1 else 1
+        place = slot(way, left, s + way * left, c)
+        remote(place, place, line_send.at[side, left, c], line_recv.at[side, left, c], (d, s)).wait_recv()
+
+    def pass_line(steps, c):
+        for way in (1, -1):
+            @pl.when(valid(way, steps))
+            def _():
+                if steps < parts - 1:
+                    @pl.when(upstream(way))
+                    def _():
+                        line_wait(way, steps, c)
+                        mine = dn_rows(s + way * steps, c)
+                        came = dn_recv[s + way * steps, c * chunk : (c + 1) * chunk, :]
+                        dn[mine, :] = (dn[mine, :].astype(jnp.float32) + came.astype(jnp.float32)).astype(jnp.bfloat16)
+
+                line_copy(way, steps, c).start()
+
+    def dn_part(part):
+        at = pl.ds(pl.multiple_of(part * rows, rows), rows)
+
+        def columns(n, carry):
+            cols = pl.ds(pl.multiple_of(n * tile, tile), tile)
+            dn[at, cols] = lax.dot_general(
+                dmixed_ref[at, :], weight_ref[cols, :], (((1,), (1,)), ((), ())), preferred_element_type=jnp.float32
+            ).astype(jnp.bfloat16)
+            return carry
+
+        lax.fori_loop(0, width // tile, columns, 0)
+
+    def each_part(part, carry):
+        dn_part(part)
+        return carry
+
+    lax.fori_loop(0, parts, each_part, 0)
+    for c in range(4):
+        pass_line(parts - 1, c)
+
+    def grad_block(owner, store):
+        left = pl.ds(pl.multiple_of(owner * tall, tall), tall)
+
+        def columns(n, carry):
+            cols = pl.ds(pl.multiple_of(n * tile, tile), tile)
+            store(
+                cols,
+                lax.dot_general(
+                    normed_ref[:, left], dmixed_ref[:, cols], (((0,), (0,)), ((), ())),
+                    preferred_element_type=jnp.float32,
+                ),
+            )
+            return carry
+
+        lax.fori_loop(0, both // tile, columns, 0)
+
+    mates = (diag, xm, ym, d)
+    sib_of = lambda mate: mate + sib - d
+
+    def pair_copy(r):
+        return remote(sib_send.at[r], sib_recv.at[r], pair_send.at[0, r], pair_recv.at[0, r], (sib, s))
+
+    def pair_copy_small(r):
+        return remote(small_sib_send.at[r], small_sib_recv.at[r], pair_send.at[1, r], pair_recv.at[1, r], (sib, s))
+
+    def cross_copy(r):
+        return remote(q_send.at[r], q_recv.at[r], cross_send.at[0, r], cross_recv.at[0, r], (mates[r], s))
+
+    def cross_copy_small(r):
+        return remote(small_q_send.at[r], small_q_recv.at[r], cross_send.at[1, r], cross_recv.at[1, r], (mates[r], s))
+
+    for r in range(4):
+        def store_pair(cols, value):
+            sib_send[r, :, cols] = value.astype(jnp.bfloat16)
+
+        grad_block(sib_of(mates[r]), store_pair)
+        pair_copy(r).start()
+        small_sib_send[r] = small_ref[sib_of(mates[r])].astype(jnp.bfloat16)
+        pair_copy_small(r).start()
+        if parts > 2:
+            pass_line(parts - 2, r)
+    for r in range(4):
+        pair_copy(r).wait_recv()
+        pair_copy_small(r).wait_recv()
+        both_small = small_ref[mates[r]] + small_sib_recv[r].astype(jnp.float32)
+        if r < 3:
+            def store_cross(cols, value):
+                q_send[r, :, cols] = (value + sib_recv[r, :, cols].astype(jnp.float32)).astype(jnp.bfloat16)
+
+            grad_block(mates[r], store_cross)
+            cross_copy(r).start()
+            small_q_send[r] = both_small.astype(jnp.bfloat16)
+            cross_copy_small(r).start()
+        else:
+            def store_total(cols, value):
+                total[:, cols] = value + sib_recv[r, :, cols].astype(jnp.float32)
+
+            grad_block(mates[r], store_total)
+            small_grad_ref[...] = both_small
+        if parts > 3:
+            pass_line(parts - 3, r)
+
+    for r in range(3):
+        cross_copy(r).wait_recv()
+        cross_copy_small(r).wait_recv()
+        total[...] += q_recv[r].astype(jnp.float32)
+        small_grad_ref[...] += small_q_recv[r].astype(jnp.float32)
+    z_send[...] = total[...].astype(jnp.bfloat16)
+
+    def near_copy(k):
+        to = lax.rem(s + k, parts)
+        return remote(
+            z_send.at[pl.ds(pl.multiple_of(to * own, own), own), :], z_recv.at[k], near_send.at[k], near_recv.at[k], (d, to)
+        )
+
+    for k in range(1, parts):
+        near_copy(k).start()
+
+    for c in range(4):
+        mine = dn_rows(s, c)
+        dn_total = dn[mine, :].astype(jnp.float32)
+        for way in (1, -1):
+            @pl.when(upstream(way))
+            def _():
+                line_wait(way, 0, c)
+
+        at = pl.ds(c * chunk, chunk)
+        low = jnp.where(upstream(1), dn_recv[s, at, :].astype(jnp.float32), 0.0)
+        high = jnp.where(upstream(-1), dn_recv[parts, at, :].astype(jnp.float32), 0.0)
+        v = (dn_total + low + high) * gain_ref[...]
+        flat = tokens_ref[at, :].astype(jnp.float32)
+        scale = lax.rsqrt(jnp.mean(flat * flat, axis=-1, keepdims=True) + 1e-05)
+        du = scale * v - flat * (scale * scale * scale) * jnp.mean(flat * v, axis=-1, keepdims=True)
+        input_grad_ref[at, :] = (cot_ref[at, :].astype(jnp.float32) + du).astype(jnp.bfloat16)
+
+    channel_blocks = both // block
+    gain_total = jnp.zeros((own, block), jnp.float32)
+    for k in range(parts):
+        source = lax.rem(s - k + parts, parts)
+        if k > 0:
+            near_copy(k).wait_recv()
+        for j in range(channel_blocks):
+            cols = slice(j * block, (j + 1) * block)
+            if k == 0:
+                piece = z_send[pl.ds(pl.multiple_of(s * own, own), own), cols]
+            else:
+                piece = z_recv[k, :, cols]
+            piece = piece.astype(jnp.float32)
+            to = pl.ds(pl.multiple_of((j * parts + source) * block, block), block)
+            in_grad_ref[:, to] = piece
+            gain_total = gain_total + piece * shard_ref[:, to].astype(jnp.float32)
+    gain_grad_ref[...] = jnp.broadcast_to(jnp.sum(gain_total, axis=1, keepdims=True), gain_grad_ref.shape)
+
+    for r in range(4):
+        pair_copy(r).wait_send()
+        pair_copy_small(r).wait_send()
+    for r in range(3):
+        cross_copy(r).wait_send()
+        cross_copy_small(r).wait_send()
+    for k in range(1, parts):
+        near_copy(k).wait_send()
+    for steps in range(1, parts):
+        for c in range(4):
+            for way in (1, -1):
+                @pl.when(valid(way, steps))
+                def _():
+                    line_copy(way, steps, c).wait_send()
+
+
+def end(dmixed, normed, weight, tokens, cotangent, gain, shard, small, parts, block):
+    both = dmixed.shape[1]
+    rows, width = tokens.shape
+    own = shard.shape[0]
+    dps, _, lanes = small.shape
+    tall = parts * own
+    vmem = pl.BlockSpec(memory_space=pltpu.VMEM)
+    dma = pltpu.SemaphoreType.DMA
+    low = jnp.bfloat16
+    return pl.pallas_call(
+        lambda *refs: end_body(parts, block, *refs),
+        out_shape=[
+            jax.ShapeDtypeStruct((rows, width), low),
+            jax.ShapeDtypeStruct((own, parts * both), jnp.float32),
+            jax.ShapeDtypeStruct((own, LANE), jnp.float32),
+            jax.ShapeDtypeStruct((block, lanes), jnp.float32),
+        ],
+        in_specs=[vmem] * 8,
+        out_specs=[vmem] * 4,
+        scratch_shapes=[
+            pltpu.VMEM((parts * rows, width), low),
+            pltpu.VMEM((parts + 1, rows, width), low),
+            pltpu.VMEM((4, tall, both), low), pltpu.VMEM((4, tall, both), low),
+            pltpu.VMEM((3, tall, both), low), pltpu.VMEM((3, tall, both), low),
+            pltpu.VMEM((tall, both), jnp.float32),
+            pltpu.VMEM((tall, both), low), pltpu.VMEM((parts, own, both), low),
+            pltpu.VMEM((4, block, lanes), low), pltpu.VMEM((4, block, lanes), low),
+            pltpu.VMEM((3, block, lanes), low), pltpu.VMEM((3, block, lanes), low),
+            dma((2, parts, 4)), dma((2, parts, 4)),
+            dma((2, 4)), dma((2, 4)), dma((2, 3)), dma((2, 3)), dma((parts,)), dma((parts,)),
+        ],
+        compiler_params=pltpu.CompilerParams(
+            collective_id=2, has_side_effects=True, vmem_limit_bytes=60 * 1024 * 1024
+        ),
+        cost_estimate=pl.CostEstimate(
+            flops=4 * parts * rows * width * both, bytes_accessed=30 * 1024 * 1024, transcendentals=0
+        ),
+    )(dmixed, normed, weight, tokens, cotangent, gain, shard, small)
+
+
 def contract(left, right, left_dim, right_dim):
     return lax.dot_general(
         left, right, (((left_dim,), (right_dim,)), ((), ())), preferred_element_type=jnp.float32
@@ -659,16 +966,20 @@
     kq = jnp.pad(projected[:, rank:], ((0, 0), (0, LANE - 2 * states)))
 
     gated, mixed, history, final = forward_scan(low, kq, values, gate, beta_w, beta_b, skip, states)
-    result_part = jnp.dot(gated, out_w, preferred_element_type=jnp.float32)
-    result = (flat + summed_rows(result_part, "seq")).astype(jnp.bfloat16)
-    out_grad = summed_rows(contract(gated, cot, 0, 0), "dp")
+    result_part = jnp.dot(gated, out_w, preferred_element_type=jnp.float32).astype(jnp.bfloat16)
+    result_part = result_part.reshape(parts, rows, width)
+    out_part = contract(gated, cot, 0, 0).astype(jnp.bfloat16).reshape(dps, block, width)
     dgated = contract(cot, out_w, 1, 1)
-    dgate, dpre_low, dvalues, dlow, dkq, bias_grad, skip_grad = backward_scan(
-        low, kq, values, gate, mixed, dgated, history, final, beta_w, beta_b, skip, states
+    dgate, dpre_low, dvalues, dlow, dkq, bias_grad, skip_grad, result_came, out_came = backward_scan(
+        low, kq, values, gate, mixed, dgated, history, final, beta_w, beta_b, skip, result_part, out_part, states
     )
+    part_here = lax.dynamic_index_in_dim(result_part, lax.axis_index("seq"), 0, False).astype(jnp.float32)
+    result = (flat + (part_here + jnp.sum(result_came.astype(jnp.float32), axis=0))).astype(jnp.bfloat16)
+    out_here = lax.dynamic_index_in_dim(out_part, lax.axis_index("dp"), 0, False).astype(jnp.float32)
+    out_grad = out_here + jnp.sum(out_came.astype(jnp.float32), axis=0)
     dprojected = lax.psum(jnp.concatenate([dlow, dkq[:, : 2 * states]], axis=1), "seq").astype(jnp.bfloat16)
-    beta_grad = scattered(contract(dpre_low, low, 0, 0), "dp")
-    select_grad = scattered(contract(values, dprojected, 0, 0), "dp")
+    beta_grad = contract(dpre_low, low, 0, 0)
+    select_grad = contract(values, dprojected, 0, 0)
     dvalues = contract(dprojected, select_w, 1, 1) + dvalues
     s = jax.nn.sigmoid(conv_sum)
     dconv = dvalues * (s + conv_sum * s * (1.0 - s))
@@ -680,29 +991,43 @@
     for tap in range(taps):
         dconv_in = dconv_in + sooner(dconv, taps - 1 - tap) * conv_w[:, tap]
     dmixed = jnp.concatenate([dconv_in.astype(jnp.bfloat16), dgate], axis=1)
-    in_grad = summed_rows(contract(normed, dmixed, 0, 0), "dp").astype(jnp.bfloat16)
-    in_grad = lax.all_to_all(in_grad.reshape(parts, own, 2 * channels), "seq", 0, 0)
-    in_grad = in_grad.reshape(parts, own, 2, dps, block).transpose(1, 2, 3, 0, 4).reshape(own, 2 * parts * channels)
-    dnormed = summed_rows(contract(dmixed, in_w, 1, 1), "seq")
-    v = dnormed * gain
-    du = scale * v - flat * (scale * scale * scale) * jnp.mean(flat * v, axis=-1, keepdims=True)
-    input_grad = (cotangent.reshape(rows, width).astype(jnp.float32) + du).astype(jnp.bfloat16)
-    gain_grad = scattered(jnp.sum(dnormed * flat * scale, axis=0), ("dp", "seq"))
-    rows_grad = scattered(
-        jnp.concatenate(
-            [conv_w_grad, conv_b_grad[:, None], bias_grad.reshape(channels, 1), skip_grad.reshape(channels, 1)], axis=1
-        ),
-        "dp",
+    vector_grads = jnp.concatenate(
+        [conv_w_grad, conv_b_grad[:, None], bias_grad.reshape(channels, 1), skip_grad.reshape(channels, 1)], axis=1
     )
+    small_grads = jnp.concatenate(
+        [
+            jnp.pad(select_grad, ((0, 0), (0, wide - select_grad.shape[1]))),
+            beta_grad,
+            jnp.pad(vector_grads, ((0, 0), (0, LANE - vector_grads.shape[1]))),
+        ],
+        axis=1,
+    ).reshape(dps, block, wide + rank + LANE)
+    cot_here = cotangent.reshape(rows, width)
+    if (dps, parts, 2 * own) == (8, 4, LANE):
+        input_grad, in_grad, gain_sums, small_grads = end(
+            dmixed, normed, in_w, tokens.reshape(rows, width), cot_here, gain.reshape(1, width), in_weight, small_grads,
+            parts, block,
+        )
+        gain_sums = gain_sums[:, 0]
+    else:
+        in_grad = summed_rows(contract(normed, dmixed, 0, 0), "dp").astype(jnp.bfloat16)
+        in_grad = lax.all_to_all(in_grad.reshape(parts, own, 2 * channels), "seq", 0, 0).astype(jnp.float32)
+        in_grad = in_grad.reshape(parts, own, 2, dps, block).transpose(1, 2, 3, 0, 4).reshape(own, 2 * parts * channels)
+        gain_sums = jnp.sum(in_grad * in_weight.astype(jnp.float32), axis=1)
+        v = summed_rows(contract(dmixed, in_w, 1, 1), "seq") * gain
+        du = scale * v - flat * (scale * scale * scale) * jnp.mean(flat * v, axis=-1, keepdims=True)
+        input_grad = (cot_here.astype(jnp.float32) + du).astype(jnp.bfloat16)
+        small_grads = jnp.sum(lax.all_to_all(small_grads, "dp", 0, 0), axis=0)
+    rows_grad = small_grads[:, wide + rank :]
     return (
         result.reshape(tokens.shape),
         input_grad.reshape(tokens.shape),
-        gain_grad,
-        in_grad.astype(jnp.float32),
+        gain_sums / norm_gain.astype(jnp.float32),
+        in_grad,
         rows_grad[:, :taps],
         rows_grad[:, taps],
-        select_grad,
-        beta_grad,
+        small_grads[:, : select_weight.shape[1]],
+        small_grads[:, wide : wide + rank],
         rows_grad[:, taps + 1],
         rows_grad[:, taps + 2],
         out_grad,

time: 873 us -> 628 us (0.72)
  waiting for transfers between devices: 356 us -> 109 us
  Pallas kernels: 244 us -> 371 us
  starting transfers between devices: 45.5 us -> 0.29 us
  blocking collectives: 81.2 us -> 38.8 us
  matrix products: 66.4 us -> 34.8 us
    all_to_all x5 -> x0, waiting for transfers between devices: 194 us -> none  [the longest x4 194 us: summed_rows(): parts = lax.all_to_all(parts, axis, 0, 0)]
    pallas_call x1 -> x2, Pallas kernels: 98 us -> 225 us  [the longest x1 125 us: end(): pl.pallas_call(lambda *refs: end_body(parts, block, *refs), out_shape=[ja...]
    all_to_all x5 -> x0, starting transfers between devices: 45.1 us -> none  [the longest x4 35.8 us: summed_rows(): parts = lax.all_to_all(parts, axis, 0, 0)]
    unnamed x1 -> x0, blocking collectives: 41.5 us -> none
    reduce_scatter x3 -> x0, waiting for transfers between devices: 30.6 us -> none  [scattered(): return lax.psum_scatter(total, axis, scatter_dimension=0, tiled=True)]
    dot_general x7 -> x5, matrix products: 56.5 us -> 27 us  [contract(): lax.dot_general(left, right, (((left_dim,), (right_dim,)), ((), ())), pre...]
    all_gather x2, waiting for transfers between devices: 80.1 us -> 59 us  [gathered(): return lax.all_gather(shard, axis, axis=0, tiled=True)]
    reduce_sum x6 -> x2, other arithmetic: 17.7 us -> 3.36 us  [the longest x1 2.73 us: local(): jnp.sum(result_came.astype(jnp.float32), axis=0)]
  transfers between devices with their start and end apart: 11 -> 3, of which waited for: 7 -> 3; matrix products, arithmetic and copies ran while one was open for 12% -> 2% of each run, Pallas kernels for 17% -> 8%
where the time goes in v3:
time: 628 us; the launch traced here: 621 us
  Pallas kernels  371 us (59%)
  waiting for transfers between devices  109 us (17%)
  blocking collectives  38.8 us (6%)
  matrix products  34.8 us (6%)
  local copies, waits for them, and re-layouts  26.6 us (4%)
  other arithmetic  26.3 us (4%)
  between operations  14.6 us (2%)
    pallas_call x1, Pallas kernels, end(): pl.pallas_call(lambda *refs: end_body(parts, block, *refs), out_shape=[ja...  125 us
    pallas_call x1, Pallas kernels, backward_scan(): pl.pallas_call(lambda *refs: backward_body(states, links, *refs), grid=(b...  101 us
    pallas_call x1, Pallas kernels, start(): pl.pallas_call(lambda *refs: start_body(parts, own, *refs), out_shape=[ja...  97.1 us
    all_gather x2, waiting for transfers between devices, gathered(): return lax.all_gather(shard, axis, axis=0, tiled=True)  59 us
    psum x1, waiting for transfers between devices, local(): lax.psum(jnp.dot(values, select_w, preferred_element_type=jnp.float32), '...  49.1 us
    pallas_call x1, Pallas kernels, forward_scan(): pl.pallas_call(lambda *refs: forward_body(states, *refs), grid=(blocks,),...  48.5 us
    psum x1, blocking collectives, local(): lax.psum(jnp.concatenate([dlow, dkq[:, :2 * states]], axis=1), 'seq')  38.8 us
    dot_general x5, matrix products, contract(): lax.dot_general(left, right, (((left_dim,), (right_dim,)), ((), ())), pre...  27 us
  transfers between devices with their start and end apart: 3, of which 3 were waited for; matrix products, arithmetic and copies ran while one was open for 2% of the time, Pallas kernels for 8%

profile of v3, /device:TPU:25, one launch (start us, length us, event | category | flops | bytes accessed | tf_op | source)
XLA Modules:
  0.0 621.3 jit_solution(14833044576818262059)
XLA Ops:
  9.7 1.8 reshape.90
  11.7 1.3 reshape.91.refs_1_
  14.2 97.1 %shard_map.194 = (bf16[1024,2048]{1,0:T(8,128)(2,1)}, bf16[2048,2048]{1,0:T(8,128)(2,1)}, bf16[1024,1024]{1,0:T(8,128)(2,1)}, f32[1024,1024]{1,0:T(8,128)}, bf16[8,192,512]{2,1,0:T(8,128)(2,1)}) custom-call(bf16[256,2048]{1,0:T(8,128)(2,1)} %bitcast.64, bf16[4,64,2048]{2,1,0:T(8,128)(2,1)} %reshape.91.refs_1_, bf16[128,512]{1,0:T(8,128)(2,1)} %fusion.19.refs_2_, ...), custom_call_target="tpu_custom_call" | custom-call | flops 8589934592 | bytes 41943040 | tf_op jit(solution)/shard_map/pallas_call | solution.py:578
  111.4 1.5 slice.105
  113.0 1.8 slice_reduce_fusion
  115.3 4.0 fusion.8
  119.4 1.7 fusion.12
  124.2 49.1 %all-reduce.14.cloned.1.call-done = f32[1024,160]{1,0:T(8,128)} async-done(((f32[1024,160]{1,0:T(8,128)}), f32[1024,160]{1,0:T(8,128)}) %all-reduce.14.cloned.1.call-update) | async-done | bytes 655376 | tf_op jit(solution)/shard_map/psum | solution.py:964
  174.4 1.3 slice.200.refs_0_
  175.7 48.5 %shard_map.195 = (bf16[1024,1024]{1,0:T(8,128)(2,1)S(1)}, f32[1024,1024]{1,0:T(8,128)}, bf16[16384,1024]{1,0:T(8,128)(2,1)}, f32[16,1024]{1,0:T(8,128)S(1)}) custom-call(bf16[1024,128]{1,0:T(8,128)(2,1)S(1)} %slice.200.refs_0_, f32[1024,128]{1,0:T(8,128)S(1)} %pad.52.refs_1_, bf16[1024,1024]{1,0:T(8,128)(2,1)S(1)} %get-tuple-element.109.refs_2_, ...), custom_call_target="tpu_custom_call" | custom-call | flops 234881024 | bytes 33554432 | tf_op jit(solution)/shard_map/pallas_call | solution.py:114
  224.8 1.4 copy-done.8
  226.2 28.0 %all-gather.5.cloned.1.call-done = bf16[1024,2048]{1,0:T(8,128)(2,1)} async-done(((bf16[256,2048]{1,0:T(8,128)(2,1)}), bf16[1024,2048]{1,0:T(8,128)(2,1)}) %all-gather.5.cloned.1.call-update) | async-done | bytes 4194320 | tf_op jit(solution)/shard_map/all_gather | solution.py:874
  254.2 9.3 %convolution_convert_fusion = bf16[1024,2048]{1,0:T(8,128)(2,1)} fusion(bf16[1024,1024]{1,0:T(8,128)(2,1)} %copy-done.8, bf16[1024,2048]{1,0:T(8,128)(2,1)} %all-gather.5.cloned.1.call-done), kind=kOutput, calls=%fused_computation.23 | convolution fusion | flops 4297064448 | bytes 10485760 | tf_op jit(solution)/shard_map/dot_general | solution.py:868
  263.6 31.0 %all-gather.3.cloned.1.call-done = bf16[1024,2048]{1,0:T(8,128)(2,1)} async-done(((bf16[128,2048]{1,0:T(8,128)(2,1)}), bf16[1024,2048]{1,0:T(8,128)(2,1)}) %all-gather.3.cloned.1.call-update) | async-done | bytes 4194320 | tf_op jit(solution)/shard_map/all_gather | solution.py:874
  294.5 10.0 %fusion.24.refs_5_ = f32[1024,1024]{1,0:T(8,128)} fusion(bf16[1024,2048]{1,0:T(8,128)(2,1)} %all-gather.5.cloned.1.call-done, bf16[1024,2048]{1,0:T(8,128)(2,1)} %all-gather.3.cloned.1.call-done), kind=kOutput, calls=%fused_computation.68 | convolution fusion | flops 4294967296 | bytes 12582912 | tf_op jit(solution)/shard_map/dot_general | solution.py:868
  304.6 6.2 convolution_convert_fusion.1
  310.8 100.5 %shard_map.196 = (bf16[1024,1024]{1,0:T(8,128)(2,1)}, bf16[1024,1024]{1,0:T(8,128)(2,1)}, f32[1024,1024]{1,0:T(8,128)}, f32[1024,128]{1,0:T(8,128)}, f32[1024,12...) custom-call(bf16[1024,128]{1,0:T(8,128)(2,1)} %copy-done.4, ...), custom_call_target="tpu_custom_call" | custom-call | flops 503316480 | bytes 33554432 | tf_op jit(solution)/shard_map/pallas_call | solution.py:303
  411.3 1.3 pad_maximum_fusion.1
  412.6 38.8 %all-reduce.15 = bf16[1024,160]{1,0:T(8,128)(2,1)} all-reduce(f32[1024,160]{1,0:T(8,128)S(1)} %pad_maximum_fusion.1), channel_id=1, replica_groups=mesh['dp'=8,'seq'=4] {'seq'}, use_global_device_ids=true, to_apply=%region_2.3 | all-reduce | flops 163840 | bytes 983040 | tf_op jit(solution)/shard_map/psum | solution.py:980
  451.4 1.7 fusion.25
  454.0 4.3 add_multiply_fusion
  458.4 4.9 multiply_reduce_fusion.1
  463.3 1.5 fusion.22
  465.2 1.8 copy.49
  467.0 4.7 pad_maximum_fusion.refs_0_
  471.7 124.6 %shard_map.197 = (bf16[256,2048]{1,0:T(8,128)(2,1)}, f32[64,8192]{1,0:T(8,128)}, f32[64,128]{1,0:T(8,128)}, f32[128,512]{1,0:T(8,128)}) custom-call(bf16[1024,2048]{1,0:T(8,128)(2,1)} %pad_maximum_fusion.refs_0_, bf16[1024,2048]{1,0:T(8,128)(2,1)} %get-tuple-element.51.refs_1_, bf16[2048,2048]{1,0:T(8,128)(2,1)} %get-tuple-element.52.refs_2_, ...), custom_call_target="tpu_custom_call" | custom-call | flops 17179869184 | bytes 31457280 | tf_op jit(solution)/shard_map/pallas_call | solution.py:836
  596.2 1.8 slice_reduce_fusion.7
  598.1 1.5 slice.131
  601.3 2.7 convert_reduce_fusion.1
  606.7 3.2 fusion.10
  609.9 2.1 convert_add_fusion
  613.0 1.3 copy.63
  (85 shorter events, 16.0 us)
Async XLA Ops:
  7.2 5.8 copy-start.22
  7.2 166.1 %all-reduce.14.cloned.1.call-start = ((), (), s32[]{:S(2)}) async-start(), calls=%async_computation | async-start | bytes 2097152 | tf_op jit(solution)/shard_map/psum | solution.py:964
  111.4 3.5 copy-start.12
  112.9 6.5 %copy-start.17 = (bf16[8,128,512]{2,1,0:T(8,128)(2,1)}, bf16[8,128,512]{2,1,0:T(8,128)(2,1)S(1)}, u32[]{:S(2)}) copy-start(bf16[8,128,512]{2,1,0:T(8,128)(2,1)S(1)} %slice.105) | copy-start | bytes 3145732
  113.0 62.7 %copy-start.3 = (bf16[1024,128]{1,0:T(8,128)(2,1)}, bf16[1024,128]{1,0:T(8,128)(2,1)S(1)}, u32[]{:S(2)}) copy-start(bf16[1024,128]{1,0:T(8,128)(2,1)S(1)} %get-tuple-element.112.refs_4_.refs_8_) | copy-start | bytes 786436
  114.8 60.9 %copy-start.6 = (f32[1024]{0:T(1024)}, f32[1024]{0:T(1024)S(1)}, u32[]{:S(2)}) copy-start(f32[1024]{0:T(1024)S(1)} %get-tuple-element.99) | copy-start | bytes 12292
  114.8 60.9 %copy-start.7 = (f32[1024]{0:T(1024)}, f32[1024]{0:T(1024)S(1)}, u32[]{:S(2)}) copy-start(f32[1024]{0:T(1024)S(1)} %get-tuple-element.100) | copy-start | bytes 12292
  115.3 4.1 copy-start.10
  119.4 56.3 %copy-start = (bf16[1024,1024]{1,0:T(8,128)(2,1)}, bf16[1024,1024]{1,0:T(8,128)(2,1)S(1)}, u32[]{:S(2)}) copy-start(bf16[1024,1024]{1,0:T(8,128)(2,1)S(1)} %get-tuple-element.109.refs_2_) | copy-start | bytes 6291460
  121.1 133.1 %all-gather.5.cloned.1.call-start = ((), (), s32[]{:S(2)}) async-start(), calls=%async_computation.2 | async-start | bytes 5242880 | tf_op jit(solution)/shard_map/all_gather | solution.py:874
  121.8 172.7 %all-gather.3.cloned.1.call-start = ((), (), s32[]{:S(2)}) async-start(), calls=%async_computation.1 | async-start | bytes 4718592 | tf_op jit(solution)/shard_map/all_gather | solution.py:874
  174.4 89.2 %copy-start.2 = (f32[1024,128]{1,0:T(8,128)}, f32[1024,128]{1,0:T(8,128)S(1)}, u32[]{:S(2)}) copy-start(f32[1024,128]{1,0:T(8,128)S(1)} %pad.52.refs_1_) | copy-start | bytes 1572868
  175.7 87.9 %copy-start.4 = (bf16[1024,128]{1,0:T(8,128)(2,1)}, bf16[1024,128]{1,0:T(8,128)(2,1)S(1)}, u32[]{:S(2)}) copy-start(bf16[1024,128]{1,0:T(8,128)(2,1)S(1)} %slice.200.refs_0_) | copy-start | bytes 786436
  224.2 0.6 copy-start.5
  224.8 1.4 copy-start.8
  263.6 41.0 %copy-start.9 = (bf16[1024,1024]{1,0:T(8,128)(2,1)S(1)}, bf16[1024,1024]{1,0:T(8,128)(2,1)}, u32[]{:S(2)}) copy-start(bf16[1024,1024]{1,0:T(8,128)(2,1)} %copy-done.8) | copy-start | bytes 6291460
  294.5 10.1 %copy-start.25 = (bf16[1024,2048]{1,0:T(8,128)(2,1)S(1)}, bf16[1024,2048]{1,0:T(8,128)(2,1)}, u32[]{:S(2)}) copy-start(bf16[1024,2048]{1,0:T(8,128)(2,1)} %all-gather.3.cloned.1.call-done) | copy-start | bytes 12582916
  310.8 140.6 %copy-start.1 = (bf16[1024,1024]{1,0:T(8,128)(2,1)S(1)}, bf16[1024,1024]{1,0:T(8,128)(2,1)}, u32[]{:S(2)}) copy-start(bf16[1024,1024]{1,0:T(8,128)(2,1)} %copy-done) | copy-start | bytes 6291460
  451.4 2.3 copy-start.15
  451.4 2.6 copy-start.18
  454.0 4.3 copy-start.11
  454.0 4.3 copy-start.13
  458.3 4.9 copy-start.23
  458.4 4.9 copy-start.24
  458.4 5.0 copy-start.14
  596.2 7.8 %copy-start.16 = (bf16[7,128,2048]{2,1,0:T(8,128)(2,1)S(1)}, bf16[7,128,2048]{2,1,0:T(8,128)(2,1)}, u32[]{:S(2)}) copy-start(bf16[7,128,2048]{2,1,0:T(8,128)(2,1)} %get-tuple-element.60) | copy-start | bytes 11010052
  601.3 3.4 copy-start.21
  601.3 3.5 copy-start.26
  606.7 5.3 copy-start.20
  606.7 6.3 %copy-start.19 = (f32[64,8192]{1,0:T(8,128)S(1)}, f32[64,8192]{1,0:T(8,128)}, u32[]{:S(2)}) copy-start(f32[64,8192]{1,0:T(8,128)} %get-tuple-element.128) | copy-start | bytes 6291460
Sparse Core Ops, SparseCore 0:
  121.2 52.0 all-reduce.13
  174.9 79.2 all-gather.4
  256.3 38.2 all-gather.2

commit v4 on v3

--- a/solution.py
+++ b/solution.py
@@ -40,37 +40,20 @@
     lax.fori_loop(0, rows // 8, body, 0)
 
 
-def step_sizes(low_ref, kq_ref, weight_ref, bias_ref, states):
+def step_sizes(low, kq, weight_ref, bias_ref, states):
     pre = lax.dot_general(
-        low_ref[...], weight_ref[...], (((1,), (1,)), ((), ())), preferred_element_type=jnp.float32
+        low, weight_ref[...], (((1,), (1,)), ((), ())), preferred_element_type=jnp.float32
     )
     beta = sigmoid(pre + bias_ref[...])
-    lane = lax.broadcasted_iota(jnp.int32, kq_ref.shape, 1)
-    keys = jnp.where(lane < states, kq_ref[...], 0.0)
+    lane = lax.broadcasted_iota(jnp.int32, kq.shape, 1)
+    keys = jnp.where(lane < states, kq, 0.0)
     square = jnp.sum(keys * keys, axis=1, keepdims=True)
     return beta, 1.0 / (1.0 + beta * square)
 
 
-def forward_body(
-    states, low_ref, kq_ref, values_ref, gate_ref, weight_ref, bias_ref, skip_ref,
-    gated_ref, mixed_ref, history_ref, final_ref,
-    state_ref, key_ref, query_ref, rate_ref, input_ref, out_ref, row_ref,
-):
-    rows, channels = values_ref.shape
+def forward_rows(states, rows, channels, history_ref, state_ref, key_ref, query_ref, rate_ref, input_ref, out_ref):
     tiles = channels // LANE
     per_group = min(4, tiles)
-
-    @pl.when(pl.program_id(0) == 0)
-    def _():
-        state_ref[...] = jnp.zeros_like(state_ref)
-
-    beta, inverse = step_sizes(low_ref, kq_ref, weight_ref, bias_ref, states)
-    rates = beta * inverse
-    rate_ref[...] = by_eights(rates)
-    input_ref[...] = by_eights(rates * values_ref[...].astype(jnp.float32))
-    row_ref[...] = by_eights(kq_ref[...])
-    spread_columns(row_ref, key_ref, query_ref, rows, states)
-
     for first in range(0, tiles, per_group):
         columns = [slice((first + j) * LANE, (first + j + 1) * LANE) for j in range(per_group)]
 
@@ -94,6 +77,26 @@
         for cols, state in zip(columns, done):
             state_ref[:, cols] = state
 
+
+def forward_body(
+    states, low_ref, kq_ref, values_ref, gate_ref, weight_ref, bias_ref, skip_ref,
+    gated_ref, mixed_ref, history_ref, final_ref,
+    state_ref, key_ref, query_ref, rate_ref, input_ref, out_ref, row_ref,
+):
+    rows, channels = values_ref.shape
+
+    @pl.when(pl.program_id(0) == 0)
+    def _():
+        state_ref[...] = jnp.zeros_like(state_ref)
+
+    beta, inverse = step_sizes(low_ref[...], kq_ref[...], weight_ref, bias_ref, states)
+    rates = beta * inverse
+    rate_ref[...] = by_eights(rates)
+    input_ref[...] = by_eights(rates * values_ref[...].astype(jnp.float32))
+    row_ref[...] = by_eights(kq_ref[...])
+    spread_columns(row_ref, key_ref, query_ref, rows, states)
+
+    forward_rows(states, rows, channels, history_ref, state_ref, key_ref, query_ref, rate_ref, input_ref, out_ref)
     mixed = as_rows(out_ref[...]) + skip_ref[...] * values_ref[...].astype(jnp.float32)
     gate = gate_ref[...]
     mixed_ref[...] = mixed
@@ -160,7 +163,7 @@
         for copy in copies:
             copy.start()
 
-    beta, inverse = step_sizes(low_ref, kq_ref, weight_ref, bias_ref, states)
+    beta, inverse = step_sizes(low_ref[...], kq_ref[...], weight_ref, bias_ref, states)
     rate_ref[...] = by_eights(beta * inverse)
     values = values_ref[...].astype(jnp.float32)
     values32_ref[...] = by_eights(values)
@@ -221,7 +224,7 @@
     fed = as_rows(fed_ref[...])
     dvalues_ref[...] = fed + skip_ref[...] * as_rows(do_ref[...])
     scaled = as_rows(values32_ref[...]) * fed - as_rows(kept_ref[...])
-    beta, inverse = step_sizes(low_ref, kq_ref, weight_ref, bias_ref, states)
+    beta, inverse = step_sizes(low_ref[...], kq_ref[...], weight_ref, bias_ref, states)
     dpre = scaled * (1.0 - beta) * inverse
     bias_grad_ref[...] += jnp.sum(dpre, axis=0, keepdims=True)
     dpre_low = dpre.astype(jnp.bfloat16)
@@ -864,6 +867,292 @@
     )(dmixed, normed, weight, tokens, cotangent, gain, shard, small)
 
 
+def linked_forward_body(
+    states, parts, dps, taps,
+    conv_in_ref, gate_ref, select_ref, conv_w_ref, conv_b_ref, weight_ref, bias_ref, skip_ref, out_shard, cot_shard,
+    gated_ref, mixed_ref, history_ref, final_ref, values_ref, low_ref, kq_ref, out_all, cot_all,
+    state_ref, key_ref, query_ref, rate_ref, input_ref, out_ref, row_ref,
+    part_low, part_kq, came_low, came_kq, sum_low, sum_kq,
+    rs_send, rs_recv, ag_send, ag_recv, out_send, out_recv, line_send, line_recv, local_sem,
+):
+    d, s = lax.axis_index("dp"), lax.axis_index("seq")
+    step = pl.program_id(0)
+    length, channels = values_ref.shape
+    rows = gate_ref.shape[0]
+    span = length // parts
+    block = out_shard.shape[0]
+    chunk = span // 4
+    packed = LANE // (2 * states)
+    short = span // packed
+
+    def remote(src, dst, send, recv, to):
+        return pltpu.make_async_remote_copy(
+            src_ref=src, dst_ref=dst, send_sem=send, recv_sem=recv, device_id=to, device_id_type=MESH
+        )
+
+    def out_rows(owner):
+        return out_all.at[pl.ds(pl.multiple_of(owner * block, block), block), :]
+
+    out_copies = []
+    for k in range(1, dps):
+        out_copies.append(
+            remote(out_shard, out_rows(d), out_send.at[k - 1], out_recv.at[k - 1], (lax.rem(d + k, dps), s))
+        )
+
+    def cot_rows(part, c):
+        return cot_all.at[pl.ds(pl.multiple_of(part * span + c * chunk, chunk), chunk), :]
+
+    def cot_copy(way, distance, c):
+        part = s - way * (distance - 1)
+        src = cot_shard.at[pl.ds(c * chunk, chunk), :] if distance == 1 else cot_rows(part, c)
+        side = 0 if way == 1 else 1
+        return remote(
+            src, cot_rows(part, c), line_send.at[side, distance, c], line_recv.at[side, distance, c], (d, s + way)
+        )
+
+    def can_send(way, distance):
+        reach = s + 1 < parts if way == 1 else s >= 1
+        came = s - (distance - 1) >= 0 if way == 1 else s + (distance - 1) < parts
+        return jnp.logical_and(reach, came)
+
+    def send_cot(distance, c):
+        for way in (1, -1):
+            @pl.when(can_send(way, distance))
+            def _():
+                cot_copy(way, distance, c).start()
+
+    def sent_cot(distance, c):
+        for way in (1, -1):
+            @pl.when(can_send(way, distance))
+            def _():
+                cot_copy(way, distance, c).wait_send()
+
+    def take_cot(distance, c):
+        for way in (1, -1):
+            @pl.when(s >= distance if way == 1 else s + distance < parts)
+            def _():
+                part = s - way * distance
+                side = 0 if way == 1 else 1
+                remote(
+                    cot_rows(part, c), cot_rows(part, c), line_send.at[side, distance, c],
+                    line_recv.at[side, distance, c], (d, s),
+                ).wait_recv()
+
+    def own_copies():
+        return (
+            pltpu.make_async_copy(out_shard, out_rows(d), local_sem.at[0]),
+            pltpu.make_async_copy(
+                cot_shard, cot_all.at[pl.ds(pl.multiple_of(s * span, span), span), :], local_sem.at[1]
+            ),
+        )
+
+    @pl.when(step == 0)
+    def _():
+        barrier = pltpu.get_barrier_semaphore()
+        for k in range(1, parts):
+            pl.semaphore_signal(barrier, inc=1, device_id=(d, lax.rem(s + k, parts)), device_id_type=MESH)
+        for k in range(1, dps):
+            pl.semaphore_signal(barrier, inc=1, device_id=(lax.rem(d + k, dps), s), device_id_type=MESH)
+        pl.semaphore_wait(barrier, parts + dps - 2)
+        state_ref[...] = jnp.zeros_like(state_ref)
+        for copy in out_copies:
+            copy.start()
+        for copy in own_copies():
+            copy.start()
+        for c in range(4):
+            send_cot(1, c)
+
+    def rs_copies(k):
+        at = lax.rem(s + k, parts)
+        return (
+            remote(part_low.at[at], came_low.at[k - 1], rs_send.at[0, k - 1], rs_recv.at[0, k - 1], (d, at)),
+            remote(part_kq.at[at], came_kq.at[k - 1], rs_send.at[1, k - 1], rs_recv.at[1, k - 1], (d, at)),
+        )
+
+    def ag_copies(k):
+        to = lax.rem(s + k, parts)
+        return (
+            remote(sum_low.at[s], sum_low.at[s], ag_send.at[0, k - 1], ag_recv.at[0, k - 1], (d, to)),
+            remote(sum_kq.at[s], sum_kq.at[s], ag_send.at[1, k - 1], ag_recv.at[1, k - 1], (d, to)),
+        )
+
+    def ag_taken(k, part):
+        return (
+            remote(sum_low.at[part], sum_low.at[part], ag_send.at[0, k - 1], ag_recv.at[0, k - 1], (d, s)),
+            remote(sum_kq.at[part], sum_kq.at[part], ag_send.at[1, k - 1], ag_recv.at[1, k - 1], (d, s)),
+        )
+
+    def convolve(part):
+        start = pl.multiple_of(part * span, span)
+        before = pl.multiple_of(jnp.maximum(start - 16, 0), 16)
+        wide = min(256, channels)
+        for left in range(0, channels, wide):
+            cols = slice(left, left + wide)
+            head = conv_in_ref[pl.ds(before, 16), cols].astype(jnp.float32)
+            head = jnp.where(part == 0, 0.0, head)
+            body = jnp.concatenate([head, conv_in_ref[pl.ds(start, span), cols].astype(jnp.float32)], axis=0)
+            total = conv_b_ref[:, cols]
+            for tap in range(taps):
+                by = taps - 1 - tap
+                total = total + body[16 - by : 16 - by + span] * conv_w_ref[tap : tap + 1, cols]
+            values_ref[pl.ds(start, span), cols] = (total * sigmoid(total)).astype(jnp.bfloat16)
+        projected = jnp.dot(values_ref[pl.ds(start, span), :], select_ref[...], preferred_element_type=jnp.float32)
+        part_low[part] = projected[:, :LANE]
+        pack = projected[:short, LANE:]
+        for g in range(1, packed):
+            pack = pack + pltpu.roll(projected[g * short : (g + 1) * short, LANE:], g * 2 * states, 1)
+        part_kq[part] = pack
+
+    @pl.when(step < parts - 1)
+    def _():
+        convolve(lax.rem(s + 1 + step, parts))
+
+    for k in range(1, parts):
+        @pl.when(step == k - 1)
+        def _():
+            for copy in rs_copies(k):
+                copy.start()
+
+    @pl.when(step == parts - 1)
+    def _():
+        convolve(s)
+        low = part_low[s]
+        kq = part_kq[s]
+        for k in range(1, parts):
+            for copy in rs_copies(k):
+                copy.wait_recv()
+            low = low + came_low[k - 1]
+            kq = kq + came_kq[k - 1]
+        sum_low[s] = low.astype(jnp.bfloat16)
+        sum_kq[s] = kq
+        for k in range(1, parts):
+            for copy in ag_copies(k):
+                copy.start()
+
+    per_part = span // rows
+    at_block = step - parts
+
+    def unpack(part):
+        start = pl.multiple_of(part * span, span)
+        low_ref[pl.ds(start, span), :] = sum_low[part]
+        pack = sum_kq[part]
+        lane = lax.broadcasted_iota(jnp.int32, pack.shape, 1)
+        for g in range(packed):
+            turned = pack if g == 0 else pltpu.roll(pack, LANE - g * 2 * states, 1)
+            kq_ref[pl.ds(pl.multiple_of(start + g * short, short), short), :] = jnp.where(lane < 2 * states, turned, 0.0)
+
+    for part in range(parts):
+        @pl.when(at_block == part * per_part)
+        def _():
+            for k in range(1, parts):
+                @pl.when(lax.rem(s - k + parts, parts) == part)
+                def _():
+                    for copy in ag_taken(k, part):
+                        copy.wait_recv()
+
+            unpack(part)
+
+    plan = {0: ((1, 0), (1, 1)), 1: ((1, 2), (1, 3)), 2: ((2, 0),), 3: ((2, 1),), 4: ((2, 2),), 5: ((2, 3),)}
+    for at, moves in plan.items():
+        @pl.when(at_block == at)
+        def _():
+            for distance, c in moves:
+                take_cot(distance, c)
+                send_cot(distance + 1, c)
+
+    @pl.when(at_block >= 0)
+    def _():
+        here = pl.ds(pl.multiple_of(at_block * rows, rows), rows)
+        kq = kq_ref[here, :]
+        values = values_ref[here, :].astype(jnp.float32)
+        beta, inverse = step_sizes(low_ref[here, :], kq, weight_ref, bias_ref, states)
+        rates = beta * inverse
+        rate_ref[...] = by_eights(rates)
+        input_ref[...] = by_eights(rates * values)
+        row_ref[...] = by_eights(kq)
+        spread_columns(row_ref, key_ref, query_ref, rows, states)
+        forward_rows(states, rows, channels, history_ref, state_ref, key_ref, query_ref, rate_ref, input_ref, out_ref)
+        mixed = as_rows(out_ref[...]) + skip_ref[...] * values
+        gate = gate_ref[...]
+        mixed_ref[...] = mixed
+        gated_ref[...] = (mixed * gate * sigmoid(gate)).astype(jnp.bfloat16)
+
+    @pl.when(step == pl.num_programs(0) - 1)
+    def _():
+        final_ref[...] = state_ref[...]
+        for c in range(4):
+            take_cot(parts - 1, c)
+        for copy in own_copies():
+            copy.wait()
+        for copy in out_copies:
+            copy.wait_recv()
+        for copy in out_copies:
+            copy.wait_send()
+        for distance in range(1, parts):
+            for c in range(4):
+                sent_cot(distance, c)
+        for k in range(1, parts):
+            for copy in rs_copies(k) + ag_copies(k):
+                copy.wait_send()
+
+
+def linked_forward(conv_in, gate, select, conv_w, conv_b, weight, bias, skip, out_shard, cot_shard, parts, dps, states):
+    length, channels = conv_in.shape
+    taps = conv_w.shape[0]
+    block, width = out_shard.shape
+    span = length // parts
+    rows = min(128, span)
+    blocks = length // rows
+    short = span // (LANE // (2 * states))
+    at = lambda i: jnp.maximum(i - parts, 0)
+    by_row = lambda size: pl.BlockSpec((rows, size), lambda i: (at(i), 0))
+    whole = lambda a: pl.BlockSpec(a.shape, lambda i: (0, 0))
+    kept = lambda *shape: pl.BlockSpec(shape, lambda i: (0, 0))
+    anywhere = pl.BlockSpec(memory_space=pl.ANY)
+    dma = pltpu.SemaphoreType.DMA
+    f32, low = jnp.float32, jnp.bfloat16
+    eights = pltpu.VMEM((rows // 8, 8, channels), f32)
+    return pl.pallas_call(
+        lambda *refs: linked_forward_body(states, parts, dps, taps, *refs),
+        grid=(parts + blocks,),
+        in_specs=[
+            whole(conv_in), by_row(channels), whole(select), whole(conv_w), whole(conv_b), whole(weight), whole(bias),
+            whole(skip), anywhere, anywhere,
+        ],
+        out_specs=[
+            by_row(channels), by_row(channels), pl.BlockSpec((rows * states, channels), lambda i: (at(i), 0)),
+            kept(states, channels), kept(length, channels), kept(length, LANE), kept(length, LANE), anywhere, anywhere,
+        ],
+        out_shape=[
+            jax.ShapeDtypeStruct((length, channels), low),
+            jax.ShapeDtypeStruct((length, channels), f32),
+            jax.ShapeDtypeStruct((length * states, channels), low),
+            jax.ShapeDtypeStruct((states, channels), f32),
+            jax.ShapeDtypeStruct((length, channels), low),
+            jax.ShapeDtypeStruct((length, LANE), low),
+            jax.ShapeDtypeStruct((length, LANE), f32),
+            jax.ShapeDtypeStruct((dps * block, width), low),
+            jax.ShapeDtypeStruct((length, width), low),
+        ],
+        scratch_shapes=[
+            pltpu.VMEM((states, channels), f32),
+            pltpu.VMEM((rows * states, LANE), f32), pltpu.VMEM((rows * states, LANE), f32),
+            eights, eights, eights, pltpu.VMEM((rows // 8, 8, LANE), f32),
+            pltpu.VMEM((parts, span, LANE), f32), pltpu.VMEM((parts, short, LANE), f32),
+            pltpu.VMEM((parts - 1, span, LANE), f32), pltpu.VMEM((parts - 1, short, LANE), f32),
+            pltpu.VMEM((parts, span, LANE), low), pltpu.VMEM((parts, short, LANE), f32),
+            dma((2, parts - 1)), dma((2, parts - 1)), dma((2, parts - 1)), dma((2, parts - 1)),
+            dma((dps - 1,)), dma((dps - 1,)), dma((2, parts, 4)), dma((2, parts, 4)), dma((2,)),
+        ],
+        compiler_params=pltpu.CompilerParams(
+            collective_id=4, has_side_effects=True, vmem_limit_bytes=56 * 1024 * 1024
+        ),
+        cost_estimate=pl.CostEstimate(
+            flops=14 * length * states * channels, bytes_accessed=2 * length * states * channels, transcendentals=0
+        ),
+    )(conv_in, gate, select, conv_w, conv_b, weight, bias, skip, out_shard, cot_shard)
+
+
 def contract(left, right, left_dim, right_dim):
     return lax.dot_general(
         left, right, (((left_dim,), (right_dim,)), ((), ())), preferred_element_type=jnp.float32
@@ -934,7 +1223,8 @@
         ],
         axis=1,
     )
-    if (dps, parts, 2 * own) == (8, 4, LANE):
+    small_slice = (dps, parts, 2 * own, rank) == (8, 4, LANE, LANE)
+    if small_slice:
         doubled = jnp.broadcast_to(jnp.tile(norm_gain.reshape(1, own), (1, 2)), (GAIN_ROWS, LANE))
         normed, in_w, conv_in, gate, extra = start(tokens.reshape(rows, width), spread, small, doubled, dps)
         smalls = extra[:, :block].reshape(channels, small.shape[1])
@@ -952,20 +1242,24 @@
     vectors = smalls[:, wide + rank :].astype(jnp.float32)
     conv_w, conv_b = vectors[:, :taps], vectors[:, taps]
     beta_b, skip = vectors[:, taps + 1].reshape(1, channels), vectors[:, taps + 2].reshape(1, channels)
-    out_shard, cot_shard, conv_in = lax.optimization_barrier((out_weight, cotangent.reshape(rows, width), conv_in))
-    out_w = gathered(out_shard, "dp")
-    cot = gathered(cot_shard, "seq")
-
+    cot_here = cotangent.reshape(rows, width)
     conv_wide = conv_in.astype(jnp.float32)
     conv_sum = conv_b
     for tap in range(taps):
         conv_sum = conv_sum + later(conv_wide, taps - 1 - tap) * conv_w[:, tap]
-    values = jax.nn.silu(conv_sum).astype(jnp.bfloat16)
-    projected = lax.psum(jnp.dot(values, select_w, preferred_element_type=jnp.float32), "seq")
-    low = projected[:, :rank].astype(jnp.bfloat16)
-    kq = jnp.pad(projected[:, rank:], ((0, 0), (0, LANE - 2 * states)))
-
-    gated, mixed, history, final = forward_scan(low, kq, values, gate, beta_w, beta_b, skip, states)
+    if small_slice:
+        gated, mixed, history, final, values, low, kq, out_w, cot = linked_forward(
+            conv_in, gate, smalls[:, :wide], conv_w.T, conv_b.reshape(1, channels), beta_w, beta_b, skip, out_weight,
+            cot_here, parts, dps, states,
+        )
+    else:
+        out_w = gathered(out_weight, "dp")
+        cot = gathered(cot_here, "seq")
+        values = jax.nn.silu(conv_sum).astype(jnp.bfloat16)
+        projected = lax.psum(jnp.dot(values, select_w, preferred_element_type=jnp.float32), "seq")
+        low = projected[:, :rank].astype(jnp.bfloat16)
+        kq = jnp.pad(projected[:, rank:], ((0, 0), (0, LANE - 2 * states)))
+        gated, mixed, history, final = forward_scan(low, kq, values, gate, beta_w, beta_b, skip, states)
     result_part = jnp.dot(gated, out_w, preferred_element_type=jnp.float32).astype(jnp.bfloat16)
     result_part = result_part.reshape(parts, rows, width)
     out_part = contract(gated, cot, 0, 0).astype(jnp.bfloat16).reshape(dps, block, width)
@@ -1002,8 +1296,7 @@
         ],
         axis=1,
     ).reshape(dps, block, wide + rank + LANE)
-    cot_here = cotangent.reshape(rows, width)
-    if (dps, parts, 2 * own) == (8, 4, LANE):
+    if small_slice:
         input_grad, in_grad, gain_sums, small_grads = end(
             dmixed, normed, in_w, tokens.reshape(rows, width), cot_here, gain.reshape(1, width), in_weight, small_grads,
             parts, block,

time: 628 us -> 549 us (0.87)
  waiting for transfers between devices: 109 us -> 0 us
  Pallas kernels: 371 us -> 424 us
  between operations: 14.6 us -> 1.5 us
    all_gather x2 -> x0, waiting for transfers between devices: 59 us -> none  [gathered(): return lax.all_gather(shard, axis, axis=0, tiled=True)]
    pallas_call x1, Pallas kernels: 48.5 us -> 97.6 us  [linked_forward(): pl.pallas_call(lambda *refs: linked_forward_body(states, parts, dps, taps...]
    psum x1 -> x0, waiting for transfers between devices: 49.1 us -> none  [local(): lax.psum(jnp.dot(values, select_w, preferred_element_type=jnp.float32), '...]
  transfers between devices with their start and end apart: 3 -> 0, of which waited for: 3 -> 0; matrix products, arithmetic and copies ran while one was open for 2% -> 0% of each run, Pallas kernels for 8% -> 0%
where the time goes in v4:
time: 549 us; the launch traced here: 541 us
  Pallas kernels  424 us (77%)
  blocking collectives  38.8 us (7%)
  matrix products  29.1 us (5%)
  local copies, waits for them, and re-layouts  24.9 us (5%)
  other arithmetic  23.5 us (4%)
    pallas_call x1, Pallas kernels, end(): pl.pallas_call(lambda *refs: end_body(parts, block, *refs), out_shape=[ja...  124 us
    pallas_call x1, Pallas kernels, backward_scan(): pl.pallas_call(lambda *refs: backward_body(states, links, *refs), grid=(b...  105 us
    pallas_call x1, Pallas kernels, linked_forward(): pl.pallas_call(lambda *refs: linked_forward_body(states, parts, dps, taps...  97.6 us
    pallas_call x1, Pallas kernels, start(): pl.pallas_call(lambda *refs: start_body(parts, own, *refs), out_shape=[ja...  97.2 us
    psum x1, blocking collectives, local(): lax.psum(jnp.concatenate([dlow, dkq[:, :2 * states]], axis=1), 'seq')  38.8 us
    dot_general x5, matrix products, contract(): lax.dot_general(left, right, (((left_dim,), (right_dim,)), ((), ())), pre...  23.1 us

profile of v4, /device:TPU:25, one launch (start us, length us, event | category | flops | bytes accessed | tf_op | source)
XLA Modules:
  0.0 541.4 jit_solution(14976706745188235246)
XLA Ops:
  0.7 1.8 reshape.89
  2.7 1.3 reshape.90.refs_1_
  5.7 97.2 %shard_map.194 = (bf16[1024,2048]{1,0:T(8,128)(2,1)}, bf16[2048,2048]{1,0:T(8,128)(2,1)}, bf16[1024,1024]{1,0:T(8,128)(2,1)}, f32[1024,1024]{1,0:T(8,128)}, bf16[8,192,512]{2,1,0:T(8,128)(2,1)}) custom-call(bf16[256,2048]{1,0:T(8,128)(2,1)} %bitcast.63, bf16[4,64,2048]{2,1,0:T(8,128)(2,1)} %reshape.90.refs_1_, bf16[128,512]{1,0:T(8,128)(2,1)} %fusion.15.refs_2_, ...), custom_call_target="tpu_custom_call" | custom-call | flops 8589934592 | bytes 41943040 | tf_op jit(solution)/shard_map/pallas_call | solution.py:581
  102.8 1.3 slice.103
  104.2 0.9 fusion.17
  105.0 2.4 slice_reduce_fusion.3
  109.1 97.6 %shard_map.195 = (bf16[1024,1024]{1,0:T(8,128)(2,1)}, f32[1024,1024]{1,0:T(8,128)}, bf16[16384,1024]{1,0:T(8,128)(2,1)}, f32[16,1024]{1,0:T(8,128)}, bf16[1024,1...) custom-call(bf16[1024,1024]{1,0:T(8,128)(2,1)} %get-tuple-element.38, ...), custom_call_target="tpu_custom_call" | custom-call | flops 234881024 | bytes 33554432 | tf_op jit(solution)/shard_map/pallas_call | solution.py:1115
  206.7 9.5 %convolution_convert_fusion = bf16[1024,2048]{1,0:T(8,128)(2,1)} fusion(bf16[1024,1024]{1,0:T(8,128)(2,1)} %get-tuple-element.41, bf16[1024,2048]{1,0:T(8,128)(2,1)} %get-tuple-element.47), kind=kOutput, calls=%fused_computation.21 | convolution fusion | flops 4297064448 | bytes 10485760 | tf_op jit(solution)/shard_map/dot_general | solution.py:1157
  216.2 6.1 %convolution_convert_fusion.1 = bf16[1024,2048]{1,0:T(8,128)(2,1)} fusion(bf16[1024,1024]{1,0:T(8,128)(2,1)S(1)} %copy-done.23, bf16[1024,2048]{1,0:T(8,128)(2,1)S(1)} %copy-done.21), kind=kOutput, calls=%fused_computation.22 | convolution fusion | flops 4297064448 | bytes 10485760 | tf_op jit(solution)/shard_map/dot_general | solution.py:1263
  222.3 6.1 %fusion.18.refs_5_ = f32[1024,1024]{1,0:T(8,128)} fusion(bf16[1024,2048]{1,0:T(8,128)(2,1)S(1)} %copy-done.22, bf16[1024,2048]{1,0:T(8,128)(2,1)S(1)} %copy-done.21), kind=kOutput, calls=%fused_computation.60 | convolution fusion | flops 4294967296 | bytes 12582912 | tf_op jit(solution)/shard_map/dot_general | solution.py:1157
  228.4 104.5 %shard_map.196 = (bf16[1024,1024]{1,0:T(8,128)(2,1)}, bf16[1024,1024]{1,0:T(8,128)(2,1)}, f32[1024,1024]{1,0:T(8,128)}, f32[1024,128]{1,0:T(8,128)}, f32[1024,12...) custom-call(bf16[1024,128]{1,0:T(8,128)(2,1)} %get-tuple-element.43., ...), custom_call_target="tpu_custom_call" | custom-call | flops 503316480 | bytes 33554432 | tf_op jit(solution)/shard_map/pallas_call | solution.py:306
  333.0 2.9 convert_reduce_fusion
  335.9 2.2 convert_add_fusion
  338.1 1.3 fusion.19
  339.5 38.8 %all-reduce.11 = bf16[1024,160]{1,0:T(8,128)(2,1)} all-reduce(f32[1024,160]{1,0:T(8,128)S(1)} %pad_maximum_fusion.1), channel_id=1, replica_groups=mesh['dp'=8,'seq'=4] {'seq'}, use_global_device_ids=true, to_apply=%region_1.2 | all-reduce | flops 163840 | bytes 983040 | tf_op jit(solution)/shard_map/psum | solution.py:1274
  378.3 2.2 fusion.20
  381.9 1.3 copy-done.20
  383.2 4.0 add_multiply_fusion
  387.2 4.9 multiply_reduce_fusion.1
  392.4 1.9 copy.49
  394.3 4.7 pad_maximum_fusion.refs_0_
  399.0 0.9 slice.123
  400.6 124.4 %shard_map.197 = (bf16[256,2048]{1,0:T(8,128)(2,1)}, f32[64,8192]{1,0:T(8,128)}, f32[64,128]{1,0:T(8,128)}, f32[128,512]{1,0:T(8,128)}) custom-call(bf16[1024,2048]{1,0:T(8,128)(2,1)} %pad_maximum_fusion.refs_0_, bf16[1024,2048]{1,0:T(8,128)(2,1)} %get-tuple-element.55.refs_1_, bf16[2048,2048]{1,0:T(8,128)(2,1)} %get-tuple-element.56.refs_2_, ...), custom_call_target="tpu_custom_call" | custom-call | flops 17179869184 | bytes 31457280 | tf_op jit(solution)/shard_map/pallas_call | solution.py:839
  525.0 0.9 slice.128
  526.7 0.8 slice.126
  528.2 1.5 slice.129
  529.6 1.7 slice_reduce_fusion.7
  531.3 0.9 slice_reduce_fusion.10
  532.7 2.8 convert_reduce_fusion.1
  535.5 3.2 fusion.8
  538.7 1.0 copy.60
  539.7 1.3 copy.61
  (70 shorter events, 7.8 us)
Async XLA Ops:
  0.6 3.3 copy-start.11
  0.7 3.4 copy-start.19
  0.7 3.4 copy-start.18
  0.7 3.4 copy-start.17
  0.7 3.4 copy-start.16
  0.7 3.6 copy-start.12
  0.7 4.3 copy-start.24
  104.2 102.5 %copy-start.2 = (bf16[8,128,512]{2,1,0:T(8,128)(2,1)}, bf16[8,128,512]{2,1,0:T(8,128)(2,1)S(1)}, u32[]{:S(2)}) copy-start(bf16[8,128,512]{2,1,0:T(8,128)(2,1)S(1)} %slice.103) | copy-start | bytes 3145732
  206.7 9.5 %copy-start.21 = (bf16[1024,2048]{1,0:T(8,128)(2,1)S(1)}, bf16[1024,2048]{1,0:T(8,128)(2,1)}, u32[]{:S(2)}) copy-start(bf16[1024,2048]{1,0:T(8,128)(2,1)} %get-tuple-element.42) | copy-start | bytes 12582916
  206.7 9.5 %copy-start.23 = (bf16[1024,1024]{1,0:T(8,128)(2,1)S(1)}, bf16[1024,1024]{1,0:T(8,128)(2,1)}, u32[]{:S(2)}) copy-start(bf16[1024,1024]{1,0:T(8,128)(2,1)} %get-tuple-element.41) | copy-start | bytes 6291460
  216.2 6.1 %copy-start.22 = (bf16[1024,2048]{1,0:T(8,128)(2,1)S(1)}, bf16[1024,2048]{1,0:T(8,128)(2,1)}, u32[]{:S(2)}) copy-start(bf16[1024,2048]{1,0:T(8,128)(2,1)} %get-tuple-element.47) | copy-start | bytes 12582916
  333.0 5.2 copy-start.1
  333.0 5.2 copy-start.7
  335.9 3.5 copy-start.9
  335.9 3.5 copy-start.10
  339.4 41.1 %copy-start = (bf16[1024,1024]{1,0:T(8,128)(2,1)S(1)}, bf16[1024,1024]{1,0:T(8,128)(2,1)}, u32[]{:S(2)}) copy-start(bf16[1024,1024]{1,0:T(8,128)(2,1)} %get-tuple-element.38.refs_0_) | copy-start | bytes 6291460
  380.5 1.2 copy-start.3
  380.5 1.3 copy-start.6
  380.5 1.3 copy-start.13
  380.5 2.7 copy-start.20
  387.2 4.9 copy-start.14
  387.2 4.9 copy-start.15
  387.2 5.0 copy-start.4
  532.7 6.0 %copy-start.8 = (bf16[256,2048]{1,0:T(8,128)(2,1)S(1)}, bf16[256,2048]{1,0:T(8,128)(2,1)}, u32[]{:S(2)}) copy-start(bf16[256,2048]{1,0:T(8,128)(2,1)} %get-tuple-element.60) | copy-start | bytes 3145732
  535.5 4.2 copy-start.5

commit v5 on v4

--- a/solution.py
+++ b/solution.py
@@ -6,6 +6,7 @@
 from jax.sharding import PartitionSpec as P
 
 LANE = 128
+PER_GROUP = 4
 
 
 def sigmoid(v):
@@ -20,24 +21,38 @@
     return value.reshape(value.shape[0] * 8, value.shape[2])
 
 
-def spread_columns(row_ref, key_ref, query_ref, rows, states):
+def spread_columns(kq, row_ref, pick_ref, key_ref, query_ref, states):
+    rows = kq.shape[0]
+    high = kq.astype(jnp.bfloat16).astype(jnp.float32)
+    rest = kq - high
+    middle = rest.astype(jnp.bfloat16).astype(jnp.float32)
+    row_ref[...] = by_eights(high + pltpu.roll(middle, 2 * states, 1) + pltpu.roll(rest - middle, 4 * states, 1))
     lane = lax.broadcasted_iota(jnp.int32, (states, LANE), 1)
     entry = lax.broadcasted_iota(jnp.int32, (states, LANE), 0)
-    pick_key = lane == entry
-    pick_query = lane == entry + states
+    pick = lax.rem(lane, states) == entry
 
     def body(group, carry):
         for offset in range(8):
-            t = group * 8 + offset
+            at = pl.multiple_of((group * 8 + offset) * states, states)
             row = jnp.broadcast_to(row_ref[group, offset : offset + 1, :], (states, LANE))
-            at = pl.multiple_of(t * states, states)
-            key = jnp.sum(jnp.where(pick_key, row, 0.0), axis=1, keepdims=True)
-            query = jnp.sum(jnp.where(pick_query, row, 0.0), axis=1, keepdims=True)
-            key_ref[pl.ds(at, states), :] = jnp.broadcast_to(key, (states, LANE))
-            query_ref[pl.ds(at, states), :] = jnp.broadcast_to(query, (states, LANE))
+            pick_ref[pl.ds(at, states), :] = jnp.where(pick, row, 0.0).astype(jnp.bfloat16)
         return carry
 
     lax.fori_loop(0, rows // 8, body, 0)
+    term = lax.broadcasted_iota(jnp.int32, (LANE, 2 * LANE), 0)
+    side = lax.broadcasted_iota(jnp.int32, (LANE, 2 * LANE), 1)
+    is_query = lax.rem(term, 2 * states) >= states
+    halves = jnp.where(is_query == (side >= LANE), 1.0, 0.0).astype(jnp.bfloat16)
+    both = jnp.dot(pick_ref[...], halves, preferred_element_type=jnp.float32)
+    key_ref[...] = both[:, :LANE]
+    query_ref[...] = both[:, LANE:]
+
+
+def sum_eights(half_ref, first):
+    total = half_ref[pl.ds(first, 8, stride=8), :]
+    for n in range(1, 8):
+        total = total + half_ref[pl.ds(first + n, 8, stride=8), :]
+    return total
 
 
 def step_sizes(low, kq, weight_ref, bias_ref, states):
@@ -51,9 +66,9 @@
     return beta, 1.0 / (1.0 + beta * square)
 
 
-def forward_rows(states, rows, channels, history_ref, state_ref, key_ref, query_ref, rate_ref, input_ref, out_ref):
+def forward_rows(states, rows, channels, history_ref, state_ref, key_ref, query_ref, rate_ref, input_ref, out_ref, half_ref):
     tiles = channels // LANE
-    per_group = min(4, tiles)
+    per_group = min(8, tiles)
     for first in range(0, tiles, per_group):
         columns = [slice((first + j) * LANE, (first + j + 1) * LANE) for j in range(per_group)]
 
@@ -70,7 +85,10 @@
                     rate = rate_ref[group, offset : offset + 1, cols]
                     fed = input_ref[group, offset : offset + 1, cols]
                     carry[j] = (1.0 - rate * square) * carry[j] + key * fed
-                    out_ref[group, offset : offset + 1, cols] = jnp.sum(query * carry[j], axis=0, keepdims=True)
+                    read = query * carry[j]
+                    half_ref[j * 64 + offset * 8 : j * 64 + offset * 8 + 8, :] = read[0:8] + read[8:16]
+            for j, cols in enumerate(columns):
+                out_ref[group, :, cols] = sum_eights(half_ref, j * 64)
             return tuple(carry)
 
         done = lax.fori_loop(0, rows // 8, body, tuple(state_ref[:, cols] for cols in columns))
@@ -81,7 +99,7 @@
 def forward_body(
     states, low_ref, kq_ref, values_ref, gate_ref, weight_ref, bias_ref, skip_ref,
     gated_ref, mixed_ref, history_ref, final_ref,
-    state_ref, key_ref, query_ref, rate_ref, input_ref, out_ref, row_ref,
+    state_ref, key_ref, query_ref, rate_ref, input_ref, out_ref, row_ref, pick_ref, half_ref,
 ):
     rows, channels = values_ref.shape
 
@@ -93,10 +111,9 @@
     rates = beta * inverse
     rate_ref[...] = by_eights(rates)
     input_ref[...] = by_eights(rates * values_ref[...].astype(jnp.float32))
-    row_ref[...] = by_eights(kq_ref[...])
-    spread_columns(row_ref, key_ref, query_ref, rows, states)
-
-    forward_rows(states, rows, channels, history_ref, state_ref, key_ref, query_ref, rate_ref, input_ref, out_ref)
+    spread_columns(kq_ref[...], row_ref, pick_ref, key_ref, query_ref, states)
+
+    forward_rows(states, rows, channels, history_ref, state_ref, key_ref, query_ref, rate_ref, input_ref, out_ref, half_ref)
     mixed = as_rows(out_ref[...]) + skip_ref[...] * values_ref[...].astype(jnp.float32)
     gate = gate_ref[...]
     mixed_ref[...] = mixed
@@ -137,46 +154,20 @@
             pltpu.VMEM((rows // 8, 8, channels), jnp.float32),
             pltpu.VMEM((rows // 8, 8, channels), jnp.float32),
             pltpu.VMEM((rows // 8, 8, channels), jnp.float32),
-            pltpu.VMEM((rows // 8, 8, LANE), jnp.float32),
+            pltpu.VMEM((rows // 8, 8, LANE), jnp.float32), pltpu.VMEM((rows * states, LANE), jnp.bfloat16),
+            pltpu.VMEM((channels // LANE * 64, LANE), jnp.float32),
         ],
         compiler_params=pltpu.CompilerParams(vmem_limit_bytes=48 * 1024 * 1024),
         cost_estimate=pl.CostEstimate(flops=14 * length * states * channels, bytes_accessed=2 * length * states * channels, transcendentals=0),
     )(low, kq, values, gate, weight, bias, skip)
 
 
-def backward_body(
-    states, links, low_ref, kq_ref, values_ref, gate_ref, mixed_ref, dgated_ref, history_ref, final_ref, weight_ref, bias_ref, skip_ref,
-    result_ref, out_ref, dgate_ref, dpre_ref, dvalues_ref, dlow_ref, dkq_ref, bias_grad_ref, skip_grad_ref, result_came, out_came,
-    grad_ref, state_ref, key_ref, query_ref, rate_ref, do_ref, values32_ref, fed_ref, kept_ref, part_key_ref, part_query_ref, row_ref, placed_ref, *sems,
+def backward_rows(
+    states, rows, channels, history_ref, grad_ref, state_ref, key_ref, query_ref, rate_ref, do_ref, values32_ref,
+    fed_ref, kept_ref, part_key_ref, part_query_ref, half_ref,
 ):
-    rows, channels = values_ref.shape
     tiles = channels // LANE
-    per_group = min(4, tiles)
-    copies = links(result_ref, out_ref, result_came, out_came, *sems)
-
-    @pl.when(pl.program_id(0) == 0)
-    def _():
-        grad_ref[...] = jnp.zeros_like(grad_ref)
-        state_ref[...] = final_ref[...]
-        bias_grad_ref[...] = jnp.zeros_like(bias_grad_ref)
-        skip_grad_ref[...] = jnp.zeros_like(skip_grad_ref)
-        for copy in copies:
-            copy.start()
-
-    beta, inverse = step_sizes(low_ref[...], kq_ref[...], weight_ref, bias_ref, states)
-    rate_ref[...] = by_eights(beta * inverse)
-    values = values_ref[...].astype(jnp.float32)
-    values32_ref[...] = by_eights(values)
-    gate = gate_ref[...]
-    dgated = dgated_ref[...].astype(jnp.float32)
-    s = sigmoid(gate)
-    do = dgated * (gate * s)
-    do_ref[...] = by_eights(do)
-    dgate_ref[...] = (dgated * mixed_ref[...] * (s + gate * s * (1.0 - s))).astype(jnp.bfloat16)
-    skip_grad_ref[...] += jnp.sum(do * values, axis=0, keepdims=True)
-    row_ref[...] = by_eights(kq_ref[...])
-    spread_columns(row_ref, key_ref, query_ref, rows, states)
-
+    per_group = min(PER_GROUP, tiles)
     for first in range(0, tiles, per_group):
         columns = [slice((first + j) * LANE, (first + j + 1) * LANE) for j in range(per_group)]
 
@@ -199,9 +190,13 @@
                     scaled = rate * grad
                     by_key = key * scaled
                     kept = scaled * before
-                    fed_ref[group, offset : offset + 1, cols] = jnp.sum(by_key, axis=0, keepdims=True)
-                    kept_ref[group, offset : offset + 1, cols] = jnp.sum(key * (key * kept), axis=0, keepdims=True)
-                    term_key = value * scaled - 2.0 * (key * kept)
+                    kept = key * kept
+                    twice = key * kept
+                    at_fed = j * 64 + offset * 8
+                    at_kept = (per_group + j) * 64 + offset * 8
+                    half_ref[at_fed : at_fed + 8, :] = by_key[0:8] + by_key[8:16]
+                    half_ref[at_kept : at_kept + 8, :] = twice[0:8] + twice[8:16]
+                    term_key = value * scaled - 2.0 * kept
                     term_query = lates[j] * out_grad
                     sum_key = term_key if sum_key is None else sum_key + term_key
                     sum_query = term_query if sum_query is None else sum_query + term_query
@@ -213,6 +208,9 @@
                 else:
                     part_key_ref[pl.ds(at, states), :] += sum_key
                     part_query_ref[pl.ds(at, states), :] += sum_query
+            for j, cols in enumerate(columns):
+                fed_ref[group, :, cols] = sum_eights(half_ref, j * 64)
+                kept_ref[group, :, cols] = sum_eights(half_ref, (per_group + j) * 64)
             return (tuple(grads), tuple(lates))
 
         start = (tuple(grad_ref[:, cols] for cols in columns), tuple(state_ref[:, cols] for cols in columns))
@@ -221,6 +219,68 @@
             grad_ref[:, cols] = grad
             state_ref[:, cols] = late
 
+
+def lane_sums(part_ref, wide_ref, states):
+    part = part_ref[...]
+    high = part.astype(jnp.bfloat16)
+    wide_ref[:, :LANE] = high
+    wide_ref[:, LANE:] = (part - high.astype(jnp.float32)).astype(jnp.bfloat16)
+    ones = jnp.ones((2 * LANE, LANE), jnp.bfloat16)
+    part_ref[...] = jnp.dot(wide_ref[...], ones, preferred_element_type=jnp.float32)
+
+
+def gather_columns(part_key_ref, part_query_ref, wide_ref, placed_ref, rows, states):
+    lane_sums(part_key_ref, wide_ref, states)
+    lane_sums(part_query_ref, wide_ref, states)
+    lane = lax.broadcasted_iota(jnp.int32, (8, LANE), 1)
+
+    def body(group, carry):
+        total = jnp.zeros((8, LANE), jnp.float32)
+        for n in range(states):
+            at = group * 8 * states + n
+            total = jnp.where(lane == n, part_key_ref[pl.ds(at, 8, stride=states), :], total)
+            total = jnp.where(lane == n + states, part_query_ref[pl.ds(at, 8, stride=states), :], total)
+        placed_ref[group] = total
+        return carry
+
+    lax.fori_loop(0, rows // 8, body, 0)
+
+
+def backward_body(
+    states, links, low_ref, kq_ref, values_ref, gate_ref, mixed_ref, dgated_ref, history_ref, final_ref, weight_ref, bias_ref, skip_ref,
+    result_ref, out_ref, dgate_ref, dpre_ref, dvalues_ref, dlow_ref, dkq_ref, bias_grad_ref, skip_grad_ref, result_came, out_came,
+    grad_ref, state_ref, key_ref, query_ref, rate_ref, do_ref, values32_ref, fed_ref, kept_ref, part_key_ref, part_query_ref, row_ref, placed_ref,
+    pick_ref, wide_ref, half_ref, *sems,
+):
+    rows, channels = values_ref.shape
+    copies = links(result_ref, out_ref, result_came, out_came, *sems)
+
+    @pl.when(pl.program_id(0) == 0)
+    def _():
+        grad_ref[...] = jnp.zeros_like(grad_ref)
+        state_ref[...] = final_ref[...]
+        bias_grad_ref[...] = jnp.zeros_like(bias_grad_ref)
+        skip_grad_ref[...] = jnp.zeros_like(skip_grad_ref)
+        for copy in copies:
+            copy.start()
+
+    beta, inverse = step_sizes(low_ref[...], kq_ref[...], weight_ref, bias_ref, states)
+    rate_ref[...] = by_eights(beta * inverse)
+    values = values_ref[...].astype(jnp.float32)
+    values32_ref[...] = by_eights(values)
+    gate = gate_ref[...]
+    dgated = dgated_ref[...].astype(jnp.float32)
+    s = sigmoid(gate)
+    do = dgated * (gate * s)
+    do_ref[...] = by_eights(do)
+    dgate_ref[...] = (dgated * mixed_ref[...] * (s + gate * s * (1.0 - s))).astype(jnp.bfloat16)
+    skip_grad_ref[...] += jnp.sum(do * values, axis=0, keepdims=True)
+    spread_columns(kq_ref[...], row_ref, pick_ref, key_ref, query_ref, states)
+
+    backward_rows(
+        states, rows, channels, history_ref, grad_ref, state_ref, key_ref, query_ref, rate_ref, do_ref, values32_ref,
+        fed_ref, kept_ref, part_key_ref, part_query_ref, half_ref,
+    )
     fed = as_rows(fed_ref[...])
     dvalues_ref[...] = fed + skip_ref[...] * as_rows(do_ref[...])
     scaled = as_rows(values32_ref[...]) * fed - as_rows(kept_ref[...])
@@ -232,20 +292,7 @@
     dlow_ref[...] = jnp.dot(dpre_low, weight_ref[...], preferred_element_type=jnp.float32)
     through = -2.0 * jnp.sum(scaled * beta * inverse, axis=1, keepdims=True)
 
-    lane = lax.broadcasted_iota(jnp.int32, (states, LANE), 1)
-    entry = lax.broadcasted_iota(jnp.int32, (states, LANE), 0)
-
-    def gather(group, carry):
-        for offset in range(8):
-            t = group * 8 + offset
-            at = pl.multiple_of(t * states, states)
-            key = jnp.sum(part_key_ref[pl.ds(at, states), :], axis=1, keepdims=True)
-            query = jnp.sum(part_query_ref[pl.ds(at, states), :], axis=1, keepdims=True)
-            placed = jnp.where(lane == entry, key, 0.0) + jnp.where(lane == entry + states, query, 0.0)
-            placed_ref[group, offset : offset + 1, :] = jnp.sum(placed, axis=0, keepdims=True)
-        return carry
-
-    lax.fori_loop(0, rows // 8, gather, 0)
+    gather_columns(part_key_ref, part_query_ref, wide_ref, placed_ref, rows, states)
     lanes = lax.broadcasted_iota(jnp.int32, kq_ref.shape, 1)
     dkq_ref[...] = as_rows(placed_ref[...]) + jnp.where(lanes < states, kq_ref[...] * through, 0.0)
 
@@ -328,6 +375,8 @@
             pltpu.VMEM((states, channels), jnp.float32),
             spread, spread, wide, wide, wide, wide, wide, spread, spread,
             pltpu.VMEM((rows // 8, 8, LANE), jnp.float32), pltpu.VMEM((rows // 8, 8, LANE), jnp.float32),
+            pltpu.VMEM((rows * states, LANE), jnp.bfloat16), pltpu.VMEM((rows * states, 2 * LANE), jnp.bfloat16),
+            pltpu.VMEM((2 * channels // LANE * 64, LANE), jnp.float32),
             dma((parts - 1,)), dma((parts - 1,)), dma((dps - 1,)), dma((dps - 1,)),
         ],
         compiler_params=pltpu.CompilerParams(collective_id=3, has_side_effects=True, vmem_limit_bytes=56 * 1024 * 1024),
@@ -609,6 +658,76 @@
     )(tokens, spread, extra, gain)
 
 
+def line_sums(parts, rows, terms, came, send, recv):
+    d, s = lax.axis_index("dp"), lax.axis_index("seq")
+    chunk = rows // 4
+
+    def own_rows(part, c):
+        return pl.ds(pl.multiple_of(part * rows + c * chunk, chunk), chunk)
+
+    def slot(way, left, part, c):
+        at = parts if way == -1 and left == 0 else part
+        return came.at[at, pl.ds(c * chunk, chunk), :]
+
+    def copy_of(way, steps, c):
+        side = 0 if way == 1 else 1
+        part = s + way * steps
+        return pltpu.make_async_remote_copy(
+            src_ref=terms.at[own_rows(part, c), :], dst_ref=slot(way, steps - 1, part, c),
+            send_sem=send.at[side, steps, c], recv_sem=recv.at[side, steps - 1, c],
+            device_id=(d, s + way), device_id_type=MESH,
+        )
+
+    def valid(way, steps):
+        return s + steps < parts if way == 1 else s >= steps
+
+    def upstream(way):
+        return s >= 1 if way == 1 else s + 1 < parts
+
+    def taken(way, left, c):
+        side = 0 if way == 1 else 1
+        place = slot(way, left, s + way * left, c)
+        pltpu.make_async_remote_copy(
+            src_ref=place, dst_ref=place, send_sem=send.at[side, left, c], recv_sem=recv.at[side, left, c],
+            device_id=(d, s), device_id_type=MESH,
+        ).wait_recv()
+
+    def pass_on(steps, c):
+        for way in (1, -1):
+            @pl.when(valid(way, steps))
+            def _():
+                if steps < parts - 1:
+                    @pl.when(upstream(way))
+                    def _():
+                        taken(way, steps, c)
+                        mine = own_rows(s + way * steps, c)
+                        more = came[s + way * steps, c * chunk : (c + 1) * chunk, :]
+                        terms[mine, :] = (terms[mine, :].astype(jnp.float32) + more.astype(jnp.float32)).astype(jnp.bfloat16)
+
+                copy_of(way, steps, c).start()
+
+    def total(c):
+        for way in (1, -1):
+            @pl.when(upstream(way))
+            def _():
+                taken(way, 0, c)
+
+        at = pl.ds(c * chunk, chunk)
+        low = jnp.where(upstream(1), came[s, at, :].astype(jnp.float32), 0.0)
+        high = jnp.where(upstream(-1), came[parts, at, :].astype(jnp.float32), 0.0)
+        return terms[own_rows(s, c), :].astype(jnp.float32) + low + high
+
+    def sent():
+        for steps in range(1, parts):
+            for c in range(4):
+                for way in (1, -1):
+                    @pl.when(valid(way, steps))
+                    def _():
+                        copy_of(way, steps, c).wait_send()
+
+    return pass_on, total, sent
+
+
 def end_body(
     parts, block,
     dmixed_ref, normed_ref, weight_ref, tokens_ref, cot_ref, gain_ref, shard_ref, small_ref,
@@ -638,45 +757,7 @@
             src_ref=src, dst_ref=dst, send_sem=send, recv_sem=recv, device_id=to, device_id_type=MESH
         )
 
-    def dn_rows(part, c):
-        return pl.ds(pl.multiple_of(part * rows + c * chunk, chunk), chunk)
-
-    def slot(way, left, part, c):
-        at = parts if way == -1 and left == 0 else part
-        return dn_recv.at[at, pl.ds(c * chunk, chunk), :]
-
-    def line_copy(way, steps, c):
-        side = 0 if way == 1 else 1
-        part = s + way * steps
-        return remote(
-            dn.at[dn_rows(part, c), :], slot(way, steps - 1, part, c), line_send.at[side, steps, c],
-            line_recv.at[side, steps - 1, c], (d, s + way),
-        )
-
-    def valid(way, steps):
-        return s + steps < parts if way == 1 else s >= steps
-
-    def upstream(way):
-        return s >= 1 if way == 1 else s + 1 < parts
-
-    def line_wait(way, left, c):
-        side = 0 if way == 1 else 1
-        place = slot(way, left, s + way * left, c)
-        remote(place, place, line_send.at[side, left, c], line_recv.at[side, left, c], (d, s)).wait_recv()
-
-    def pass_line(steps, c):
-        for way in (1, -1):
-            @pl.when(valid(way, steps))
-            def _():
-                if steps < parts - 1:
-                    @pl.when(upstream(way))
-                    def _():
-                        line_wait(way, steps, c)
-                        mine = dn_rows(s + way * steps, c)
-                        came = dn_recv[s + way * steps, c * chunk : (c + 1) * chunk, :]
-                        dn[mine, :] = (dn[mine, :].astype(jnp.float32) + came.astype(jnp.float32)).astype(jnp.bfloat16)
-
-                line_copy(way, steps, c).start()
+    pass_line, line_total, line_sent = line_sums(parts, rows, dn, dn_recv, line_send, line_recv)
 
     def dn_part(part):
         at = pl.ds(pl.multiple_of(part * rows, rows), rows)
@@ -777,17 +858,8 @@
         near_copy(k).start()
 
     for c in range(4):
-        mine = dn_rows(s, c)
-        dn_total = dn[mine, :].astype(jnp.float32)
-        for way in (1, -1):
-            @pl.when(upstream(way))
-            def _():
-                line_wait(way, 0, c)
-
         at = pl.ds(c * chunk, chunk)
-        low = jnp.where(upstream(1), dn_recv[s, at, :].astype(jnp.float32), 0.0)
-        high = jnp.where(upstream(-1), dn_recv[parts, at, :].astype(jnp.float32), 0.0)
-        v = (dn_total + low + high) * gain_ref[...]
+        v = line_total(c) * gain_ref[...]
         flat = tokens_ref[at, :].astype(jnp.float32)
         scale = lax.rsqrt(jnp.mean(flat * flat, axis=-1, keepdims=True) + 1e-05)
         du = scale * v - flat * (scale * scale * scale) * jnp.mean(flat * v, axis=-1, keepdims=True)
@@ -819,12 +891,7 @@
         cross_copy_small(r).wait_send()
     for k in range(1, parts):
         near_copy(k).wait_send()
-    for steps in range(1, parts):
-        for c in range(4):
-            for way in (1, -1):
-                @pl.when(valid(way, steps))
-                def _():
-                    line_copy(way, steps, c).wait_send()
+    line_sent()
 
 
 def end(dmixed, normed, weight, tokens, cotangent, gain, shard, small, parts, block):
@@ -871,7 +938,7 @@
     states, parts, dps, taps,
     conv_in_ref, gate_ref, select_ref, conv_w_ref, conv_b_ref, weight_ref, bias_ref, skip_ref, out_shard, cot_shard,
     gated_ref, mixed_ref, history_ref, final_ref, values_ref, low_ref, kq_ref, out_all, cot_all,
-    state_ref, key_ref, query_ref, rate_ref, input_ref, out_ref, row_ref,
+    state_ref, key_ref, query_ref, rate_ref, input_ref, out_ref, row_ref, pick_ref, half_ref,
     part_low, part_kq, came_low, came_kq, sum_low, sum_kq,
     rs_send, rs_recv, ag_send, ag_recv, out_send, out_recv, line_send, line_recv, local_sem,
 ):
@@ -959,7 +1026,7 @@
             copy.start()
         for copy in own_copies():
             copy.start()
-        for c in range(4):
+        for c in range(2):
             send_cot(1, c)
 
     def rs_copies(k):
@@ -1028,6 +1095,8 @@
         for k in range(1, parts):
             for copy in ag_copies(k):
                 copy.start()
+        for c in range(2, 4):
+            send_cot(1, c)
 
     per_part = span // rows
     at_block = step - parts
@@ -1052,7 +1121,7 @@
 
             unpack(part)
 
-    plan = {0: ((1, 0), (1, 1)), 1: ((1, 2), (1, 3)), 2: ((2, 0),), 3: ((2, 1),), 4: ((2, 2),), 5: ((2, 3),)}
+    plan = {0: ((1, 0), (1, 1)), 1: ((1, 2), (1, 3)), 2: ((2, 0), (2, 1)), 3: ((2, 2),), 4: ((2, 3),)}
     for at, moves in plan.items():
         @pl.when(at_block == at)
         def _():
@@ -1069,9 +1138,8 @@
         rates = beta * inverse
         rate_ref[...] = by_eights(rates)
         input_ref[...] = by_eights(rates * values)
-        row_ref[...] = by_eights(kq)
-        spread_columns(row_ref, key_ref, query_ref, rows, states)
-        forward_rows(states, rows, channels, history_ref, state_ref, key_ref, query_ref, rate_ref, input_ref, out_ref)
+        spread_columns(kq, row_ref, pick_ref, key_ref, query_ref, states)
+        forward_rows(states, rows, channels, history_ref, state_ref, key_ref, query_ref, rate_ref, input_ref, out_ref, half_ref)
         mixed = as_rows(out_ref[...]) + skip_ref[...] * values
         gate = gate_ref[...]
         mixed_ref[...] = mixed
@@ -1138,6 +1206,7 @@
             pltpu.VMEM((states, channels), f32),
             pltpu.VMEM((rows * states, LANE), f32), pltpu.VMEM((rows * states, LANE), f32),
             eights, eights, eights, pltpu.VMEM((rows // 8, 8, LANE), f32),
+            pltpu.VMEM((rows * states, LANE), low), pltpu.VMEM((channels // LANE * 64, LANE), f32),
             pltpu.VMEM((parts, span, LANE), f32), pltpu.VMEM((parts, short, LANE), f32),
             pltpu.VMEM((parts - 1, span, LANE), f32), pltpu.VMEM((parts - 1, short, LANE), f32),
             pltpu.VMEM((parts, span, LANE), low), pltpu.VMEM((parts, short, LANE), f32),
@@ -1151,6 +1220,292 @@
             flops=14 * length * states * channels, bytes_accessed=2 * length * states * channels, transcendentals=0
         ),
     )(conv_in, gate, select, conv_w, conv_b, weight, bias, skip, out_shard, cot_shard)
+
+
+def linked_backward_body(
+    states, parts, dps, taps,
+    low_ref, kq_ref, gate_ref, mixed_ref, dgated_ref, history_ref, final_ref, weight_ref, bias_ref, skip_ref,
+    values_ref, conv_in_ref, select_ref, conv_w_ref, conv_b_ref, tokens_ref, part_ref, out_ref,
+    dmixed_ref, small_ref, result_ref, out_came,
+    grad_ref, state_ref, key_ref, query_ref, rate_ref, do_ref, values32_ref, fed_ref, kept_ref, part_key_ref,
+    part_query_ref, row_ref, placed_ref, pick_ref, wide_ref, half_ref,
+    dvalues_ref, dproj_ref, next_ref, vector_ref, part_low, part_kq, came_low, came_kq, sum_low, sum_kq,
+    rs_send, rs_recv, ag_send, ag_recv, result_came, line_send, line_recv, out_send, out_recv,
+):
+    d, s = lax.axis_index("dp"), lax.axis_index("seq")
+    step = pl.program_id(0)
+    rows, channels = gate_ref.shape
+    length = values_ref.shape[0]
+    blocks = length // rows
+    span = length // parts
+    per_part = span // rows
+    packed = LANE // (2 * states)
+    short = span // packed
+    sel = select_ref.shape[1]
+
+    def remote(src, dst, send, recv, to):
+        return pltpu.make_async_remote_copy(
+            src_ref=src, dst_ref=dst, send_sem=send, recv_sem=recv, device_id=to, device_id_type=MESH
+        )
+
+    copies = []
+    for k in range(1, dps):
+        to = lax.rem(d + k, dps)
+        copies.append(remote(out_ref.at[to], out_came.at[k - 1], out_send.at[k - 1], out_recv.at[k - 1], (to, s)))
+    pass_line, line_total, line_sent = line_sums(parts, span, part_ref, result_came, line_send, line_recv)
+
+    @pl.when(step == 0)
+    def _():
+        barrier = pltpu.get_barrier_semaphore()
+        for k in range(1, parts):
+            pl.semaphore_signal(barrier, inc=1, device_id=(d, lax.rem(s + k, parts)), device_id_type=MESH)
+        for k in range(1, dps):
+            pl.semaphore_signal(barrier, inc=1, device_id=(lax.rem(d + k, dps), s), device_id_type=MESH)
+        pl.semaphore_wait(barrier, parts + dps - 2)
+        grad_ref[...] = jnp.zeros_like(grad_ref)
+        state_ref[...] = final_ref[...]
+        next_ref[...] = jnp.zeros_like(next_ref)
+        vector_ref[...] = jnp.zeros_like(vector_ref)
+        small_ref[...] = jnp.zeros_like(small_ref)
+        for copy in copies:
+            copy.start()
+
+    def rs_copies(k):
+        at = lax.rem(s + k, parts)
+        return (
+            remote(part_low.at[at], came_low.at[k - 1], rs_send.at[0, k - 1], rs_recv.at[0, k - 1], (d, at)),
+            remote(part_kq.at[at], came_kq.at[k - 1], rs_send.at[1, k - 1], rs_recv.at[1, k - 1], (d, at)),
+        )
+
+    def ag_copies(k):
+        to = lax.rem(s + k, parts)
+        return (
+            remote(sum_low.at[s], sum_low.at[s], ag_send.at[0, k - 1], ag_recv.at[0, k - 1], (d, to)),
+            remote(sum_kq.at[s], sum_kq.at[s], ag_send.at[1, k - 1], ag_recv.at[1, k - 1], (d, to)),
+        )
+
+    def ag_taken(k, part):
+        return (
+            remote(sum_low.at[part], sum_low.at[part], ag_send.at[0, k - 1], ag_recv.at[0, k - 1], (d, s)),
+            remote(sum_kq.at[part], sum_kq.at[part], ag_send.at[1, k - 1], ag_recv.at[1, k - 1], (d, s)),
+        )
+
+    def add_up():
+        low = part_low[s].astype(jnp.float32)
+        kq = part_kq[s]
+        for k in range(1, parts):
+            for copy in rs_copies(k):
+                copy.wait_recv()
+            low = low + came_low[k - 1].astype(jnp.float32)
+            kq = kq + came_kq[k - 1]
+        sum_low[s] = low.astype(jnp.bfloat16)
+        sum_kq[s] = kq.astype(jnp.bfloat16)
+        for k in range(1, parts):
+            for copy in ag_copies(k):
+                copy.start()
+
+    def conv_back(part):
+        for k in range(1, parts):
+            @pl.when(lax.rem(s - k + parts, parts) == part)
+            def _():
+                for copy in ag_taken(k, part):
+                    copy.wait_recv()
+
+        here = pl.ds(pl.multiple_of(part * span, span), span)
+        before = pl.multiple_of(jnp.maximum(part * span - 16, 0), 16)
+        dproj_ref[:, :LANE] = sum_low[part]
+        pack = sum_kq[part].astype(jnp.float32)
+        lane = lax.broadcasted_iota(jnp.int32, pack.shape, 1)
+        for g in range(packed):
+            turned = pack if g == 0 else pltpu.roll(pack, LANE - g * 2 * states, 1)
+            dproj_ref[g * short : (g + 1) * short, LANE:] = jnp.where(lane < 2 * states, turned, 0.0).astype(jnp.bfloat16)
+        wide = min(256, channels)
+        for left in range(0, channels, wide):
+            cols = slice(left, left + wide)
+            small_ref[cols, :sel] += lax.dot_general(
+                values_ref[here, cols], dproj_ref[...], (((0,), (0,)), ((), ())), preferred_element_type=jnp.float32
+            )
+            head = conv_in_ref[pl.ds(before, 16), cols].astype(jnp.float32)
+            head = jnp.where(part == 0, 0.0, head)
+            body = jnp.concatenate([head, conv_in_ref[here, cols].astype(jnp.float32)], axis=0)
+            total = conv_b_ref[:, cols]
+            for tap in range(taps):
+                by = taps - 1 - tap
+                total = total + body[16 - by : 16 - by + span] * conv_w_ref[tap : tap + 1, cols]
+            sg = sigmoid(total)
+            dvalues = dvalues_ref[here, cols] + lax.dot_general(
+                dproj_ref[...], select_ref[cols, :], (((1,), (1,)), ((), ())), preferred_element_type=jnp.float32
+            )
+            dconv = dvalues * (sg + total * sg * (1.0 - sg))
+            vector_ref[taps : taps + 1, cols] += jnp.sum(dconv, axis=0, keepdims=True)
+            after = jnp.concatenate([dconv, next_ref[:, cols]], axis=0)
+            dconv_in = jnp.zeros_like(dconv)
+            for tap in range(taps):
+                by = taps - 1 - tap
+                shifted = body[16 - by : 16 - by + span]
+                vector_ref[tap : tap + 1, cols] += jnp.sum(dconv * shifted, axis=0, keepdims=True)
+                dconv_in = dconv_in + after[by : by + span] * conv_w_ref[tap : tap + 1, cols]
+            next_ref[:, cols] = dconv[0:8]
+            dmixed_ref[here, cols] = dconv_in.astype(jnp.bfloat16)
+
+    plan = (((3, 0), (3, 1)), ((3, 2), (3, 3), (2, 0)), ((2, 1), (2, 2)), ((2, 3), (1, 0)), ((1, 1),), ((1, 2),), ((1, 3),))
+    for at_step, moves in enumerate(plan):
+        @pl.when(step == at_step)
+        def _():
+            for steps, c in moves:
+                pass_line(steps, c)
+
+    for part in range(parts):
+        ends = (parts - part) * per_part - 1
+        sums = ends + (2 if part > 0 else 1)
+
+        @pl.when(jnp.logical_and(step == sums, s == part))
+        def _():
+            add_up()
+
+        @pl.when(step == sums + 1)
+        def _():
+            conv_back(part)
+
+    @pl.when(step < blocks)
+    def _():
+        block = blocks - 1 - step
+        here = pl.ds(pl.multiple_of(block * rows, rows), rows)
+        low, kq = low_ref[...], kq_ref[...]
+        beta, inverse = step_sizes(low, kq, weight_ref, bias_ref, states)
+        rate_ref[...] = by_eights(beta * inverse)
+        values = values_ref[here, :].astype(jnp.float32)
+        values32_ref[...] = by_eights(values)
+        gate = gate_ref[...]
+        dgated = dgated_ref[...].astype(jnp.float32)
+        sg = sigmoid(gate)
+        do = dgated * (gate * sg)
+        do_ref[...] = by_eights(do)
+        dmixed_ref[here, channels:] = (dgated * mixed_ref[...] * (sg + gate * sg * (1.0 - sg))).astype(jnp.bfloat16)
+        vector_ref[taps + 2 : taps + 3, :] += jnp.sum(do * values, axis=0, keepdims=True)
+        spread_columns(kq, row_ref, pick_ref, key_ref, query_ref, states)
+        backward_rows(
+            states, rows, channels, history_ref, grad_ref, state_ref, key_ref, query_ref, rate_ref, do_ref, values32_ref,
+            fed_ref, kept_ref, part_key_ref, part_query_ref, half_ref,
+        )
+        fed = as_rows(fed_ref[...])
+        dvalues_ref[here, :] = fed + skip_ref[...] * as_rows(do_ref[...])
+        scaled = as_rows(values32_ref[...]) * fed - as_rows(kept_ref[...])
+        beta, inverse = step_sizes(low, kq, weight_ref, bias_ref, states)
+        dpre = scaled * (1.0 - beta) * inverse
+        vector_ref[taps + 1 : taps + 2, :] += jnp.sum(dpre, axis=0, keepdims=True)
+        dpre_low = dpre.astype(jnp.bfloat16)
+        small_ref[:, sel : sel + LANE] += lax.dot_general(
+            dpre_low, low, (((0,), (0,)), ((), ())), preferred_element_type=jnp.float32
+        )
+        through = -2.0 * jnp.sum(scaled * beta * inverse, axis=1, keepdims=True)
+        gather_columns(part_key_ref, part_query_ref, wide_ref, placed_ref, rows, states)
+        lanes = lax.broadcasted_iota(jnp.int32, kq.shape, 1)
+        dkq = as_rows(placed_ref[...]) + jnp.where(lanes < states, kq * through, 0.0)
+        part = block // per_part
+        within = lax.rem(block, per_part)
+        part_low[part, pl.ds(pl.multiple_of(within * rows, rows), rows), :] = jnp.dot(
+            dpre_low, weight_ref[...], preferred_element_type=jnp.float32
+        ).astype(jnp.bfloat16)
+        for g in range(packed):
+            first = g * short - within * rows
+
+            @pl.when(jnp.logical_and(first >= 0, first < rows))
+            def _():
+                for w in range(per_part):
+                    if w * rows <= g * short < (w + 1) * rows:
+                        lo = g * short - w * rows
+                        piece = dkq[lo : lo + short]
+                        piece = piece if g == 0 else pltpu.roll(piece, g * 2 * states, 1)
+                        if g == (per_part - 1) * rows // short:
+                            part_kq[part] = piece
+                        else:
+                            part_kq[part] += piece
+
+        @pl.when(within == 0)
+        def _():
+            for k in range(1, parts):
+                @pl.when(lax.rem(s + k, parts) == part)
+                def _():
+                    for copy in rs_copies(k):
+                        copy.start()
+
+    @pl.when(step == pl.num_programs(0) - 1)
+    def _():
+        small_ref[:, sel + LANE :] = jnp.transpose(vector_ref[...])
+        chunk = span // 4
+        for c in range(4):
+            at = pl.ds(c * chunk, chunk)
+            result_ref[at, :] = (tokens_ref[at, :].astype(jnp.float32) + line_total(c)).astype(jnp.bfloat16)
+        line_sent()
+        for copy in copies:
+            copy.wait_recv()
+        for copy in copies:
+            copy.wait_send()
+        for k in range(1, parts):
+            for copy in rs_copies(k) + ag_copies(k):
+                copy.wait_send()
+
+
+def linked_backward(
+    low, kq, gate, mixed, dgated, history, final, weight, bias, skip, values, conv_in, select, conv_w, conv_b, tokens,
+    result_part, out_part, parts, states,
+):
+    length, channels = values.shape
+    dps = out_part.shape[0]
+    width = tokens.shape[1]
+    taps, sel = conv_w.shape[0], select.shape[1]
+    span = length // parts
+    rows = min(128, span)
+    blocks = length // rows
+    short = span // (LANE // (2 * states))
+    at = lambda i: jnp.maximum(blocks - 1 - i, 0)
+    by_row = lambda size: pl.BlockSpec((rows, size), lambda i: (at(i), 0))
+    whole = lambda a: pl.BlockSpec(a.shape, lambda i: (0, 0))
+    kept = lambda *shape: pl.BlockSpec(shape, lambda i: (0, 0))
+    anywhere = pl.BlockSpec(memory_space=pl.ANY)
+    dma = pltpu.SemaphoreType.DMA
+    f32, bf16 = jnp.float32, jnp.bfloat16
+    wide = pltpu.VMEM((rows // 8, 8, channels), f32)
+    eights = pltpu.VMEM((rows // 8, 8, LANE), f32)
+    spread = pltpu.VMEM((rows * states, LANE), f32)
+    return pl.pallas_call(
+        lambda *refs: linked_backward_body(states, parts, dps, taps, *refs),
+        grid=(blocks + 2,),
+        in_specs=[
+            by_row(LANE), by_row(LANE), by_row(channels), by_row(channels), by_row(channels),
+            pl.BlockSpec((rows * states, channels), lambda i: (at(i), 0)),
+            whole(final), whole(weight), whole(bias), whole(skip), whole(values), whole(conv_in), whole(select),
+            whole(conv_w), whole(conv_b), whole(tokens), whole(result_part), anywhere,
+        ],
+        out_specs=[kept(length, 2 * channels), kept(channels, sel + 2 * LANE), kept(span, width), anywhere],
+        out_shape=[
+            jax.ShapeDtypeStruct((length, 2 * channels), bf16),
+            jax.ShapeDtypeStruct((channels, sel + 2 * LANE), f32),
+            jax.ShapeDtypeStruct((span, width), bf16),
+            jax.ShapeDtypeStruct((dps - 1,) + out_part.shape[1:], bf16),
+        ],
+        scratch_shapes=[
+            pltpu.VMEM((states, channels), f32), pltpu.VMEM((states, channels), f32),
+            spread, spread, wide, wide, wide, wide, wide, spread, spread, eights, eights,
+            pltpu.VMEM((rows * states, LANE), bf16), pltpu.VMEM((rows * states, 2 * LANE), bf16),
+            pltpu.VMEM((2 * channels // LANE * 64, LANE), f32),
+            pltpu.VMEM((length, channels), f32), pltpu.VMEM((span, sel), bf16), pltpu.VMEM((8, channels), f32),
+            pltpu.VMEM((LANE, channels), f32),
+            pltpu.VMEM((parts, span, LANE), bf16), pltpu.VMEM((parts, short, LANE), f32),
+            pltpu.VMEM((parts - 1, span, LANE), bf16), pltpu.VMEM((parts - 1, short, LANE), f32),
+            pltpu.VMEM((parts, span, LANE), bf16), pltpu.VMEM((parts, short, LANE), bf16),
+            dma((2, parts - 1)), dma((2, parts - 1)), dma((2, parts - 1)), dma((2, parts - 1)),
+            pltpu.VMEM((parts + 1, span, width), bf16), dma((2, parts, 4)), dma((2, parts, 4)),
+            dma((dps - 1,)), dma((dps - 1,)),
+        ],
+        compiler_params=pltpu.CompilerParams(
+            collective_id=5, has_side_effects=True, vmem_limit_bytes=60 * 1024 * 1024
+        ),
+        cost_estimate=pl.CostEstimate(
+            flops=30 * length * states * channels, bytes_accessed=2 * length * states * channels, transcendentals=0
+        ),
+    )(low, kq, gate, mixed, dgated, history, final, weight, bias, skip, values, conv_in, select, conv_w, conv_b, tokens, result_part, out_part)
 
 
 def contract(left, right, left_dim, right_dim):
@@ -1243,16 +1598,16 @@
     conv_w, conv_b = vectors[:, :taps], vectors[:, taps]
     beta_b, skip = vectors[:, taps + 1].reshape(1, channels), vectors[:, taps + 2].reshape(1, channels)
     cot_here = cotangent.reshape(rows, width)
-    conv_wide = conv_in.astype(jnp.float32)
-    conv_sum = conv_b
-    for tap in range(taps):
-        conv_sum = conv_sum + later(conv_wide, taps - 1 - tap) * conv_w[:, tap]
     if small_slice:
         gated, mixed, history, final, values, low, kq, out_w, cot = linked_forward(
             conv_in, gate, smalls[:, :wide], conv_w.T, conv_b.reshape(1, channels), beta_w, beta_b, skip, out_weight,
             cot_here, parts, dps, states,
         )
     else:
+        conv_wide = conv_in.astype(jnp.float32)
+        conv_sum = conv_b
+        for tap in range(taps):
+            conv_sum = conv_sum + later(conv_wide, taps - 1 - tap) * conv_w[:, tap]
         out_w = gathered(out_weight, "dp")
         cot = gathered(cot_here, "seq")
         values = jax.nn.silu(conv_sum).astype(jnp.bfloat16)
@@ -1261,41 +1616,48 @@
         kq = jnp.pad(projected[:, rank:], ((0, 0), (0, LANE - 2 * states)))
         gated, mixed, history, final = forward_scan(low, kq, values, gate, beta_w, beta_b, skip, states)
     result_part = jnp.dot(gated, out_w, preferred_element_type=jnp.float32).astype(jnp.bfloat16)
-    result_part = result_part.reshape(parts, rows, width)
     out_part = contract(gated, cot, 0, 0).astype(jnp.bfloat16).reshape(dps, block, width)
     dgated = contract(cot, out_w, 1, 1)
-    dgate, dpre_low, dvalues, dlow, dkq, bias_grad, skip_grad, result_came, out_came = backward_scan(
-        low, kq, values, gate, mixed, dgated, history, final, beta_w, beta_b, skip, result_part, out_part, states
-    )
-    part_here = lax.dynamic_index_in_dim(result_part, lax.axis_index("seq"), 0, False).astype(jnp.float32)
-    result = (flat + (part_here + jnp.sum(result_came.astype(jnp.float32), axis=0))).astype(jnp.bfloat16)
+    if small_slice:
+        dmixed, small_grads, result, out_came = linked_backward(
+            low, kq, gate, mixed, dgated, history, final, beta_w, beta_b, skip, values, conv_in, smalls[:, :wide], conv_w.T,
+            conv_b.reshape(1, channels), tokens.reshape(rows, width), result_part, out_part, parts, states,
+        )
+        small_grads = small_grads.reshape(dps, block, wide + rank + LANE)
+    else:
+        result_part = result_part.reshape(parts, rows, width)
+        dgate, dpre_low, dvalues, dlow, dkq, bias_grad, skip_grad, result_came, out_came = backward_scan(
+            low, kq, values, gate, mixed, dgated, history, final, beta_w, beta_b, skip, result_part, out_part, states
+        )
+        part_here = lax.dynamic_index_in_dim(result_part, lax.axis_index("seq"), 0, False).astype(jnp.float32)
+        result = (flat + (part_here + jnp.sum(result_came.astype(jnp.float32), axis=0))).astype(jnp.bfloat16)
+        dprojected = lax.psum(jnp.concatenate([dlow, dkq[:, : 2 * states]], axis=1), "seq").astype(jnp.bfloat16)
+        beta_grad = contract(dpre_low, low, 0, 0)
+        select_grad = contract(values, dprojected, 0, 0)
+        dvalues = contract(dprojected, select_w, 1, 1) + dvalues
+        s = jax.nn.sigmoid(conv_sum)
+        dconv = dvalues * (s + conv_sum * s * (1.0 - s))
+        conv_w_grad = jnp.stack(
+            [jnp.sum(dconv * later(conv_wide, taps - 1 - tap), axis=0) for tap in range(taps)], axis=1
+        )
+        conv_b_grad = jnp.sum(dconv, axis=0)
+        dconv_in = 0.0
+        for tap in range(taps):
+            dconv_in = dconv_in + sooner(dconv, taps - 1 - tap) * conv_w[:, tap]
+        dmixed = jnp.concatenate([dconv_in.astype(jnp.bfloat16), dgate], axis=1)
+        vector_grads = jnp.concatenate(
+            [conv_w_grad, conv_b_grad[:, None], bias_grad.reshape(channels, 1), skip_grad.reshape(channels, 1)], axis=1
+        )
+        small_grads = jnp.concatenate(
+            [
+                jnp.pad(select_grad, ((0, 0), (0, wide - select_grad.shape[1]))),
+                beta_grad,
+                jnp.pad(vector_grads, ((0, 0), (0, LANE - vector_grads.shape[1]))),
+            ],
+            axis=1,
+        ).reshape(dps, block, wide + rank + LANE)
     out_here = lax.dynamic_index_in_dim(out_part, lax.axis_index("dp"), 0, False).astype(jnp.float32)
     out_grad = out_here + jnp.sum(out_came.astype(jnp.float32), axis=0)
-    dprojected = lax.psum(jnp.concatenate([dlow, dkq[:, : 2 * states]], axis=1), "seq").astype(jnp.bfloat16)
-    beta_grad = contract(dpre_low, low, 0, 0)
-    select_grad = contract(values, dprojected, 0, 0)
-    dvalues = contract(dprojected, select_w, 1, 1) + dvalues
-    s = jax.nn.sigmoid(conv_sum)
-    dconv = dvalues * (s + conv_sum * s * (1.0 - s))
-    conv_w_grad = jnp.stack(
-        [jnp.sum(dconv * later(conv_wide, taps - 1 - tap), axis=0) for tap in range(taps)], axis=1
-    )
-    conv_b_grad = jnp.sum(dconv, axis=0)
-    dconv_in = 0.0
-    for tap in range(taps):
-        dconv_in = dconv_in + sooner(dconv, taps - 1 - tap) * conv_w[:, tap]
-    dmixed = jnp.concatenate([dconv_in.astype(jnp.bfloat16), dgate], axis=1)
-    vector_grads = jnp.concatenate(
-        [conv_w_grad, conv_b_grad[:, None], bias_grad.reshape(channels, 1), skip_grad.reshape(channels, 1)], axis=1
-    )
-    small_grads = jnp.concatenate(
-        [
-            jnp.pad(select_grad, ((0, 0), (0, wide - select_grad.shape[1]))),
-            beta_grad,
-            jnp.pad(vector_grads, ((0, 0), (0, LANE - vector_grads.shape[1]))),
-        ],
-        axis=1,
-    ).reshape(dps, block, wide + rank + LANE)
     if small_slice:
         input_grad, in_grad, gain_sums, small_grads = end(
             dmixed, normed, in_w, tokens.reshape(rows, width), cot_here, gain.reshape(1, width), in_weight, small_grads,

time: 549 us -> 513 us (0.934)
  blocking collectives: 38.8 us -> 0 us
  Pallas kernels: 424 us -> 453 us
  other arithmetic: 23.5 us -> 7.86 us
  matrix products: 29.1 us -> 21.7 us
    psum x1 -> x0, blocking collectives: 38.8 us -> none  [local(): lax.psum(jnp.concatenate([dlow, dkq[:, :2 * states]], axis=1), 'seq')]
    pallas_call x1, Pallas kernels: 105 us -> 135 us  [linked_backward(): pl.pallas_call(lambda *refs: linked_backward_body(states, parts, dps, tap...]
    reduce_sum x2 -> x0, other arithmetic: 7.69 us -> none  [the longest x1 4.89 us: local(): jnp.sum(dconv * later(conv_wide, taps - 1 - tap), axis=0)]
    dot_general x5 -> x2, matrix products: 23.1 us -> 15.6 us  [contract(): lax.dot_general(left, right, (((left_dim,), (right_dim,)), ((), ())), pre...]
where the time goes in v5:
time: 513 us; the launch traced here: 506 us
  Pallas kernels  453 us (88%)
  local copies, waits for them, and re-layouts  22 us (4%)
  matrix products  21.7 us (4%)
  other arithmetic  7.86 us (2%)
    pallas_call x1, Pallas kernels, linked_backward(): pl.pallas_call(lambda *refs: linked_backward_body(states, parts, dps, tap...  135 us
    pallas_call x1, Pallas kernels, end(): pl.pallas_call(lambda *refs: end_body(parts, block, *refs), out_shape=[ja...  122 us
    pallas_call x1, Pallas kernels, linked_forward(): pl.pallas_call(lambda *refs: linked_forward_body(states, parts, dps, taps...  99 us
    pallas_call x1, Pallas kernels, start(): pl.pallas_call(lambda *refs: start_body(parts, own, *refs), out_shape=[ja...  97.2 us
    dot_general x2, matrix products, contract(): lax.dot_general(left, right, (((left_dim,), (right_dim,)), ((), ())), pre...  15.6 us

profile of v5, /device:TPU:25, one launch (start us, length us, event | category | flops | bytes accessed | tf_op | source)
XLA Modules:
  0.0 505.7 jit_solution(7492658039532547712)
XLA Ops:
  0.6 0.7 tile.8
  1.4 0.7 pad_maximum_fusion
  2.9 0.9 copy.51
  3.7 1.4 fusion.2.refs_2_
  5.2 1.8 reshape.76
  7.1 1.3 reshape.77.refs_1_
  8.4 97.2 %shard_map.194 = (bf16[1024,2048]{1,0:T(8,128)(2,1)}, bf16[2048,2048]{1,0:T(8,128)(2,1)}, bf16[1024,1024]{1,0:T(8,128)(2,1)}, f32[1024,1024]{1,0:T(8,128)}, bf16[8,192,512]{2,1,0:T(8,128)(2,1)}) custom-call(bf16[256,2048]{1,0:T(8,128)(2,1)} %bitcast.40, bf16[4,64,2048]{2,1,0:T(8,128)(2,1)} %reshape.77.refs_1_, bf16[128,512]{1,0:T(8,128)(2,1)} %fusion.2.refs_2_, ...), custom_call_target="tpu_custom_call" | custom-call | flops 8589934592 | bytes 41943040 | tf_op jit(solution)/shard_map/pallas_call | solution.py:630
  105.6 0.9 slice.65
  106.5 1.3 slice.57
  107.9 0.7 reshape.85.refs_5_
  108.5 0.8 slice.74.refs_2_.refs_12_
  109.4 0.7 fusion.4
  110.3 0.6 slice_bitcast_fusion.1
  110.9 0.6 slice_bitcast_fusion.refs_3_.refs_13_
  111.5 99.0 %shard_map.195 = (bf16[1024,1024]{1,0:T(8,128)(2,1)}, f32[1024,1024]{1,0:T(8,128)}, bf16[16384,1024]{1,0:T(8,128)(2,1)}, f32[16,1024]{1,0:T(8,128)}, bf16[1024,1...) custom-call(bf16[1024,1024]{1,0:T(8,128)(2,1)} %get-tuple-element.33, ...), custom_call_target="tpu_custom_call" | custom-call | flops 234881024 | bytes 33554432 | tf_op jit(solution)/shard_map/pallas_call | solution.py:1183
  210.5 9.5 %convolution_convert_fusion = bf16[1024,2048]{1,0:T(8,128)(2,1)} fusion(bf16[1024,1024]{1,0:T(8,128)(2,1)} %get-tuple-element.44, bf16[1024,2048]{1,0:T(8,128)(2,1)} %get-tuple-element.39), kind=kOutput, calls=%fused_computation.1 | convolution fusion | flops 4297064448 | bytes 10485760 | tf_op jit(solution)/shard_map/dot_general | solution.py:1512
  220.0 6.1 %fusion.5.refs_4_ = f32[1024,1024]{1,0:T(8,128)} fusion(bf16[1024,2048]{1,0:T(8,128)(2,1)S(1)} %copy-done.4, bf16[1024,2048]{1,0:T(8,128)(2,1)S(1)} %copy-done.3), kind=kOutput, calls=%fused_computation.23 | convolution fusion | flops 4294967296 | bytes 12582912 | tf_op jit(solution)/shard_map/dot_general | solution.py:1512
  226.1 6.1 %convolution_convert_fusion.1.refs_16_ = bf16[1024,2048]{1,0:T(8,128)(2,1)} fusion(bf16[1024,1024]{1,0:T(8,128)(2,1)S(1)} %copy-done.5, bf16[1024,2048]{1,0:T(8,128)(2,1)S(1)} %copy-done.3), kind=kOutput, calls=%fused_computation.2 | convolution fusion | flops 4297064448 | bytes 10485760 | tf_op jit(solution)/shard_map/dot_general | solution.py:1618
  232.2 135.3 %shard_map.196 = (bf16[1024,2048]{1,0:T(8,128)(2,1)}, f32[1024,512]{1,0:T(8,128)}, bf16[256,2048]{1,0:T(8,128)(2,1)}, bf16[7,128,2048]{2,1,0:T(8,128)(2,1)}) custom-call(bf16[1024,128]{1,0:T(8,128)(2,1)} %get-tuple-element.36.refs_0_, f32[1024,128]{1,0:T(8,128)} %get-tuple-element.37.refs_1_, f32[1024,1024]{1,0:T(8,128)} %get-tuple-element.34.refs_1_.refs_2_, ...), custom_call_target="tpu_custom_call" | custom-call | flops 503316480 | bytes 33554432 | tf_op jit(solution)/shard_map/pallas_call | solution.py:1472
  367.5 121.8 %shard_map.197 = (bf16[256,2048]{1,0:T(8,128)(2,1)}, f32[64,8192]{1,0:T(8,128)}, f32[64,128]{1,0:T(8,128)}, f32[128,512]{1,0:T(8,128)}) custom-call(bf16[1024,2048]{1,0:T(8,128)(2,1)} %get-tuple-element.46.refs_0_, bf16[1024,2048]{1,0:T(8,128)(2,1)} %get-tuple-element.47.refs_1_, bf16[2048,2048]{1,0:T(8,128)(2,1)} %get-tuple-element.48.refs_2_, ...), custom_call_target="tpu_custom_call" | custom-call | flops 17179869184 | bytes 31457280 | tf_op jit(solution)/shard_map/pallas_call | solution.py:906
  489.3 0.9 slice_reduce_fusion.3
  490.7 1.7 slice_reduce_fusion
  492.5 1.5 slice.71
  493.9 0.8 slice.68
  494.8 0.9 slice.70
  495.7 0.7 copy.59
  496.3 0.7 copy.60
  497.1 2.9 convert_reduce_fusion
  500.0 2.3 convert_add_fusion
  502.2 1.0 copy.72
  503.2 1.0 copy.73
  504.2 1.3 copy.74
  (23 shorter events, 1.7 us)
Async XLA Ops:
  210.5 9.5 %copy-start.3 = (bf16[1024,2048]{1,0:T(8,128)(2,1)S(1)}, bf16[1024,2048]{1,0:T(8,128)(2,1)}, u32[]{:S(2)}) copy-start(bf16[1024,2048]{1,0:T(8,128)(2,1)} %get-tuple-element.40) | copy-start | bytes 12582916
  210.5 9.5 %copy-start.4 = (bf16[1024,2048]{1,0:T(8,128)(2,1)S(1)}, bf16[1024,2048]{1,0:T(8,128)(2,1)}, u32[]{:S(2)}) copy-start(bf16[1024,2048]{1,0:T(8,128)(2,1)} %get-tuple-element.39) | copy-start | bytes 12582916
  220.0 6.1 %copy-start.5 = (bf16[1024,1024]{1,0:T(8,128)(2,1)S(1)}, bf16[1024,1024]{1,0:T(8,128)(2,1)}, u32[]{:S(2)}) copy-start(bf16[1024,1024]{1,0:T(8,128)(2,1)} %get-tuple-element.44) | copy-start | bytes 6291460
  367.5 122.7 %copy-start.6 = (bf16[64]{0:T(256)(128)(2,1)S(1)}, bf16[64]{0:T(256)(128)(2,1)}, u32[]{:S(2)}) copy-start(bf16[64]{0:T(256)(128)(2,1)} %param.13) | copy-start | bytes 388
  489.3 13.0 %copy-start.1 = (bf16[256,2048]{1,0:T(8,128)(2,1)S(1)}, bf16[256,2048]{1,0:T(8,128)(2,1)}, u32[]{:S(2)}) copy-start(bf16[256,2048]{1,0:T(8,128)(2,1)} %get-tuple-element.45) | copy-start | bytes 3145732
  497.1 6.1 %copy-start.2 = (bf16[256,2048]{1,0:T(8,128)(2,1)S(1)}, bf16[256,2048]{1,0:T(8,128)(2,1)}, u32[]{:S(2)}) copy-start(bf16[256,2048]{1,0:T(8,128)(2,1)} %get-tuple-element.50) | copy-start | bytes 3145732
  499.9 4.2 copy-start
